TPU v7x, 32 devices: a whole 2x2x4 slice. The times are simulated.
32 devices in a mesh: member: 8 (over y, x, core), sub: 4 (over z).
Axes of the slice: x: 2, y: 2, z: 4, core: 2. Of those that a mesh axis runs over, the one named last changes fastest.
Arguments:
- velocity: float32 [8, 3, 64, 32, 128], P('member', None, 'sub'), may hold values from -8 to 8
- forcing: float32 [8, 3, 64, 32, 128], P('member', None, 'sub'), may hold values from -16 to 16
Outputs:
- new_velocity: float32 [8, 3, 64, 32, 128], P('member', None, 'sub')
All inputs are finite; a program needn't handle non-finite values.
Results may differ from a plain program's by a relative error of at most 0.00029.
Values sent between devices are 32-bit elements; how exact they have to be, the bound alone decides.
No kernel may reach another device: no remote copies, remote signals or barrier semaphores. Data moves between devices by JAX's collectives and lax.ppermute only.
A program may use at most 64 MiB of HBM per device.

v0:
```python
import math

import jax
import jax.numpy as jnp
from jax import lax
from jax.sharding import PartitionSpec as P

SWEEPS = 8


TIME_STEP = 0.25
EDDY_COEFF = 1.0
BASE_VISCOSITY = 1.0
LOWER_EDGE = 0.1
UPPER_EDGE = 1.9


def with_halo(block, sides, width):
    for axis, dim in sides:
        count = lax.axis_size(axis)
        forward = [(i, i + 1) for i in range(count - 1)]
        forward.append((count - 1, 0))
        backward = [(target, source) for source, target in forward]
        low = lax.ppermute(
            lax.slice_in_dim(block, block.shape[dim] - width, None, axis=dim), axis, forward
        )
        high = lax.ppermute(lax.slice_in_dim(block, 0, width, axis=dim), axis, backward)
        block = jnp.concatenate([low, block, high], axis=dim)
    return block


def step_sizes(sweep_count):
    middle = (UPPER_EDGE + LOWER_EDGE) / 2
    radius = (UPPER_EDGE - LOWER_EDGE) / 2
    return [
        1.0 / (middle + radius * math.cos(math.pi * (2 * position + 1) / (2 * sweep_count)))
        for position in range(sweep_count)
    ]


def coefficients(visc_ext):
    center = visc_ext[1:-1]
    east_face = 0.5 * (center + visc_ext[2:])
    west_face = 0.5 * (center + visc_ext[:-2])
    north_face = 0.5 * (center + jnp.roll(center, -1, 1))
    south_face = 0.5 * (center + jnp.roll(center, 1, 1))
    upper_face = 0.5 * (center + jnp.roll(center, -1, 2))
    lower_face = 0.5 * (center + jnp.roll(center, 1, 2))
    diagonal = 1.0 + TIME_STEP * (
        east_face + west_face + north_face + south_face + upper_face + lower_face
    )
    return (east_face, west_face, north_face, south_face, upper_face, lower_face, diagonal)


def sweep(field, coeffs, source, step_size):
    cut = [entry for entry in coeffs]
    east_face, west_face, north_face, south_face, upper_face, lower_face, diagonal = cut
    center = field[:, 1:-1]
    neighbours = east_face * field[:, 2:] + west_face * field[:, :-2]
    neighbours = (
        neighbours + north_face * jnp.roll(center, -1, 2) + south_face * jnp.roll(center, 1, 2)
    )
    neighbours = (
        neighbours + upper_face * jnp.roll(center, -1, 3) + lower_face * jnp.roll(center, 1, 3)
    )
    image = diagonal * center - TIME_STEP * neighbours
    return center + step_size * (source - image) / diagonal


def per_device(velocity, forcing):
    members = lax.axis_size("member")
    flow = velocity[0]
    member_force = forcing[0]
    flow_ext = with_halo(flow, (("sub", 1),), 1)
    differences = [
        (flow_ext[:, 2:] - flow_ext[:, :-2]) * 0.5,
        (jnp.roll(flow, -1, 2) - jnp.roll(flow, 1, 2)) * 0.5,
        (jnp.roll(flow, -1, 3) - jnp.roll(flow, 1, 3)) * 0.5,
    ]
    total, squares = lax.psum((flow, jnp.sum(flow * flow, 0)), "member")
    mean_flow = total / members
    spread = squares / members - jnp.sum(mean_flow * mean_flow, 0)
    viscosity = BASE_VISCOSITY + EDDY_COEFF * TIME_STEP * spread
    transport = (
        mean_flow[0] * differences[0]
        + mean_flow[1] * differences[1]
        + mean_flow[2] * differences[2]
    )
    source = flow - TIME_STEP * transport + TIME_STEP * member_force
    sizes_list = step_sizes(SWEEPS)
    field = source
    visc_ext = with_halo(viscosity, (("sub", 0),), 1)
    coeffs = coefficients(visc_ext)
    for step_size in sizes_list:
        extended = with_halo(field, (("sub", 1),), 1)
        field = sweep(extended, coeffs, source, step_size)
    return field[None]


def solution(mesh):
    in_specs = (P("member", None, "sub", None, None), P("member", None, "sub", None, None))
    out_specs = P("member", None, "sub", None, None)
    return jax.shard_map(
        per_device, mesh=mesh, in_specs=in_specs, out_specs=out_specs, check_vma=False
    )
```

profile of v0, /device:TPU:0, one launch (start us, length us, event | category | flops | bytes accessed | tf_op | source)
XLA Modules:
  0.0 154.6 jit_solution(10186676913635887603)
XLA Ops:
  6.5 0.8 fusion.175
  7.4 5.1 %collective-permute-start = (f32[3,1,32,128]{3,2,1,0:T(8,128)S(1)}, f32[3,1,32,128]{3,2,1,0:T(8,128)S(1)}, u32[]{:S(2)}, u32[]{:S(2)}) collective-permute-start(f32[3,1,32,128]{3,2,1,0:T(8,128)S(1)} %get-tuple-element.107), channel_id=1, source_target_pairs={{1,0},{2,1},{3,2},{0,3},{5,4},{6,5},{7,6},{4,7},{9,8},{10,9},{11,1... | collective-permute-start | bytes 147464 | tf_op jit(solution)/shard_map/ppermute | solution.py:27
  12.5 1.9 %multiply_reduce_fusion.1 = f32[16,32,128]{2,1,0:T(8,128)} fusion(f32[1,3,16,32,128]{4,3,2,1,0:T(8,128)} %param.2), kind=kLoop, calls=%fused_computation.166 | loop fusion | flops 327680 | bytes 1048576 | tf_op jit(solution)/shard_map/reduce_sum | solution.py:80
  14.4 1.1 copy-done
  15.8 1.1 fusion.174
  16.9 1.4 fusion.172
  18.3 54.4 %all-reduce.3.cloned.1.call-done = (f32[3,16,32,128]{3,2,1,0:T(8,128)}, f32[16,32,128]{2,1,0:T(8,128)}) async-done(((f32[3,16,32,128]{3,2,1,0:T(8,128)}, f32[16,32,128]{2,1,0:T(8,128)}), (f32[3,16,32,128]{3,2,1,0:T(8,128)}, f32[16,32,128]{2,1,0:T(8,128)})) %all-reduce.3.cloned.1.call-update) | async-done | bytes 1048592 | tf_op jit(solution)/shard_map/psum | solution.py:80
  72.7 1.3 multiply_reduce_fusion
  74.6 0.8 copy-done.4
  76.2 1.0 fusion.110
  77.9 1.4 collective-permute-start.3
  79.3 2.5 %collective-permute-start.2 = (f32[1,32,128]{2,1,0:T(8,128)S(1)}, f32[1,32,128]{2,1,0:T(8,128)S(1)}, u32[]{:S(2)}, u32[]{:S(2)}) collective-permute-start(f32[1,32,128]{2,1,0:T(8,128)S(1)} %get-tuple-element.118), channel_id=1, source_target_pairs={{1,0},{2,1},{3,2},{0,3},{5,4},{6,5},{7,6},{4,7},{9,8},{10,9},{11,1... | collective-permute-start | bytes 49160 | tf_op jit(solution)/shard_map/ppermute | solution.py:27
  81.8 1.4 collective-permute-start.4
  83.3 0.7 collective-permute-start.5
  83.9 0.3 multiply_add_fusion
  84.3 2.2 %collective-permute-done.4 = f32[3,1,32,128]{3,2,1,0:T(8,128)S(1)} collective-permute-done((f32[3,1,32,128]{3,2,1,0:T(8,128)S(1)}, f32[3,1,32,128]{3,2,1,0:T(8,128)S(1)}, u32[]{:S(2)}, u32[]{:S(2)}) %collective-permute-start.4) | collective-permute-done | bytes 49184 | tf_op jit(solution)/shard_map/ppermute | solution.py:27
  86.5 2.8 %collective-permute-done.5 = f32[3,1,32,128]{3,2,1,0:T(8,128)S(1)} collective-permute-done((f32[3,1,32,128]{3,2,1,0:T(8,128)S(1)}, f32[3,1,32,128]{3,2,1,0:T(8,128)S(1)}, u32[]{:S(2)}, u32[]{:S(2)}) %collective-permute-start.5) | collective-permute-done | bytes 49184 | tf_op jit(solution)/shard_map/ppermute | solution.py:24
  89.3 1.0 fusion.102
  91.2 2.0 %collective-permute-start.7 = (f32[3,1,32,128]{3,2,1,0:T(8,128)S(1)}, f32[3,1,32,128]{3,2,1,0:T(8,128)S(1)}, u32[]{:S(2)}, u32[]{:S(2)}) collective-permute-start(f32[3,1,32,128]{3,2,1,0:T(8,128)S(1)} %get-tuple-element.83), channel_id=1, source_target_pairs={{0,1},{1,2},{2,3},{3,0},{4,5},{5,6},{6,7},{7,4},{8,9},{9,10},{10,1... | collective-permute-start | bytes 147464 | tf_op jit(solution)/shard_map/ppermute | solution.py:24
  93.2 2.0 %collective-permute-done.6 = f32[3,1,32,128]{3,2,1,0:T(8,128)S(1)} collective-permute-done((f32[3,1,32,128]{3,2,1,0:T(8,128)S(1)}, f32[3,1,32,128]{3,2,1,0:T(8,128)S(1)}, u32[]{:S(2)}, u32[]{:S(2)}) %collective-permute-start.6) | collective-permute-done | bytes 49184 | tf_op jit(solution)/shard_map/ppermute | solution.py:27
  95.2 2.3 %collective-permute-done.7 = f32[3,1,32,128]{3,2,1,0:T(8,128)S(1)} collective-permute-done((f32[3,1,32,128]{3,2,1,0:T(8,128)S(1)}, f32[3,1,32,128]{3,2,1,0:T(8,128)S(1)}, u32[]{:S(2)}, u32[]{:S(2)}) %collective-permute-start.7) | collective-permute-done | bytes 49184 | tf_op jit(solution)/shard_map/ppermute | solution.py:24
  97.6 1.0 fusion.89
  99.5 2.0 %collective-permute-start.9 = (f32[3,1,32,128]{3,2,1,0:T(8,128)S(1)}, f32[3,1,32,128]{3,2,1,0:T(8,128)S(1)}, u32[]{:S(2)}, u32[]{:S(2)}) collective-permute-start(f32[3,1,32,128]{3,2,1,0:T(8,128)S(1)} %get-tuple-element.73), channel_id=1, source_target_pairs={{0,1},{1,2},{2,3},{3,0},{4,5},{5,6},{6,7},{7,4},{8,9},{9,10},{10,1... | collective-permute-start | bytes 147464 | tf_op jit(solution)/shard_map/ppermute | solution.py:24
  101.5 2.0 %collective-permute-done.8 = f32[3,1,32,128]{3,2,1,0:T(8,128)S(1)} collective-permute-done((f32[3,1,32,128]{3,2,1,0:T(8,128)S(1)}, f32[3,1,32,128]{3,2,1,0:T(8,128)S(1)}, u32[]{:S(2)}, u32[]{:S(2)}) %collective-permute-start.8) | collective-permute-done | bytes 49184 | tf_op jit(solution)/shard_map/ppermute | solution.py:27
  103.6 2.0 %collective-permute-done.9 = f32[3,1,32,128]{3,2,1,0:T(8,128)S(1)} collective-permute-done((f32[3,1,32,128]{3,2,1,0:T(8,128)S(1)}, f32[3,1,32,128]{3,2,1,0:T(8,128)S(1)}, u32[]{:S(2)}, u32[]{:S(2)}) %collective-permute-start.9) | collective-permute-done | bytes 49184 | tf_op jit(solution)/shard_map/ppermute | solution.py:24
  105.5 1.0 fusion.76
  107.4 2.0 %collective-permute-start.11 = (f32[3,1,32,128]{3,2,1,0:T(8,128)S(1)}, f32[3,1,32,128]{3,2,1,0:T(8,128)S(1)}, u32[]{:S(2)}, u32[]{:S(2)}) collective-permute-start(f32[3,1,32,128]{3,2,1,0:T(8,128)S(1)} %get-tuple-element.63), channel_id=1, source_target_pairs={{0,1},{1,2},{2,3},{3,0},{4,5},{5,6},{6,7},{7,4},{8,9},{9,10},{10,1... | collective-permute-start | bytes 147464 | tf_op jit(solution)/shard_map/ppermute | solution.py:24
  109.5 2.3 %collective-permute-done.10 = f32[3,1,32,128]{3,2,1,0:T(8,128)S(1)} collective-permute-done((f32[3,1,32,128]{3,2,1,0:T(8,128)S(1)}, f32[3,1,32,128]{3,2,1,0:T(8,128)S(1)}, u32[]{:S(2)}, u32[]{:S(2)}) %collective-permute-start.10) | collective-permute-done | bytes 49184 | tf_op jit(solution)/shard_map/ppermute | solution.py:27
  111.8 1.8 %collective-permute-done.11 = f32[3,1,32,128]{3,2,1,0:T(8,128)S(1)} collective-permute-done((f32[3,1,32,128]{3,2,1,0:T(8,128)S(1)}, f32[3,1,32,128]{3,2,1,0:T(8,128)S(1)}, u32[]{:S(2)}, u32[]{:S(2)}) %collective-permute-start.11) | collective-permute-done | bytes 49184 | tf_op jit(solution)/shard_map/ppermute | solution.py:24
  113.5 1.0 fusion.63
  115.4 0.8 collective-permute-start.12
  116.2 1.3 collective-permute-start.13
  117.5 2.0 %collective-permute-done.12 = f32[3,1,32,128]{3,2,1,0:T(8,128)S(1)} collective-permute-done((f32[3,1,32,128]{3,2,1,0:T(8,128)S(1)}, f32[3,1,32,128]{3,2,1,0:T(8,128)S(1)}, u32[]{:S(2)}, u32[]{:S(2)}) %collective-permute-start.12) | collective-permute-done | bytes 49184 | tf_op jit(solution)/shard_map/ppermute | solution.py:27
  119.5 2.5 %collective-permute-done.13 = f32[3,1,32,128]{3,2,1,0:T(8,128)S(1)} collective-permute-done((f32[3,1,32,128]{3,2,1,0:T(8,128)S(1)}, f32[3,1,32,128]{3,2,1,0:T(8,128)S(1)}, u32[]{:S(2)}, u32[]{:S(2)}) %collective-permute-start.13) | collective-permute-done | bytes 49184 | tf_op jit(solution)/shard_map/ppermute | solution.py:24
  122.0 1.0 fusion.50
  123.9 0.4 collective-permute-start.14
  124.2 1.7 %collective-permute-start.15 = (f32[3,1,32,128]{3,2,1,0:T(8,128)S(1)}, f32[3,1,32,128]{3,2,1,0:T(8,128)S(1)}, u32[]{:S(2)}, u32[]{:S(2)}) collective-permute-start(f32[3,1,32,128]{3,2,1,0:T(8,128)S(1)} %get-tuple-element.43), channel_id=1, source_target_pairs={{0,1},{1,2},{2,3},{3,0},{4,5},{5,6},{6,7},{7,4},{8,9},{9,10},{10,1... | collective-permute-start | bytes 147464 | tf_op jit(solution)/shard_map/ppermute | solution.py:24
  126.0 2.3 %collective-permute-done.14 = f32[3,1,32,128]{3,2,1,0:T(8,128)S(1)} collective-permute-done((f32[3,1,32,128]{3,2,1,0:T(8,128)S(1)}, f32[3,1,32,128]{3,2,1,0:T(8,128)S(1)}, u32[]{:S(2)}, u32[]{:S(2)}) %collective-permute-start.14) | collective-permute-done | bytes 49184 | tf_op jit(solution)/shard_map/ppermute | solution.py:27
  128.3 1.8 %collective-permute-done.15 = f32[3,1,32,128]{3,2,1,0:T(8,128)S(1)} collective-permute-done((f32[3,1,32,128]{3,2,1,0:T(8,128)S(1)}, f32[3,1,32,128]{3,2,1,0:T(8,128)S(1)}, u32[]{:S(2)}, u32[]{:S(2)}) %collective-permute-start.15) | collective-permute-done | bytes 49184 | tf_op jit(solution)/shard_map/ppermute | solution.py:24
  130.1 1.0 fusion.37
  132.0 2.0 %collective-permute-start.17 = (f32[3,1,32,128]{3,2,1,0:T(8,128)S(1)}, f32[3,1,32,128]{3,2,1,0:T(8,128)S(1)}, u32[]{:S(2)}, u32[]{:S(2)}) collective-permute-start(f32[3,1,32,128]{3,2,1,0:T(8,128)S(1)} %get-tuple-element.33), channel_id=1, source_target_pairs={{0,1},{1,2},{2,3},{3,0},{4,5},{5,6},{6,7},{7,4},{8,9},{9,10},{10,1... | collective-permute-start | bytes 147464 | tf_op jit(solution)/shard_map/ppermute | solution.py:24
  134.1 2.0 %collective-permute-done.16 = f32[3,1,32,128]{3,2,1,0:T(8,128)S(1)} collective-permute-done((f32[3,1,32,128]{3,2,1,0:T(8,128)S(1)}, f32[3,1,32,128]{3,2,1,0:T(8,128)S(1)}, u32[]{:S(2)}, u32[]{:S(2)}) %collective-permute-start.16) | collective-permute-done | bytes 49184 | tf_op jit(solution)/shard_map/ppermute | solution.py:27
  136.1 1.9 %collective-permute-done.17 = f32[3,1,32,128]{3,2,1,0:T(8,128)S(1)} collective-permute-done((f32[3,1,32,128]{3,2,1,0:T(8,128)S(1)}, f32[3,1,32,128]{3,2,1,0:T(8,128)S(1)}, u32[]{:S(2)}, u32[]{:S(2)}) %collective-permute-start.17) | collective-permute-done | bytes 49184 | tf_op jit(solution)/shard_map/ppermute | solution.py:24
  138.0 1.0 fusion.24
  139.9 2.0 %collective-permute-start.19 = (f32[3,1,32,128]{3,2,1,0:T(8,128)S(1)}, f32[3,1,32,128]{3,2,1,0:T(8,128)S(1)}, u32[]{:S(2)}, u32[]{:S(2)}) collective-permute-start(f32[3,1,32,128]{3,2,1,0:T(8,128)S(1)} %get-tuple-element.15), channel_id=1, source_target_pairs={{0,1},{1,2},{2,3},{3,0},{4,5},{5,6},{6,7},{7,4},{8,9},{9,10},{10,1... | collective-permute-start | bytes 147464 | tf_op jit(solution)/shard_map/ppermute | solution.py:24
  141.9 2.0 %collective-permute-done.18 = f32[3,1,32,128]{3,2,1,0:T(8,128)S(1)} collective-permute-done((f32[3,1,32,128]{3,2,1,0:T(8,128)S(1)}, f32[3,1,32,128]{3,2,1,0:T(8,128)S(1)}, u32[]{:S(2)}, u32[]{:S(2)}) %collective-permute-start.18) | collective-permute-done | bytes 49184 | tf_op jit(solution)/shard_map/ppermute | solution.py:27
  143.9 1.9 %collective-permute-done.19 = f32[3,1,32,128]{3,2,1,0:T(8,128)S(1)} collective-permute-done((f32[3,1,32,128]{3,2,1,0:T(8,128)S(1)}, f32[3,1,32,128]{3,2,1,0:T(8,128)S(1)}, u32[]{:S(2)}, u32[]{:S(2)}) %collective-permute-start.19) | collective-permute-done | bytes 49184 | tf_op jit(solution)/shard_map/ppermute | solution.py:24
  145.8 1.9 %fusion.113 = f32[1,3,16,32,128]{4,3,2,1,0:T(8,128)} fusion(f32[3,16,32,128]{3,2,1,0:T(8,128)S(1)} %fusion.24, f32[3,16,32,128]{3,2,1,0:T(8,128)S(1)} %fusion.110, f32[3,16,32,127]{3,2,1,0:T(8,128)S(1)} %get-tuple-element.21, f32[3,16,32,1]{3,2,1,0:T(8,128)S(1)} %get-tuple-element.23, f32[3,16,32,1]{3,2,1,0:T(8,128)S(1)} %get-tuple-element.22, ...), kind=kLoop, calls=%fused_computation.167 | loop fusion | flops 4718592 | bytes 7438336 | tf_op jit(solution)/shard_map/broadcast_in_dim | solution.py:97
  (71 shorter events, 8.2 us)
Async XLA Ops:
  6.5 66.2 %all-reduce.3.cloned.1.call-start = ((), (), s32[]{:S(2)}) async-start(), calls=%async_computation | async-start | bytes 2097152 | tf_op jit(solution)/shard_map/psum | solution.py:80
  7.4 67.2 %collective-permute-start = (f32[3,1,32,128]{3,2,1,0:T(8,128)S(1)}, f32[3,1,32,128]{3,2,1,0:T(8,128)S(1)}, u32[]{:S(2)}, u32[]{:S(2)}) collective-permute-start(f32[3,1,32,128]{3,2,1,0:T(8,128)S(1)} %get-tuple-element.107), channel_id=1, source_target_pairs={{1,0},{2,1},{3,2},{0,3},{5,4},{6,5},{7,6},{4,7},{9,8},{10,9},{11,1... | collective-permute-start | bytes 147464 | tf_op jit(solution)/shard_map/ppermute | solution.py:27
  12.5 62.2 %collective-permute-start.1 = (f32[3,1,32,128]{3,2,1,0:T(8,128)S(1)}, f32[3,1,32,128]{3,2,1,0:T(8,128)S(1)}, u32[]{:S(2)}, u32[]{:S(2)}) collective-permute-start(f32[3,1,32,128]{3,2,1,0:T(8,128)S(1)} %get-tuple-element.108), channel_id=1, source_target_pairs={{0,1},{1,2},{2,3},{3,0},{4,5},{5,6},{6,7},{7,4},{8,9},{9,10},{10,1... | collective-permute-start | bytes 147464 | tf_op jit(solution)/shard_map/ppermute | solution.py:24
  14.4 1.1 copy-start
  72.7 1.3 copy-start.5
  74.3 1.1 copy-start.4
  74.4 1.3 copy-start.3
  74.5 1.5 copy-start.1
  74.5 1.7 %copy-start.2 = (f32[3,16,32,127]{3,2,1,0:T(8,128)S(1)}, f32[3,16,32,127]{3,2,1,0:T(8,128)}, u32[]{:S(2)}) copy-start(f32[3,16,32,127]{3,2,1,0:T(8,128)} %get-tuple-element.101) | copy-start | bytes 2340868
  77.9 6.0 %collective-permute-start.3 = (f32[1,32,128]{2,1,0:T(8,128)S(1)}, f32[1,32,128]{2,1,0:T(8,128)S(1)}, u32[]{:S(2)}, u32[]{:S(2)}) collective-permute-start(f32[1,32,128]{2,1,0:T(8,128)S(1)} %get-tuple-element.117), channel_id=1, source_target_pairs={{0,1},{1,2},{2,3},{3,0},{4,5},{5,6},{6,7},{7,4},{8,9},{9,10},{10,1... | collective-permute-start | bytes 49160 | tf_op jit(solution)/shard_map/ppermute | solution.py:24
  79.3 4.6 %collective-permute-start.2 = (f32[1,32,128]{2,1,0:T(8,128)S(1)}, f32[1,32,128]{2,1,0:T(8,128)S(1)}, u32[]{:S(2)}, u32[]{:S(2)}) collective-permute-start(f32[1,32,128]{2,1,0:T(8,128)S(1)} %get-tuple-element.118), channel_id=1, source_target_pairs={{1,0},{2,1},{3,2},{0,3},{5,4},{6,5},{7,6},{4,7},{9,8},{10,9},{11,1... | collective-permute-start | bytes 49160 | tf_op jit(solution)/shard_map/ppermute | solution.py:27
  81.8 4.7 %collective-permute-start.4 = (f32[3,1,32,128]{3,2,1,0:T(8,128)S(1)}, f32[3,1,32,128]{3,2,1,0:T(8,128)S(1)}, u32[]{:S(2)}, u32[]{:S(2)}) collective-permute-start(f32[3,1,32,128]{3,2,1,0:T(8,128)S(1)} %get-tuple-element.94), channel_id=1, source_target_pairs={{1,0},{2,1},{3,2},{0,3},{5,4},{6,5},{7,6},{4,7},{9,8},{10,9},{11,1... | collective-permute-start | bytes 147464 | tf_op jit(solution)/shard_map/ppermute | solution.py:27
  83.3 6.1 %collective-permute-start.5 = (f32[3,1,32,128]{3,2,1,0:T(8,128)S(1)}, f32[3,1,32,128]{3,2,1,0:T(8,128)S(1)}, u32[]{:S(2)}, u32[]{:S(2)}) collective-permute-start(f32[3,1,32,128]{3,2,1,0:T(8,128)S(1)} %get-tuple-element.95), channel_id=1, source_target_pairs={{0,1},{1,2},{2,3},{3,0},{4,5},{5,6},{6,7},{7,4},{8,9},{9,10},{10,1... | collective-permute-start | bytes 147464 | tf_op jit(solution)/shard_map/ppermute | solution.py:24
  91.1 4.1 %collective-permute-start.6 = (f32[3,1,32,128]{3,2,1,0:T(8,128)S(1)}, f32[3,1,32,128]{3,2,1,0:T(8,128)S(1)}, u32[]{:S(2)}, u32[]{:S(2)}) collective-permute-start(f32[3,1,32,128]{3,2,1,0:T(8,128)S(1)} %get-tuple-element.82), channel_id=1, source_target_pairs={{1,0},{2,1},{3,2},{0,3},{5,4},{6,5},{7,6},{4,7},{9,8},{10,9},{11,1... | collective-permute-start | bytes 147464 | tf_op jit(solution)/shard_map/ppermute | solution.py:27
  91.2 6.4 %collective-permute-start.7 = (f32[3,1,32,128]{3,2,1,0:T(8,128)S(1)}, f32[3,1,32,128]{3,2,1,0:T(8,128)S(1)}, u32[]{:S(2)}, u32[]{:S(2)}) collective-permute-start(f32[3,1,32,128]{3,2,1,0:T(8,128)S(1)} %get-tuple-element.83), channel_id=1, source_target_pairs={{0,1},{1,2},{2,3},{3,0},{4,5},{5,6},{6,7},{7,4},{8,9},{9,10},{10,1... | collective-permute-start | bytes 147464 | tf_op jit(solution)/shard_map/ppermute | solution.py:24
  99.4 4.1 %collective-permute-start.8 = (f32[3,1,32,128]{3,2,1,0:T(8,128)S(1)}, f32[3,1,32,128]{3,2,1,0:T(8,128)S(1)}, u32[]{:S(2)}, u32[]{:S(2)}) collective-permute-start(f32[3,1,32,128]{3,2,1,0:T(8,128)S(1)} %get-tuple-element.72), channel_id=1, source_target_pairs={{1,0},{2,1},{3,2},{0,3},{5,4},{6,5},{7,6},{4,7},{9,8},{10,9},{11,1... | collective-permute-start | bytes 147464 | tf_op jit(solution)/shard_map/ppermute | solution.py:27
  99.5 6.0 %collective-permute-start.9 = (f32[3,1,32,128]{3,2,1,0:T(8,128)S(1)}, f32[3,1,32,128]{3,2,1,0:T(8,128)S(1)}, u32[]{:S(2)}, u32[]{:S(2)}) collective-permute-start(f32[3,1,32,128]{3,2,1,0:T(8,128)S(1)} %get-tuple-element.73), channel_id=1, source_target_pairs={{0,1},{1,2},{2,3},{3,0},{4,5},{5,6},{6,7},{7,4},{8,9},{9,10},{10,1... | collective-permute-start | bytes 147464 | tf_op jit(solution)/shard_map/ppermute | solution.py:24
  107.4 4.4 %collective-permute-start.10 = (f32[3,1,32,128]{3,2,1,0:T(8,128)S(1)}, f32[3,1,32,128]{3,2,1,0:T(8,128)S(1)}, u32[]{:S(2)}, u32[]{:S(2)}) collective-permute-start(f32[3,1,32,128]{3,2,1,0:T(8,128)S(1)} %get-tuple-element.62), channel_id=1, source_target_pairs={{1,0},{2,1},{3,2},{0,3},{5,4},{6,5},{7,6},{4,7},{9,8},{10,9},{11,1... | collective-permute-start | bytes 147464 | tf_op jit(solution)/shard_map/ppermute | solution.py:27
  107.4 6.1 %collective-permute-start.11 = (f32[3,1,32,128]{3,2,1,0:T(8,128)S(1)}, f32[3,1,32,128]{3,2,1,0:T(8,128)S(1)}, u32[]{:S(2)}, u32[]{:S(2)}) collective-permute-start(f32[3,1,32,128]{3,2,1,0:T(8,128)S(1)} %get-tuple-element.63), channel_id=1, source_target_pairs={{0,1},{1,2},{2,3},{3,0},{4,5},{5,6},{6,7},{7,4},{8,9},{9,10},{10,1... | collective-permute-start | bytes 147464 | tf_op jit(solution)/shard_map/ppermute | solution.py:24
  115.4 4.1 %collective-permute-start.12 = (f32[3,1,32,128]{3,2,1,0:T(8,128)S(1)}, f32[3,1,32,128]{3,2,1,0:T(8,128)S(1)}, u32[]{:S(2)}, u32[]{:S(2)}) collective-permute-start(f32[3,1,32,128]{3,2,1,0:T(8,128)S(1)} %get-tuple-element.52), channel_id=1, source_target_pairs={{1,0},{2,1},{3,2},{0,3},{5,4},{6,5},{7,6},{4,7},{9,8},{10,9},{11,1... | collective-permute-start | bytes 147464 | tf_op jit(solution)/shard_map/ppermute | solution.py:27
  116.2 5.9 %collective-permute-start.13 = (f32[3,1,32,128]{3,2,1,0:T(8,128)S(1)}, f32[3,1,32,128]{3,2,1,0:T(8,128)S(1)}, u32[]{:S(2)}, u32[]{:S(2)}) collective-permute-start(f32[3,1,32,128]{3,2,1,0:T(8,128)S(1)} %get-tuple-element.53), channel_id=1, source_target_pairs={{0,1},{1,2},{2,3},{3,0},{4,5},{5,6},{6,7},{7,4},{8,9},{9,10},{10,1... | collective-permute-start | bytes 147464 | tf_op jit(solution)/shard_map/ppermute | solution.py:24
  123.9 4.5 %collective-permute-start.14 = (f32[3,1,32,128]{3,2,1,0:T(8,128)S(1)}, f32[3,1,32,128]{3,2,1,0:T(8,128)S(1)}, u32[]{:S(2)}, u32[]{:S(2)}) collective-permute-start(f32[3,1,32,128]{3,2,1,0:T(8,128)S(1)} %get-tuple-element.42), channel_id=1, source_target_pairs={{1,0},{2,1},{3,2},{0,3},{5,4},{6,5},{7,6},{4,7},{9,8},{10,9},{11,1... | collective-permute-start | bytes 147464 | tf_op jit(solution)/shard_map/ppermute | solution.py:27
  124.2 5.9 %collective-permute-start.15 = (f32[3,1,32,128]{3,2,1,0:T(8,128)S(1)}, f32[3,1,32,128]{3,2,1,0:T(8,128)S(1)}, u32[]{:S(2)}, u32[]{:S(2)}) collective-permute-start(f32[3,1,32,128]{3,2,1,0:T(8,128)S(1)} %get-tuple-element.43), channel_id=1, source_target_pairs={{0,1},{1,2},{2,3},{3,0},{4,5},{5,6},{6,7},{7,4},{8,9},{9,10},{10,1... | collective-permute-start | bytes 147464 | tf_op jit(solution)/shard_map/ppermute | solution.py:24
  132.0 4.1 %collective-permute-start.16 = (f32[3,1,32,128]{3,2,1,0:T(8,128)S(1)}, f32[3,1,32,128]{3,2,1,0:T(8,128)S(1)}, u32[]{:S(2)}, u32[]{:S(2)}) collective-permute-start(f32[3,1,32,128]{3,2,1,0:T(8,128)S(1)} %get-tuple-element.32), channel_id=1, source_target_pairs={{1,0},{2,1},{3,2},{0,3},{5,4},{6,5},{7,6},{4,7},{9,8},{10,9},{11,1... | collective-permute-start | bytes 147464 | tf_op jit(solution)/shard_map/ppermute | solution.py:27
  132.0 5.9 %collective-permute-start.17 = (f32[3,1,32,128]{3,2,1,0:T(8,128)S(1)}, f32[3,1,32,128]{3,2,1,0:T(8,128)S(1)}, u32[]{:S(2)}, u32[]{:S(2)}) collective-permute-start(f32[3,1,32,128]{3,2,1,0:T(8,128)S(1)} %get-tuple-element.33), channel_id=1, source_target_pairs={{0,1},{1,2},{2,3},{3,0},{4,5},{5,6},{6,7},{7,4},{8,9},{9,10},{10,1... | collective-permute-start | bytes 147464 | tf_op jit(solution)/shard_map/ppermute | solution.py:24
  139.8 4.1 %collective-permute-start.18 = (f32[3,1,32,128]{3,2,1,0:T(8,128)S(1)}, f32[3,1,32,128]{3,2,1,0:T(8,128)S(1)}, u32[]{:S(2)}, u32[]{:S(2)}) collective-permute-start(f32[3,1,32,128]{3,2,1,0:T(8,128)S(1)} %get-tuple-element.14), channel_id=1, source_target_pairs={{1,0},{2,1},{3,2},{0,3},{5,4},{6,5},{7,6},{4,7},{9,8},{10,9},{11,1... | collective-permute-start | bytes 147464 | tf_op jit(solution)/shard_map/ppermute | solution.py:27
  139.9 5.9 %collective-permute-start.19 = (f32[3,1,32,128]{3,2,1,0:T(8,128)S(1)}, f32[3,1,32,128]{3,2,1,0:T(8,128)S(1)}, u32[]{:S(2)}, u32[]{:S(2)}) collective-permute-start(f32[3,1,32,128]{3,2,1,0:T(8,128)S(1)} %get-tuple-element.15), channel_id=1, source_target_pairs={{0,1},{1,2},{2,3},{3,0},{4,5},{5,6},{6,7},{7,4},{8,9},{9,10},{10,1... | collective-permute-start | bytes 147464 | tf_op jit(solution)/shard_map/ppermute | solution.py:24
Sparse Core Ops, SparseCore 0:
  14.5 58.1 all-reduce.2
where the time goes:
time: 155 us
  waiting for transfers between devices  88.4 us (57%)
  starting transfers between devices  25.6 us (17%)
  other arithmetic  13.8 us (9%)
  between operations  13.8 us (9%)
  local copies, waits for them, and re-layouts  13 us (8%)
    psum x1, waiting for transfers between devices, per_device(): total, squares = lax.psum((flow, jnp.sum(flow * flow, 0)), 'member')  54.4 us
    ppermute x10, waiting for transfers between devices, with_halo(): lax.ppermute(lax.slice_in_dim(block, 0, width, axis=dim), axis, backward)  17 us
    ppermute x10, waiting for transfers between devices, with_halo(): lax.ppermute(lax.slice_in_dim(block, block.shape[dim] - width, None, axis...  17 us
    ppermute x10, starting transfers between devices, with_halo(): lax.ppermute(lax.slice_in_dim(block, block.shape[dim] - width, None, axis...  15.1 us
    ppermute x10, starting transfers between devices, with_halo(): lax.ppermute(lax.slice_in_dim(block, 0, width, axis=dim), axis, backward)  10.5 us
    add x7, other arithmetic, sweep(): return center + step_size * (source - image) / diagonal  7.2 us
    slice x14, local copies, waits for them, and re-layouts, sweep(): jnp.roll(center, 1, 3)  4.09 us
  transfers between devices with their start and end apart: 21, of which 17 were waited for; matrix products, arithmetic and copies ran while one was open for 5% of the time, Pallas kernels for 0%

commit v1 on v0

v1 whole, which is shorter than its diff:
```python
import functools
import math

import jax
import jax.numpy as jnp
from jax import lax
from jax.experimental import pallas as pl
from jax.experimental.pallas import tpu as pltpu
from jax.sharding import PartitionSpec as P

SWEEPS = 8


TIME_STEP = 0.25
EDDY_COEFF = 1.0
BASE_VISCOSITY = 1.0
LOWER_EDGE = 0.1
UPPER_EDGE = 1.9

ROWS = 8
PIECES = ((0, 4), (4, 8))
EARLY = 4
VMEM_LIMIT = 40 * 1024 * 1024


def step_sizes(sweep_count):
    middle = (UPPER_EDGE + LOWER_EDGE) / 2
    radius = (UPPER_EDGE - LOWER_EDGE) / 2
    return [
        1.0 / (middle + radius * math.cos(math.pi * (2 * position + 1) / (2 * sweep_count)))
        for position in range(sweep_count)
    ]


def north(planes):
    return planes[1:] + [pltpu.roll(planes[0], ROWS - 1, 0)]


def south(planes):
    return [pltpu.roll(planes[-1], 1, 0)] + planes[:-1]


def upper(plane):
    return pltpu.roll(plane, plane.shape[-1] - 1, 1)


def lower(plane):
    return pltpu.roll(plane, 1, 1)


def rows_of(j, count):
    return pl.ds(j, ROWS, stride=count)


def parity():
    return lax.rem(lax.axis_index("member"), 2)


def for_layers(count, body, unroll=1):
    def step(i, carry):
        body(i)
        return carry

    lax.fori_loop(0, count, step, 0, unroll=unroll)


def arrange_kernel(vel, force, vp, gp, first, last):
    comps, nx, planes = vp.shape[:3]

    def body(x):
        for c in range(comps):
            for j in range(planes):
                value = vel[0, c, x, rows_of(j, planes), :]
                vp[c, x, j] = value
                gp[c, x, j] = value + TIME_STEP * force[0, c, x, rows_of(j, planes), :]

    for_layers(nx, body, 2)
    first[...] = vp[:, :1]
    last[...] = vp[:, nx - 1 :]


def sums_kernel(pieces, vp, other, *outs):
    comps, nx, planes = vp.shape[:3]
    side = parity()
    for (near, far), out in zip(pieces, outs):
        start = jnp.where(side == 0, near, nx - far)

        def body(i, out=out, start=start):
            x = start + i
            for j in range(planes):
                squares = None
                for c in range(comps):
                    a = vp[c, x, j]
                    b = other[0, c, x, rows_of(j, planes), :]
                    out[c, i, j] = a + b
                    both = a * a + b * b
                    squares = both if squares is None else squares + both
                out[comps, i, j] = squares

        for_layers(far - near, body)


def stats_kernel(members, add_two, *refs):
    out = refs[-1]
    comps, layers, planes = out.shape[0] - 1, out.shape[1], out.shape[2]

    def body(i):
        for j in range(planes):
            def total(c):
                value = refs[0][c, i, j]
                return value + refs[1][c, i, j] if add_two else value

            spread = total(comps) * (1.0 / members)
            for c in range(comps):
                mean = total(c) * (1.0 / members)
                out[c, i, j] = mean
                spread = spread - mean * mean
            out[comps, i, j] = BASE_VISCOSITY + EDDY_COEFF * TIME_STEP * spread

    for_layers(layers, body)


def source_kernel(piece, vp, gp, below, above, mine, theirs, out_mine, out_theirs):
    comps, nx, planes = vp.shape[:3]
    near, far = piece
    side = parity()
    for which, stats, out in ((side, mine, out_mine), (1 - side, theirs, out_theirs)):
        start = jnp.where(which == 0, near, nx - far)

        def body(i, stats=stats, out=out, start=start):
            x = start + i
            down, up = jnp.maximum(x - 1, 0), jnp.minimum(x + 1, nx - 1)
            for c in range(comps):
                here = [vp[c, x, j] for j in range(planes)]
                ns, ss = north(here), south(here)
                for j in range(planes):
                    west = jnp.where(x == 0, below[c, 0, j], vp[c, down, j])
                    east = jnp.where(x == nx - 1, above[c, 0, j], vp[c, up, j])
                    transport = (
                        stats[0, i, j] * (east - west)
                        + stats[1, i, j] * (ns[j] - ss[j])
                        + stats[2, i, j] * (upper(here[j]) - lower(here[j]))
                    )
                    out[c, i, j] = gp[c, x, j] - (0.5 * TIME_STEP) * transport

        for_layers(far - near, body)


def relax(load_center, load_out, load_in, coef, load_source, store, comps, planes, step_size, flip):
    near_coef, far_coef = (0, 1) if not flip else (1, 0)
    for c in range(comps):
        here = [load_center(c, j) for j in range(planes)]
        ns, ss = north(here), south(here)
        for j in range(planes):
            image = load_source(c, j)
            image = image + coef(near_coef, j) * load_in(c, j)
            image = image + coef(far_coef, j) * load_out(c, j)
            image = image + coef(2, j) * ns[j] + coef(3, j) * ss[j]
            image = image + coef(4, j) * upper(here[j]) + coef(5, j) * lower(here[j])
            store(c, j, (1.0 - step_size) * here[j] + step_size * image)


def early_kernel(pieces, early, sizes, count, *refs):
    number = len(pieces)
    n_early = sum(1 for piece in pieces if piece[1] <= early)
    refs = list(refs)

    def take(n):
        head = refs[:n]
        del refs[:n]
        return head

    src_mine, src_theirs = take(number), take(number)
    stat_mine, stat_theirs = take(number), take(number)
    visc_got, visc_other = take(1)[0], take(1)[0]
    halo_mine, halo_theirs = take(n_early), take(n_early)
    coef, scaled, edges, middle = take(4)
    visc, field = take(2)
    depth = len(sizes)
    comps, planes = scaled.shape[0], scaled.shape[2]
    side = parity()

    for which, stats, srcs in ((side, stat_mine, src_mine), (1 - side, stat_theirs, src_theirs)):
        for (near, far), stat, src in zip(pieces, stats, srcs):
            start = jnp.where(which == 0, near, count - far)
            visc[pl.ds(depth + start, far - near)] = stat[comps]
            for c in range(comps):
                field[0, c, pl.ds(early + start, far - near)] = src[c]
    for which, got in ((side, visc_got), (1 - side, visc_other)):
        for near, far in pieces:
            start = jnp.where(which == 0, depth + count + near, depth - far)
            visc[pl.ds(start, far - near)] = got[near:far]
    for which, halos in ((side, halo_mine), (1 - side, halo_theirs)):
        for (near, far), halo in zip(pieces, halos):
            start = jnp.where(which == 0, early + count + near, early - far)
            for c in range(comps):
                field[0, c, pl.ds(start, far - near)] = halo[c]

    half = 0.5 * TIME_STEP

    def coefs(i):
        x = i + 1
        here = [visc[x, j] for j in range(planes)]
        ns, ss = north(here), south(here)
        for j in range(planes):
            faces = [
                here[j] + visc[x + 1, j],
                here[j] + visc[x - 1, j],
                here[j] + ns[j],
                here[j] + ss[j],
                here[j] + upper(here[j]),
                here[j] + lower(here[j]),
            ]
            total = (faces[0] + faces[1]) + (faces[2] + faces[3]) + (faces[4] + faces[5])
            inverse = 1.0 / (1.0 + half * total)
            scale = half * inverse
            for a in range(6):
                coef[a, x, j] = faces[a] * scale
            coef[6, x, j] = inverse

    for_layers(count + 2 * depth - 2, coefs)

    def scale_source(i):
        x = i + depth - early
        for c in range(comps):
            for j in range(planes):
                scaled[c, x, j] = field[0, c, i, j] * coef[6, x, j]

    for_layers(count + 2 * early, scale_source)

    total = count + 2 * early
    for k in range(depth + 1):
        if k:
            now, before = field.at[k], field.at[k - 1]

            def body(i, k=k, now=now, before=before):
                p = k + i
                x = p + depth - early

                def store(c, j, value):
                    if k < depth:
                        now[c, p, j] = value
                    else:
                        middle[c, i, rows_of(j, planes), :] = value

                relax(
                    lambda c, j: before[c, p, j],
                    lambda c, j: before[c, p - 1, j],
                    lambda c, j: before[c, p + 1, j],
                    lambda a, j: coef[a, x, j],
                    lambda c, j: scaled[c, x, j],
                    store,
                    comps,
                    planes,
                    sizes[k - 1],
                    False,
                )

            for_layers(total - 2 * k, body, 2)
        if k < depth:
            for c in range(comps):
                edges[k, 0, c, 0] = field[k, c, k]
                edges[k, 0, c, 1] = field[k, c, k + 1]
                edges[k, 1, c, 0] = field[k, c, total - 1 - k]
                edges[k, 1, c, 1] = field[k, c, total - 2 - k]


def late_kernel(pieces, early, sizes, count, *refs):
    n_late = sum(1 for piece in pieces if piece[1] > early)
    late = [piece for piece in pieces if piece[1] > early]
    refs = list(refs)

    def take(n):
        head = refs[:n]
        del refs[:n]
        return head

    coef, scaled, edges, middle = take(4)
    halo_mine, halo_theirs = take(n_late), take(n_late)
    out = take(1)[0]
    field, source, tail, sems = take(4)
    depth = len(sizes)
    width = depth - early
    comps, planes = scaled.shape[0], scaled.shape[2]
    side = parity()
    total = count + 2 * depth

    mid = pltpu.make_async_copy(middle, out.at[0, :, width : count - width], sems.at[0])
    mid.start()

    for which, halos in ((side, halo_mine), (1 - side, halo_theirs)):
        high = which == 0
        slot = 1 - which
        for (near, far), halo in zip(late, halos):
            for i in range(far - near):
                position = jnp.where(high, depth - 1 - near - i, depth - far + i)
                x = jnp.where(high, depth + count + near + i, depth - far + i)
                for c in range(comps):
                    for j in range(planes):
                        value = halo[c, i, j]
                        field[0, slot, c, position, j] = value
                        source[slot, c, position, j] = value * coef[6, x, j]
    for i in range(width, 2 * depth - early):
        for c in range(comps):
            source[0, c, i] = scaled[c, i]
            source[1, c, i] = scaled[c, total - 1 - i]
    for s in range(2):
        for c in range(comps):
            for e in range(2):
                field[0, s, c, width + e] = edges[0, s, c, e]

    def sweep(k, carry):
        step_size = jnp.float32(sizes[0])
        for position in range(1, depth):
            step_size = jnp.where(k == position + 1, jnp.float32(sizes[position]), step_size)
        for s in range(2):
            for r in range(width):
                inner = k + r
                x = inner if s == 0 else total - 1 - inner

                def store(c, j, value, s=s, r=r):
                    field[k, s, c, r, j] = value

                relax(
                    lambda c, j: field[k - 1, s, c, r + 1, j],
                    lambda c, j: field[k - 1, s, c, r, j],
                    lambda c, j: field[k - 1, s, c, r + 2, j],
                    lambda a, j: coef[a, x, j],
                    lambda c, j: source[s, c, inner, j],
                    store,
                    comps,
                    planes,
                    step_size,
                    s == 1,
                )
        edge = jnp.minimum(k, depth - 1)
        for s in range(2):
            for c in range(comps):
                for e in range(2):
                    field[k, s, c, width + e] = edges[edge, s, c, e]
        return carry

    lax.fori_loop(1, depth + 1, sweep, 0)
    copies = []
    for s in range(2):
        for r in range(width):
            place = r if s == 0 else width - 1 - r
            for c in range(comps):
                for j in range(planes):
                    tail[s, c, place, rows_of(j, planes), :] = field[depth, s, c, r, j]
        where = 0 if s == 0 else count - width
        copy = pltpu.make_async_copy(
            tail.at[s], out.at[0, :, where : where + width], sems.at[1 + s]
        )
        copy.start()
        copies.append(copy)
    for copy in copies:
        copy.wait()
    mid.wait()


def vmem(n):
    return [pl.BlockSpec(memory_space=pltpu.VMEM)] * n


def call(kernel, outs, ins, flops, scratch=(), any_out=False, name=None):
    shapes = [jax.ShapeDtypeStruct(shape, jnp.float32) for shape in outs]
    size = 4 * sum(math.prod(shape) for shape in outs) + 4 * sum(x.size for x in ins)
    result = pl.pallas_call(
        kernel,
        out_shape=shapes,
        in_specs=vmem(len(ins)),
        out_specs=[pl.BlockSpec(memory_space=pl.ANY)] * len(outs) if any_out else vmem(len(outs)),
        scratch_shapes=list(scratch),
        compiler_params=pltpu.CompilerParams(vmem_limit_bytes=VMEM_LIMIT),
        cost_estimate=pl.CostEstimate(flops=flops, bytes_accessed=size, transcendentals=0),
        name=name,
    )(*ins)
    return result


def fast(velocity, forcing):
    members = lax.axis_size("member")
    subs = lax.axis_size("sub")
    _, comps, nx, ny, nz = velocity.shape
    planes = ny // ROWS
    layer = (planes, ROWS, nz)
    sizes = step_sizes(SWEEPS)
    depth = SWEEPS
    bits = members.bit_length() - 1
    f32 = jnp.float32

    swap = [(m, m ^ 1) for m in range(members)]

    def pair(step):
        order = [list(range(1, bits)), list(range(2, bits)) + [1]]
        return [(m, m ^ (1 << order[m % 2][step])) for m in range(members)]

    def along(mine):
        moves = []
        for m in range(members):
            step = -1 if (m % 2 == 0) == mine else 1
            for s in range(subs):
                moves.append((m * subs + s, m * subs + (s + step) % subs))
        return moves

    other = lax.ppermute(velocity, "member", swap)
    vp, gp, first, last = call(
        arrange_kernel,
        [(comps, nx, *layer)] * 2 + [(comps, 1, *layer)] * 2,
        [velocity, forcing],
        10 * velocity.size,
        name="arrange",
    )
    above = lax.ppermute(first, "sub", [(s, (s - 1) % subs) for s in range(subs)])
    below = lax.ppermute(last, "sub", [(s, (s + 1) % subs) for s in range(subs)])
    sums = call(
        functools.partial(sums_kernel, PIECES),
        [(comps + 1, far - near, *layer) for near, far in PIECES],
        [vp, other],
        6 * velocity.size,
        name="sums",
    )
    stats_mine, stats_theirs, src_mine, src_theirs, halo_mine, halo_theirs = [], [], [], [], [], []
    for (near, far), part in zip(PIECES, sums):
        terms = [part]
        for step in range(bits - 1):
            part = terms[0] + terms[1] if len(terms) == 2 else terms[0]
            terms = [part, lax.ppermute(part, "member", pair(step))]
        stats = call(
            functools.partial(stats_kernel, members, len(terms) == 2),
            [(comps + 1, far - near, *layer)],
            terms,
            10 * part.size,
            name="stats",
        )[0]
        stats_mine.append(stats)
        stats_theirs.append(lax.ppermute(stats, "member", swap))
        mine, theirs = call(
            functools.partial(source_kernel, (near, far)),
            [(comps, far - near, *layer)] * 2,
            [vp, gp, below, above, stats, stats_theirs[-1]],
            20 * part.size,
            name="source",
        )
        src_mine.append(mine)
        src_theirs.append(theirs)
        halo_mine.append(lax.ppermute(mine, ("member", "sub"), along(True)))
        halo_theirs.append(lax.ppermute(theirs, ("member", "sub"), along(False)))
    visc = jnp.concatenate([stats[comps] for stats in stats_mine], 0)
    visc_got = lax.ppermute(visc, ("member", "sub"), along(True))
    visc_other = lax.ppermute(visc_got, "member", swap)

    early = EARLY
    n_early = sum(1 for piece in PIECES if piece[1] <= early)
    width = depth - early
    coef, scaled, edges, middle = call(
        functools.partial(early_kernel, PIECES, early, sizes, nx),
        [
            (7, nx + 2 * depth, *layer),
            (comps, nx + 2 * depth, *layer),
            (depth, 2, comps, 2, *layer),
            (comps, nx - 2 * width, ny, nz),
        ],
        src_mine + src_theirs + stats_mine + stats_theirs + [visc_got, visc_other]
        + halo_mine[:n_early] + halo_theirs[:n_early],
        20 * 8 * velocity.size,
        scratch=[
            pltpu.VMEM((nx + 2 * depth, *layer), f32),
            pltpu.VMEM((depth + 1, comps, nx + 2 * early, *layer), f32),
        ],
        name="early",
    )
    return call(
        functools.partial(late_kernel, PIECES, early, sizes, nx),
        [velocity.shape],
        [coef, scaled, edges, middle] + halo_mine[n_early:] + halo_theirs[n_early:],
        20 * 4 * velocity.size,
        scratch=[
            pltpu.VMEM((depth + 1, 2, comps, width + 2, *layer), f32),
            pltpu.VMEM((2, comps, 2 * depth, *layer), f32),
            pltpu.VMEM((2, comps, width, ny, nz), f32),
            pltpu.SemaphoreType.DMA((3,)),
        ],
        any_out=True,
        name="late",
    )[0]


def solution(mesh):
    in_specs = (P("member", None, "sub", None, None), P("member", None, "sub", None, None))
    out_specs = P("member", None, "sub", None, None)
    return jax.shard_map(fast, mesh=mesh, in_specs=in_specs, out_specs=out_specs, check_vma=False)
```

time: 155 us -> 76.5 us (0.49)
  waiting for transfers between devices: 88.4 us -> 16.7 us
  Pallas kernels: 0 us -> 33.6 us
  other arithmetic: 13.8 us -> 0.08 us
  between operations: 13.8 us -> 0.15 us
  local copies, waits for them, and re-layouts: 13 us -> 2.28 us
  starting transfers between devices: 25.6 us -> 23.5 us
    psum x1 -> x0, waiting for transfers between devices: 54.4 us -> none  [per_device(): total, squares = lax.psum((flow, jnp.sum(flow * flow, 0)), 'member')]
    pallas_call x0 -> x8, Pallas kernels: none -> 33.6 us  [call(): pl.pallas_call(kernel, out_shape=shapes, in_specs=vmem(len(ins)), out_spe...]
    ppermute x20 -> x15, waiting for transfers between devices: 34 us -> 16.7 us  [the longest x4 9.23 us: fast(): terms = [part, lax.ppermute(part, 'member', pair(step))]]
    slice x50 -> x0, local copies, waits for them, and re-layouts: 10.3 us -> none  [the longest x14 4.09 us: sweep(): jnp.roll(center, 1, 3)]
    add x10 -> x2, other arithmetic: 8.54 us -> 0.07 us  [fast(): part = terms[0] + terms[1] if len(terms) == 2 else terms[0]]
    reduce_sum x2 -> x0, other arithmetic: 3.27 us -> none  [the longest x1 1.94 us: per_device(): total, squares = lax.psum((flow, jnp.sum(flow * flow, 0)), 'member')]
    ppermute x20 -> x15, starting transfers between devices: 25.6 us -> 23.5 us  [the longest x2 7.74 us: fast(): halo_mine.append(lax.ppermute(mine, ('member', 'sub'), along(True)))]
    broadcast_in_dim x1 -> x0, other arithmetic: 1.92 us -> none  [per_device(): return field[None]]
  transfers between devices with their start and end apart: 21 -> 15, of which waited for: 17 -> 8; matrix products, arithmetic and copies ran while one was open for 5% -> 0% of each run, Pallas kernels for 0% -> 16%
where the time goes in v1:
time: 76.5 us; the launch traced here: 76.3 us
  Pallas kernels  33.6 us (44%)
  starting transfers between devices  23.5 us (31%)
  waiting for transfers between devices  16.7 us (22%)
  local copies, waits for them, and re-layouts  2.28 us (3%)
    pallas_call x8, Pallas kernels, call(): pl.pallas_call(kernel, out_shape=shapes, in_specs=vmem(len(ins)), out_spe...  33.6 us
    ppermute x4, waiting for transfers between devices, fast(): terms = [part, lax.ppermute(part, 'member', pair(step))]  9.23 us
    ppermute x2, starting transfers between devices, fast(): halo_mine.append(lax.ppermute(mine, ('member', 'sub'), along(True)))  7.74 us
    ppermute x4, starting transfers between devices, fast(): terms = [part, lax.ppermute(part, 'member', pair(step))]  7.2 us
    ppermute x1, starting transfers between devices, fast(): visc_got = lax.ppermute(visc, ('member', 'sub'), along(True))  4.15 us
    ppermute x1, starting transfers between devices, fast(): lax.ppermute(first, 'sub', [(s, (s - 1) % subs) for s in range(subs)])  3.82 us
    ppermute x2, waiting for transfers between devices, fast(): halo_mine.append(lax.ppermute(mine, ('member', 'sub'), along(True)))  3.57 us
    unnamed x4, local copies, waits for them, and re-layouts  2.27 us
  transfers between devices with their start and end apart: 15, of which 8 were waited for; matrix products, arithmetic and copies ran while one was open for 0% of the time, Pallas kernels for 16%

profile of v1, /device:TPU:0, one launch (start us, length us, event | category | flops | bytes accessed | tf_op | source)
XLA Modules:
  0.0 76.3 jit_solution(10759855619919784414)
XLA Ops:
  0.0 0.5 collective-permute-start.2
  0.5 0.0 copy-start
  0.5 1.1 %copy-done = f32[1,3,16,32,128]{4,3,2,1,0:T(8,128)S(1)} copy-done((f32[1,3,16,32,128]{4,3,2,1,0:T(8,128)S(1)}, f32[1,3,16,32,128]{4,3,2,1,0:T(8,128)}, u32[]{:S(2)}) %copy-start) | copy-done | bytes 786456
  1.6 0.0 copy-start.1
  1.6 1.1 %copy-done.1 = f32[1,3,16,32,128]{4,3,2,1,0:T(8,128)S(1)} copy-done((f32[1,3,16,32,128]{4,3,2,1,0:T(8,128)S(1)}, f32[1,3,16,32,128]{4,3,2,1,0:T(8,128)}, u32[]{:S(2)}) %copy-start.1) | copy-done | bytes 786456
  2.7 0.2 arrange.1
  2.9 0.0 collective-permute-done.2.other
  2.9 0.1 sums.1
  3.0 2.6 %collective-permute-start.6 = (f32[4,4,4,8,128]{4,3,2,1,0:T(8,128)S(1)}, f32[4,4,4,8,128]{4,3,2,1,0:T(8,128)S(1)}, u32[]{:S(2)}, u32[]{:S(2)}) collective-permute-start(f32[4,4,4,8,128]{4,3,2,1,0:T(8,128)S(1)} %get-tuple-element.25), channel_id=1, source_target_pairs={{0,8},{4,20},{8,0},{12,28},{16,24},{20,4},{24,16},{28,12},{1,9},{5... | collective-permute-start | bytes 786440 | tf_op jit(solution)/shard_map/ppermute | solution.py:429
  5.6 0.1 collective-permute-start.3
  5.7 4.3 %collective-permute-done.6 = f32[4,4,4,8,128]{4,3,2,1,0:T(8,128)S(1)} collective-permute-done((f32[4,4,4,8,128]{4,3,2,1,0:T(8,128)S(1)}, f32[4,4,4,8,128]{4,3,2,1,0:T(8,128)S(1)}, u32[]{:S(2)}, u32[]{:S(2)}) %collective-permute-start.6) | collective-permute-done | bytes 262176 | tf_op jit(solution)/shard_map/ppermute | solution.py:429
  10.0 2.1 %collective-permute-start.7 = (f32[4,4,4,8,128]{4,3,2,1,0:T(8,128)S(1)}, f32[4,4,4,8,128]{4,3,2,1,0:T(8,128)S(1)}, u32[]{:S(2)}, u32[]{:S(2)}) collective-permute-start(f32[4,4,4,8,128]{4,3,2,1,0:T(8,128)S(1)} %add.7.refs_0_), channel_id=1, source_target_pairs={{0,16},{4,12},{8,24},{12,4},{16,0},{20,28},{24,8},{28,20},{1,17},{... | collective-permute-start | bytes 786440 | tf_op jit(solution)/shard_map/ppermute | solution.py:429
  12.1 0.8 %collective-permute-done.3 = f32[4,4,4,8,128]{4,3,2,1,0:T(8,128)S(1)} collective-permute-done((f32[4,4,4,8,128]{4,3,2,1,0:T(8,128)S(1)}, f32[4,4,4,8,128]{4,3,2,1,0:T(8,128)S(1)}, u32[]{:S(2)}, u32[]{:S(2)}) %collective-permute-start.3) | collective-permute-done | bytes 262176 | tf_op jit(solution)/shard_map/ppermute | solution.py:429
  12.9 2.4 %collective-permute-start.4 = (f32[4,4,4,8,128]{4,3,2,1,0:T(8,128)S(1)}, f32[4,4,4,8,128]{4,3,2,1,0:T(8,128)S(1)}, u32[]{:S(2)}, u32[]{:S(2)}) collective-permute-start(f32[4,4,4,8,128]{4,3,2,1,0:T(8,128)S(1)} %add.6.refs_0_), channel_id=1, source_target_pairs={{0,16},{4,12},{8,24},{12,4},{16,0},{20,28},{24,8},{28,20},{1,17},{... | collective-permute-start | bytes 786440 | tf_op jit(solution)/shard_map/ppermute | solution.py:429
  15.3 1.1 %collective-permute-done.7.refs_1_ = f32[4,4,4,8,128]{4,3,2,1,0:T(8,128)S(1)} collective-permute-done((f32[4,4,4,8,128]{4,3,2,1,0:T(8,128)S(1)}, f32[4,4,4,8,128]{4,3,2,1,0:T(8,128)S(1)}, u32[]{:S(2)}, u32[]{:S(2)}) %collective-permute-start.7) | collective-permute-done | bytes 262176 | tf_op jit(solution)/shard_map/ppermute | solution.py:429
  16.5 0.1 stats.3.mine.refs_5_
  16.5 0.1 collective-permute-start.8
  16.6 3.1 %collective-permute-done.4.refs_1_ = f32[4,4,4,8,128]{4,3,2,1,0:T(8,128)S(1)} collective-permute-done((f32[4,4,4,8,128]{4,3,2,1,0:T(8,128)S(1)}, f32[4,4,4,8,128]{4,3,2,1,0:T(8,128)S(1)}, u32[]{:S(2)}, u32[]{:S(2)}) %collective-permute-start.4) | collective-permute-done | bytes 262176 | tf_op jit(solution)/shard_map/ppermute | solution.py:429
  19.7 0.1 stats.2.mine.refs_4_
  19.8 0.1 collective-permute-start.5
  19.9 4.2 %collective-permute-start.9 = (f32[8,4,8,128]{3,2,1,0:T(8,128)S(1)}, f32[8,4,8,128]{3,2,1,0:T(8,128)S(1)}, u32[]{:S(2)}, u32[]{:S(2)}) collective-permute-start(f32[8,4,8,128]{3,2,1,0:T(8,128)S(1)} %pad_maximum_fusion), channel_id=1, source_target_pairs={{0,3},{1,0},{2,1},{3,2},{4,5},{5,6},{6,7},{7,4},{8,11},{9,8},{10,9... | collective-permute-start | bytes 393224 | tf_op jit(solution)/shard_map/ppermute | solution.py:451
  24.0 0.0 collective-permute-start
  24.0 3.8 %collective-permute-start.1 = (f32[3,1,4,8,128]{4,3,2,1,0:T(8,128)S(1)}, f32[3,1,4,8,128]{4,3,2,1,0:T(8,128)S(1)}, u32[]{:S(2)}, u32[]{:S(2)}) collective-permute-start(f32[3,1,4,8,128]{4,3,2,1,0:T(8,128)S(1)} %get-tuple-element.22), channel_id=1, source_target_pairs={{0,3},{1,0},{2,1},{3,2},{4,7},{5,4},{6,5},{7,6},{8,11},{9,8},{10,9... | collective-permute-start | bytes 147464 | tf_op jit(solution)/shard_map/ppermute | solution.py:415
  27.9 2.1 %collective-permute-done.below = f32[3,1,4,8,128]{4,3,2,1,0:T(8,128)S(1)} collective-permute-done((f32[3,1,4,8,128]{4,3,2,1,0:T(8,128)S(1)}, f32[3,1,4,8,128]{4,3,2,1,0:T(8,128)S(1)}, u32[]{:S(2)}, u32[]{:S(2)}) %collective-permute-start) | collective-permute-done | bytes 49184 | tf_op jit(solution)/shard_map/ppermute | solution.py:416
  29.9 0.0 collective-permute-done.1.above
  29.9 0.0 collective-permute-done.5.theirs.refs_6_
  29.9 0.8 %source.2 = (f32[3,4,4,8,128]{4,3,2,1,0:T(8,128)S(1)}, f32[3,4,4,8,128]{4,3,2,1,0:T(8,128)S(1)}) custom-call(f32[3,16,4,8,128]{4,3,2,1,0:T(8,128)S(1)} %get-tuple-element.19.vp, f32[3,16,4,8,128]{4,3,2,1,0:T(8,128)S(1)} %get-tuple-element.20.gp, f32[3,1,4,8,128]{4,3,2,1,0:T(8,128)S(1)} %collective-permute-done.below, ...), custom_call_target="tpu_custom_call" | custom-call | flops 1310720 | bytes 2588672 | tf_op jit(solution)/shard_map/source/pallas_call | solution.py:369
  30.7 3.9 %collective-permute-start.11 = (f32[3,4,4,8,128]{4,3,2,1,0:T(8,128)S(1)}, f32[3,4,4,8,128]{4,3,2,1,0:T(8,128)S(1)}, u32[]{:S(2)}, u32[]{:S(2)}) collective-permute-start(f32[3,4,4,8,128]{4,3,2,1,0:T(8,128)S(1)} %get-tuple-element.24.refs_0_), channel_id=1, source_target_pairs={{0,3},{1,0},{2,1},{3,2},{4,5},{5,6},{6,7},{7,4},{8,11},{9,8},{10,9... | collective-permute-start | bytes 589832 | tf_op jit(solution)/shard_map/ppermute | solution.py:448
  34.6 0.0 collective-permute-start.12
  34.6 0.0 collective-permute-done.8.theirs.refs_7_
  34.6 0.8 %source.3 = (f32[3,4,4,8,128]{4,3,2,1,0:T(8,128)S(1)}, f32[3,4,4,8,128]{4,3,2,1,0:T(8,128)S(1)}) custom-call(f32[3,16,4,8,128]{4,3,2,1,0:T(8,128)S(1)} %get-tuple-element.19.vp, f32[3,16,4,8,128]{4,3,2,1,0:T(8,128)S(1)} %get-tuple-element.20.gp, f32[3,1,4,8,128]{4,3,2,1,0:T(8,128)S(1)} %collective-permute-done.below, ...), custom_call_target="tpu_custom_call" | custom-call | flops 1310720 | bytes 2588672 | tf_op jit(solution)/shard_map/source/pallas_call | solution.py:369
  35.4 3.9 %collective-permute-start.13 = (f32[3,4,4,8,128]{4,3,2,1,0:T(8,128)S(1)}, f32[3,4,4,8,128]{4,3,2,1,0:T(8,128)S(1)}, u32[]{:S(2)}, u32[]{:S(2)}) collective-permute-start(f32[3,4,4,8,128]{4,3,2,1,0:T(8,128)S(1)} %get-tuple-element.26.refs_1_), channel_id=1, source_target_pairs={{0,3},{1,0},{2,1},{3,2},{4,5},{5,6},{6,7},{7,4},{8,11},{9,8},{10,9... | collective-permute-start | bytes 589832 | tf_op jit(solution)/shard_map/ppermute | solution.py:448
  39.3 0.0 collective-permute-start.14
  39.3 0.0 collective-permute-done.9.refs_8_
  39.3 0.0 collective-permute-start.10
  39.3 1.3 %collective-permute-done.10.refs_9_ = f32[8,4,8,128]{3,2,1,0:T(8,128)S(1)} collective-permute-done((f32[8,4,8,128]{3,2,1,0:T(8,128)S(1)}, f32[8,4,8,128]{3,2,1,0:T(8,128)S(1)}, u32[]{:S(2)}, u32[]{:S(2)}) %collective-permute-start.10) | collective-permute-done | bytes 131104 | tf_op jit(solution)/shard_map/ppermute | solution.py:452
  40.6 3.6 %collective-permute-done.11.refs_10_ = f32[3,4,4,8,128]{4,3,2,1,0:T(8,128)S(1)} collective-permute-done((f32[3,4,4,8,128]{4,3,2,1,0:T(8,128)S(1)}, f32[3,4,4,8,128]{4,3,2,1,0:T(8,128)S(1)}, u32[]{:S(2)}, u32[]{:S(2)}) %collective-permute-start.11) | collective-permute-done | bytes 196640 | tf_op jit(solution)/shard_map/ppermute | solution.py:448
  44.2 0.5 collective-permute-done.12.refs_11_
  44.7 10.4 %early.1 = (f32[7,32,4,8,128]{4,3,2,1,0:T(8,128)S(1)}, f32[3,32,4,8,128]{4,3,2,1,0:T(8,128)S(1)}, f32[8,2,3,2,4,8,128]{6,5,4,3,2,1,0:T(8,128)S(1)}, f32[3,8,32,128]{3,2,1,0:T(8,128)S(1)}) custom-call(f32[3,4,4,8,128]{4,3,2,1,0:T(8,128)S(1)} %get-tuple-element.24.refs_0_, f32[3,4,4,8,128]{4,3,2,1,0:T(8,128)S(1)} %get-tuple-element.26.refs_1_, ...), custom_call_target="tpu_custom_call" | custom-call | flops 31457280 | bytes 9699328 | tf_op jit(solution)/shard_map/early/pallas_call | solution.py:369
  55.1 0.0 collective-permute-done.13.refs_4_
  55.1 0.0 collective-permute-done.14.refs_5_
  55.1 21.2 %late.1 = f32[1,3,16,32,128]{4,3,2,1,0:T(8,128)} custom-call(f32[7,32,4,8,128]{4,3,2,1,0:T(8,128)S(1)} %get-tuple-element.29.refs_0_, f32[3,32,4,8,128]{4,3,2,1,0:T(8,128)S(1)} %get-tuple-element.30.refs_1_, f32[8,2,3,2,4,8,128]{6,5,4,3,2,1,0:T(8,128)S(1)} %get-tuple-element.31.refs_2_, f32[3,8,32,128]{3,2,1,0:T(8,128)S(1)} %get-tuple-element.32.refs_3_, ...), custom_call_target="tpu_custom_call" | custom-call | flops 15728640 | bytes 8388608 | tf_op jit(solution)/shard_map/late/pallas_call | solution.py:369
  (5 shorter events, 0.1 us)
Async XLA Ops:
  0.0 2.9 %collective-permute-start.2 = (f32[1,3,16,32,128]{4,3,2,1,0:T(8,128)}, f32[1,3,16,32,128]{4,3,2,1,0:T(8,128)S(1)}, u32[]{:S(2)}, u32[]{:S(2)}) collective-permute-start(f32[1,3,16,32,128]{4,3,2,1,0:T(8,128)} %vel.1), channel_id=1, source_target_pairs={{0,4},{4,0},{8,12},{12,8},{16,20},{20,16},{24,28},{28,24},{1,5},{5... | collective-permute-start | bytes 2359304 | tf_op jit(solution)/shard_map/ppermute | solution.py:407
  0.5 1.1 %copy-start = (f32[1,3,16,32,128]{4,3,2,1,0:T(8,128)S(1)}, f32[1,3,16,32,128]{4,3,2,1,0:T(8,128)}, u32[]{:S(2)}) copy-start(f32[1,3,16,32,128]{4,3,2,1,0:T(8,128)} %force.1) | copy-start | bytes 2359300
  1.6 1.1 %copy-start.1 = (f32[1,3,16,32,128]{4,3,2,1,0:T(8,128)S(1)}, f32[1,3,16,32,128]{4,3,2,1,0:T(8,128)}, u32[]{:S(2)}) copy-start(f32[1,3,16,32,128]{4,3,2,1,0:T(8,128)} %vel.1) | copy-start | bytes 2359300
  3.0 6.9 %collective-permute-start.6 = (f32[4,4,4,8,128]{4,3,2,1,0:T(8,128)S(1)}, f32[4,4,4,8,128]{4,3,2,1,0:T(8,128)S(1)}, u32[]{:S(2)}, u32[]{:S(2)}) collective-permute-start(f32[4,4,4,8,128]{4,3,2,1,0:T(8,128)S(1)} %get-tuple-element.25), channel_id=1, source_target_pairs={{0,8},{4,20},{8,0},{12,28},{16,24},{20,4},{24,16},{28,12},{1,9},{5... | collective-permute-start | bytes 786440 | tf_op jit(solution)/shard_map/ppermute | solution.py:429
  5.6 7.3 %collective-permute-start.3 = (f32[4,4,4,8,128]{4,3,2,1,0:T(8,128)S(1)}, f32[4,4,4,8,128]{4,3,2,1,0:T(8,128)S(1)}, u32[]{:S(2)}, u32[]{:S(2)}) collective-permute-start(f32[4,4,4,8,128]{4,3,2,1,0:T(8,128)S(1)} %get-tuple-element.23), channel_id=1, source_target_pairs={{0,8},{4,20},{8,0},{12,28},{16,24},{20,4},{24,16},{28,12},{1,9},{5... | collective-permute-start | bytes 786440 | tf_op jit(solution)/shard_map/ppermute | solution.py:429
  10.0 6.5 %collective-permute-start.7 = (f32[4,4,4,8,128]{4,3,2,1,0:T(8,128)S(1)}, f32[4,4,4,8,128]{4,3,2,1,0:T(8,128)S(1)}, u32[]{:S(2)}, u32[]{:S(2)}) collective-permute-start(f32[4,4,4,8,128]{4,3,2,1,0:T(8,128)S(1)} %add.7.refs_0_), channel_id=1, source_target_pairs={{0,16},{4,12},{8,24},{12,4},{16,0},{20,28},{24,8},{28,20},{1,17},{... | collective-permute-start | bytes 786440 | tf_op jit(solution)/shard_map/ppermute | solution.py:429
  12.9 6.8 %collective-permute-start.4 = (f32[4,4,4,8,128]{4,3,2,1,0:T(8,128)S(1)}, f32[4,4,4,8,128]{4,3,2,1,0:T(8,128)S(1)}, u32[]{:S(2)}, u32[]{:S(2)}) collective-permute-start(f32[4,4,4,8,128]{4,3,2,1,0:T(8,128)S(1)} %add.6.refs_0_), channel_id=1, source_target_pairs={{0,16},{4,12},{8,24},{12,4},{16,0},{20,28},{24,8},{28,20},{1,17},{... | collective-permute-start | bytes 786440 | tf_op jit(solution)/shard_map/ppermute | solution.py:429
  16.5 18.1 %collective-permute-start.8 = (f32[4,4,4,8,128]{4,3,2,1,0:T(8,128)S(1)}, f32[4,4,4,8,128]{4,3,2,1,0:T(8,128)S(1)}, u32[]{:S(2)}, u32[]{:S(2)}) collective-permute-start(f32[4,4,4,8,128]{4,3,2,1,0:T(8,128)S(1)} %stats.3.mine.refs_5_), channel_id=1, source_target_pairs={{0,4},{4,0},{8,12},{12,8},{16,20},{20,16},{24,28},{28,24},{1,5},{5... | collective-permute-start | bytes 786440 | tf_op jit(solution)/shard_map/ppermute | solution.py:438
  19.8 10.2 %collective-permute-start.5 = (f32[4,4,4,8,128]{4,3,2,1,0:T(8,128)S(1)}, f32[4,4,4,8,128]{4,3,2,1,0:T(8,128)S(1)}, u32[]{:S(2)}, u32[]{:S(2)}) collective-permute-start(f32[4,4,4,8,128]{4,3,2,1,0:T(8,128)S(1)} %stats.2.mine.refs_4_), channel_id=1, source_target_pairs={{0,4},{4,0},{8,12},{12,8},{16,20},{20,16},{24,28},{28,24},{1,5},{5... | collective-permute-start | bytes 786440 | tf_op jit(solution)/shard_map/ppermute | solution.py:438
  19.9 19.4 %collective-permute-start.9 = (f32[8,4,8,128]{3,2,1,0:T(8,128)S(1)}, f32[8,4,8,128]{3,2,1,0:T(8,128)S(1)}, u32[]{:S(2)}, u32[]{:S(2)}) collective-permute-start(f32[8,4,8,128]{3,2,1,0:T(8,128)S(1)} %pad_maximum_fusion), channel_id=1, source_target_pairs={{0,3},{1,0},{2,1},{3,2},{4,5},{5,6},{6,7},{7,4},{8,11},{9,8},{10,9... | collective-permute-start | bytes 393224 | tf_op jit(solution)/shard_map/ppermute | solution.py:451
  24.0 5.9 %collective-permute-start = (f32[3,1,4,8,128]{4,3,2,1,0:T(8,128)S(1)}, f32[3,1,4,8,128]{4,3,2,1,0:T(8,128)S(1)}, u32[]{:S(2)}, u32[]{:S(2)}) collective-permute-start(f32[3,1,4,8,128]{4,3,2,1,0:T(8,128)S(1)} %get-tuple-element.21), channel_id=1, source_target_pairs={{0,1},{1,2},{2,3},{3,0},{4,5},{5,6},{6,7},{7,4},{8,9},{9,10},{10,1... | collective-permute-start | bytes 147464 | tf_op jit(solution)/shard_map/ppermute | solution.py:416
  24.0 5.9 %collective-permute-start.1 = (f32[3,1,4,8,128]{4,3,2,1,0:T(8,128)S(1)}, f32[3,1,4,8,128]{4,3,2,1,0:T(8,128)S(1)}, u32[]{:S(2)}, u32[]{:S(2)}) collective-permute-start(f32[3,1,4,8,128]{4,3,2,1,0:T(8,128)S(1)} %get-tuple-element.22), channel_id=1, source_target_pairs={{0,3},{1,0},{2,1},{3,2},{4,7},{5,4},{6,5},{7,6},{8,11},{9,8},{10,9... | collective-permute-start | bytes 147464 | tf_op jit(solution)/shard_map/ppermute | solution.py:415
  30.7 13.5 %collective-permute-start.11 = (f32[3,4,4,8,128]{4,3,2,1,0:T(8,128)S(1)}, f32[3,4,4,8,128]{4,3,2,1,0:T(8,128)S(1)}, u32[]{:S(2)}, u32[]{:S(2)}) collective-permute-start(f32[3,4,4,8,128]{4,3,2,1,0:T(8,128)S(1)} %get-tuple-element.24.refs_0_), channel_id=1, source_target_pairs={{0,3},{1,0},{2,1},{3,2},{4,5},{5,6},{6,7},{7,4},{8,11},{9,8},{10,9... | collective-permute-start | bytes 589832 | tf_op jit(solution)/shard_map/ppermute | solution.py:448
  34.6 10.1 %collective-permute-start.12 = (f32[3,4,4,8,128]{4,3,2,1,0:T(8,128)S(1)}, f32[3,4,4,8,128]{4,3,2,1,0:T(8,128)S(1)}, u32[]{:S(2)}, u32[]{:S(2)}) collective-permute-start(f32[3,4,4,8,128]{4,3,2,1,0:T(8,128)S(1)} %get-tuple-element.27.refs_2_), channel_id=1, source_target_pairs={{0,1},{1,2},{2,3},{3,0},{4,7},{5,4},{6,5},{7,6},{8,9},{9,10},{10,1... | collective-permute-start | bytes 589832 | tf_op jit(solution)/shard_map/ppermute | solution.py:449
  35.4 19.7 %collective-permute-start.13 = (f32[3,4,4,8,128]{4,3,2,1,0:T(8,128)S(1)}, f32[3,4,4,8,128]{4,3,2,1,0:T(8,128)S(1)}, u32[]{:S(2)}, u32[]{:S(2)}) collective-permute-start(f32[3,4,4,8,128]{4,3,2,1,0:T(8,128)S(1)} %get-tuple-element.26.refs_1_), channel_id=1, source_target_pairs={{0,3},{1,0},{2,1},{3,2},{4,5},{5,6},{6,7},{7,4},{8,11},{9,8},{10,9... | collective-permute-start | bytes 589832 | tf_op jit(solution)/shard_map/ppermute | solution.py:448
  39.3 15.8 %collective-permute-start.14 = (f32[3,4,4,8,128]{4,3,2,1,0:T(8,128)S(1)}, f32[3,4,4,8,128]{4,3,2,1,0:T(8,128)S(1)}, u32[]{:S(2)}, u32[]{:S(2)}) collective-permute-start(f32[3,4,4,8,128]{4,3,2,1,0:T(8,128)S(1)} %get-tuple-element.28.refs_3_), channel_id=1, source_target_pairs={{0,1},{1,2},{2,3},{3,0},{4,7},{5,4},{6,5},{7,6},{8,9},{9,10},{10,1... | collective-permute-start | bytes 589832 | tf_op jit(solution)/shard_map/ppermute | solution.py:449
  39.3 1.3 %collective-permute-start.10 = (f32[8,4,8,128]{3,2,1,0:T(8,128)S(1)}, f32[8,4,8,128]{3,2,1,0:T(8,128)S(1)}, u32[]{:S(2)}, u32[]{:S(2)}) collective-permute-start(f32[8,4,8,128]{3,2,1,0:T(8,128)S(1)} %collective-permute-done.9.refs_8_), channel_id=1, source_target_pairs={{0,4},{4,0},{8,12},{12,8},{16,20},{20,16},{24,28},{28,24},{1,5},{5... | collective-permute-start | bytes 393224 | tf_op jit(solution)/shard_map/ppermute | solution.py:452

commit v2 on v0

v2 whole, which is shorter than its diff:
```python
import functools
import math

import jax
import jax.numpy as jnp
from jax import lax
from jax.experimental import pallas as pl
from jax.experimental.pallas import tpu as pltpu
from jax.sharding import PartitionSpec as P

SWEEPS = 8


TIME_STEP = 0.25
EDDY_COEFF = 1.0
BASE_VISCOSITY = 1.0
LOWER_EDGE = 0.1
UPPER_EDGE = 1.9

ROWS = 8
PIECES = ((0, 4), (4, 8))
STAGES = ((0, 4), (4, 8))
OWN = True
GATE = True
PAD = 1
TIE = False
SINGLE = False
FAKE = 11
WEIGHT = {}
VMEM_LIMIT = 40 * 1024 * 1024


def step_sizes(sweep_count):
    middle = (UPPER_EDGE + LOWER_EDGE) / 2
    radius = (UPPER_EDGE - LOWER_EDGE) / 2
    return [
        1.0 / (middle + radius * math.cos(math.pi * (2 * position + 1) / (2 * sweep_count)))
        for position in range(sweep_count)
    ]


def north(planes, j):
    return planes[j + 1] if j + 1 < len(planes) else pltpu.roll(planes[0], ROWS - 1, 0)


def south(planes, j):
    return planes[j - 1] if j else pltpu.roll(planes[-1], 1, 0)


def upper(plane):
    return pltpu.roll(plane, plane.shape[-1] - 1, 1)


def lower(plane):
    return pltpu.roll(plane, 1, 1)


def rows_of(j, count):
    return pl.ds(j, ROWS, stride=count)


def parity():
    return lax.rem(lax.axis_index("member"), 2)


def for_layers(count, body, unroll=1):
    def step(i, carry):
        body(i)
        return carry

    lax.fori_loop(0, count, step, 0, unroll=unroll)


def arrange_kernel(vel, force, vp, gp, first, last):
    comps, nx, planes = vp.shape[:3]

    def body(x):
        for c in range(comps):
            for j in range(planes):
                value = vel[0, c, x, rows_of(j, planes), :]
                vp[c, x, j] = value
                gp[c, x, j] = value + TIME_STEP * force[0, c, x, rows_of(j, planes), :]

    for_layers(nx, body, 2)
    first[...] = vp[:, :1]
    last[...] = vp[:, nx - 1 :]


def sums_kernel(pieces, vp, other, *refs):
    outs = refs[len(refs) - len(pieces) :]
    comps, nx, planes = vp.shape[:3]
    side = parity()
    for (near, far), out in zip(pieces, outs):
        start = jnp.where(side == 0, near, nx - far)

        def body(i, out=out, start=start):
            x = start + i
            for j in range(planes):
                squares = None
                for c in range(comps):
                    a = vp[c, x, j]
                    b = other[0, c, x, rows_of(j, planes), :]
                    out[c, i, j] = a + b
                    both = a * a + b * b
                    squares = both if squares is None else squares + both
                out[comps, i, j] = squares

        for_layers(far - near, body)


def add_kernel(*refs):
    refs[-1][...] = refs[0][...] + refs[1][...]


def gate_kernel(*refs):
    count = refs[0].shape[0]
    refs[-1][:count] = refs[0][...]


def stats_kernel(members, add_two, *refs):
    flow, rest = refs[-2:]
    comps, layers, planes = refs[0].shape[0] - 1, refs[0].shape[1], refs[0].shape[2]

    def body(i):
        for j in range(planes):
            def total(c):
                value = refs[0][c, i, j]
                return value + refs[1][c, i, j] if add_two else value

            spread = total(comps) * (1.0 / members)
            for c in range(comps):
                mean = total(c) * (1.0 / members)
                if c < comps - 1:
                    flow[c, i, j] = mean
                else:
                    rest[0, i, j] = mean
                spread = spread - mean * mean
            rest[1, i, j] = BASE_VISCOSITY + EDDY_COEFF * TIME_STEP * spread

    for_layers(layers, body)


def source_kernel(piece, vp, gp, below, above, mine, mine_rest, theirs, theirs_rest, *refs):
    out_mine, out_theirs = refs[-2:]
    comps, nx, planes = vp.shape[:3]
    near, far = piece
    side = parity()
    for which, stats, rest, out in (
        (side, mine, mine_rest, out_mine),
        (1 - side, theirs, theirs_rest, out_theirs),
    ):
        start = jnp.where(which == 0, near, nx - far)

        def body(i, stats=stats, rest=rest, out=out, start=start):
            x = start + i
            down, up = jnp.maximum(x - 1, 0), jnp.minimum(x + 1, nx - 1)
            for c in range(comps):
                here = [vp[c, x, j] for j in range(planes)]
                for j in range(planes):
                    west = jnp.where(x == 0, below[c, 0, j], vp[c, down, j])
                    east = jnp.where(x == nx - 1, above[c, 0, j], vp[c, up, j])
                    transport = (
                        stats[0, i, j] * (east - west)
                        + stats[1, i, j] * (north(here, j) - south(here, j))
                        + rest[0, i, j] * (upper(here[j]) - lower(here[j]))
                    )
                    out[c, i, j] = gp[c, x, j] - (0.5 * TIME_STEP) * transport

        for_layers(far - near, body, far - near)


def relaxed(center, outward, inward, coef, source, comps, planes, step_size):
    here = [[center(c, j) for j in range(planes)] for c in range(comps)]
    values = []
    for j in range(planes):
        faces = [coef(a, j) for a in range(6)]
        for c in range(comps):
            ns, ss = north(here[c], j), south(here[c], j)
            image = source(c, j) + faces[0] * inward(c, j)
            image = image + faces[1] * outward(c, j)
            image = image + (faces[2] * ns + faces[3] * ss)
            image = image + (faces[4] * upper(here[c][j]) + faces[5] * lower(here[c][j]))
            values.append((c, j, (1.0 - step_size) * here[c][j] + step_size * image))
    return values


class Taker:
    def __init__(self, refs):
        self.refs, self.at = refs, 0

    def __call__(self, n=1):
        self.at += n
        return list(self.refs[self.at - n : self.at])


def make_coefs(visc_here, visc_in, visc_out, put, planes):
    half = 0.5 * TIME_STEP
    for j in range(planes):
        here = visc_here[j]
        faces = [
            here + visc_in[j],
            here + visc_out[j],
            here + north(visc_here, j),
            here + south(visc_here, j),
            here + upper(here),
            here + lower(here),
        ]
        total = (faces[0] + faces[1]) + (faces[2] + faces[3]) + (faces[4] + faces[5])
        inverse = 1.0 / (1.0 + half * total)
        scale = half * inverse
        for a in range(6):
            put(a, j, faces[a] * scale)
        put(6, j, inverse)


def run_sweeps(reach, before, sizes, comps, planes, load, coef, source, keep, last):
    depth = len(sizes)
    for k in range(1, depth + 1):
        layers = range(k + depth - reach, min(k + depth - before, 2 * depth))
        for s in range(2):
            found = []
            for i in layers:
                found.append(
                    relaxed(
                        lambda c, j: load(k - 1, s, c, i, j),
                        lambda c, j: load(k - 1, s, c, i - 1, j),
                        lambda c, j: load(k - 1, s, c, i + 1, j),
                        lambda a, j: coef(s, a, i, j),
                        lambda c, j: source(s, c, i, j),
                        comps,
                        planes,
                        sizes[k - 1],
                    )
                )
            for i, values in zip(layers, found):
                for c, j, value in values:
                    if k < depth:
                        keep(k, s, c, i, j, value)
                    else:
                        last(s, c, i, j, value)


def own_kernel(pieces, sizes, count, *refs):
    number = len(pieces)
    take = Taker(refs)
    src_mine, src_theirs = take(number), take(number)
    stat_mine, stat_theirs = take(number), take(number)
    coef, scaled, edges, visc = take(4)
    (field,) = take(1)
    depth = len(sizes)
    comps, planes = scaled.shape[1], scaled.shape[3]
    side = parity()
    for which, stats, srcs in ((side, stat_mine, src_mine), (1 - side, stat_theirs, src_theirs)):
        for (near, far), stat, src in zip(pieces, stats, srcs):
            for e in range(far - near):
                d = jnp.where(which == 0, near + e, far - 1 - e)
                visc[which, d] = stat[1, e]
                for c in range(comps):
                    field[0, which, c, d] = src[c, e]
    for s in range(2):
        for d in range(1, depth):
            def put(a, j, value):
                coef[s, a, d, j] = value

            make_coefs(
                [visc[s, d, j] for j in range(planes)],
                [visc[s, d + 1, j] if d + 1 < depth else visc[1 - s, d, j] for j in range(planes)],
                [visc[s, d - 1, j] for j in range(planes)],
                put,
                planes,
            )
            for c in range(comps):
                for j in range(planes):
                    scaled[s, c, d, j] = field[0, s, c, d, j] * coef[s, 6, d, j]

    def load(k, s, c, i, j):
        return field[k, s, c, i - depth, j] if i < 2 * depth else field[k, 1 - s, c, depth - 1, j]

    def keep(k, s, c, i, j, value):
        field[k, s, c, i - depth, j] = value

    triangle(sizes, comps, planes, load, coef, scaled, keep)
    for k in range(depth):
        for s in range(2):
            for c in range(comps):
                edges[k, s, c, 0] = field[k, s, c, k]
                edges[k, s, c, 1] = (
                    field[k, s, c, k + 1] if k + 1 < depth else field[k, 1 - s, c, depth - 1]
                )


def triangle(sizes, comps, planes, load, coef, scaled, keep):
    depth = len(sizes)
    for k in range(1, depth):
        for s in range(2):
            layers = range(k + depth, 2 * depth)
            found = [
                relaxed(
                    lambda c, j: load(k - 1, s, c, i, j),
                    lambda c, j: load(k - 1, s, c, i - 1, j),
                    lambda c, j: load(k - 1, s, c, i + 1, j),
                    lambda a, j: coef[s, a, i - depth, j],
                    lambda c, j: scaled[s, c, i - depth, j],
                    comps,
                    planes,
                    sizes[k - 1],
                )
                for i in layers
            ]
            for i, values in zip(layers, found):
                for c, j, value in values:
                    keep(k, s, c, i, j, value)


def stage_kernel(pieces, piece, first, final, sizes, count, olds, *refs):
    take = Taker(refs)
    depth = len(sizes)
    near, far = piece
    width = far - near
    (coef_own,) = take()
    if first:
        visc_own, visc_got, visc_other = take(3)
    else:
        (coef_halo,) = take()
    scaled_own = take()[0]
    scaled_old = take(len(olds))
    edges_in, halo_mine, halo_theirs = take(3)
    if final:
        parts = take(len(olds))
        (out,) = take()
    else:
        scaled_new, edges, part = take(3)
        if first:
            (coef_halo,) = take()
    (field,) = take()
    if first:
        (visc,) = take()
    if final:
        scaled_new, tail, sems = take(3)
    comps, planes = scaled_own.shape[1], scaled_own.shape[3]
    side = parity()

    copies = []
    if final:
        for n, ((lo, hi), done) in enumerate(zip(olds, parts)):
            for s in range(2):
                where = depth - hi if s == 0 else count - depth + lo
                copies.append(
                    pltpu.make_async_copy(
                        done.at[s], out.at[0, :, where : where + hi - lo], sems.at[2 * n + s]
                    )
                )
                copies[-1].start()

    for which, halo in ((side, halo_mine), (1 - side, halo_theirs)):
        for e in range(width):
            spot = jnp.where(which == 0, width - 1 - e, e)
            for c in range(comps):
                field[0, 1 - which, c, spot] = halo[c, e]
    for k in range(depth):
        for s in range(2):
            for c in range(comps):
                for e in range(2):
                    field[k, s, c, width + e] = edges_in[k, s, c, e]

    if first:
        for which, got in ((side, visc_got), (1 - side, visc_other)):
            for lo, hi in pieces:
                for e in range(hi - lo):
                    i = jnp.where(which == 0, depth - 1 - lo - e, depth - hi + e)
                    visc[1 - which, i] = got[lo + e]
        for s in range(2):
            for d in range(2):
                visc[s, depth + d] = visc_own[s, d]
        for s in range(2):
            for i in range(1, depth + 1):
                def put(a, j, value):
                    coef_halo[s, a, i, j] = value

                make_coefs(
                    [visc[s, i, j] for j in range(planes)],
                    [visc[s, i + 1, j] for j in range(planes)],
                    [visc[s, i - 1, j] for j in range(planes)],
                    put,
                    planes,
                )

    def coef(s, a, i, j):
        return coef_halo[s, a, i, j] if i <= depth else coef_own[s, a, i - depth, j]

    base = depth - far
    for s in range(2):
        for p in range(width):
            i = base + p
            if i > 0:
                for c in range(comps):
                    for j in range(planes):
                        scaled_new[s, c, p, j] = field[0, s, c, p, j] * coef_halo[s, 6, i, j]
        if first:
            for c in range(comps):
                for j in range(planes):
                    scaled_new[s, c, width, j] = edges_in[0, s, c, 0, j] * coef_halo[s, 6, depth, j]

    def source(s, c, i, j):
        if i > depth:
            return scaled_own[s, c, i - depth, j]
        if first:
            return scaled_new[s, c, i - base, j]
        if i == depth:
            lo, hi = olds[0]
            return scaled_old[0][s, c, hi - lo, j]
        d = depth - 1 - i
        if near <= d < far:
            return scaled_new[s, c, i - base, j]
        for (lo, hi), ref in zip(olds, scaled_old):
            if lo <= d < hi:
                return ref[s, c, i - (depth - hi), j]
        raise ValueError("no source")

    def load(k, s, c, i, j):
        return field[k, s, c, i - (k + depth - far), j]

    def keep(k, s, c, i, j, value):
        field[k, s, c, i - (k + depth - far), j] = value

    def last(s, c, i, j, value):
        p = i - (2 * depth - far)
        place = p if s == 0 else width - 1 - p
        target = tail if final else part
        target[s, c, place, rows_of(j, planes), :] = value

    run_sweeps(far, near, sizes, comps, planes, load, coef, source, keep, last)

    if final:
        for s in range(2):
            where = depth - far if s == 0 else count - depth + near
            copies.append(
                pltpu.make_async_copy(
                    tail.at[s], out.at[0, :, where : where + width], sems.at[2 * len(olds) + s]
                )
            )
            copies[-1].start()
        for copy in copies:
            copy.wait()
    else:
        for k in range(depth):
            for s in range(2):
                for c in range(comps):
                    for e in range(2):
                        edges[k, s, c, e] = field[k, s, c, e]


def vmem(n):
    return [pl.BlockSpec(memory_space=pltpu.VMEM)] * n


def call(kernel, outs, ins, flops, scratch=(), any_out=False, name=None):
    shapes = [jax.ShapeDtypeStruct(shape, jnp.float32) for shape in outs]
    size = int(3.7e6 * WEIGHT[name]) if name in WEIGHT else 4 * sum(math.prod(shape) for shape in outs) + 4 * sum(x.size for x in ins)
    flops = 0 if name in WEIGHT else flops
    result = pl.pallas_call(
        kernel,
        out_shape=shapes,
        in_specs=vmem(len(ins)),
        out_specs=[pl.BlockSpec(memory_space=pl.ANY)] * len(outs) if any_out else vmem(len(outs)),
        scratch_shapes=list(scratch),
        compiler_params=pltpu.CompilerParams(vmem_limit_bytes=VMEM_LIMIT),
        cost_estimate=pl.CostEstimate(flops=flops, bytes_accessed=size, transcendentals=0),
        name=name,
    )(*ins)
    return result


def fast(velocity, forcing):
    members = lax.axis_size("member")
    subs = lax.axis_size("sub")
    _, comps, nx, ny, nz = velocity.shape
    planes = ny // ROWS
    layer = (planes, ROWS, nz)
    sizes = step_sizes(SWEEPS)
    depth = SWEEPS
    bits = members.bit_length() - 1
    f32 = jnp.float32

    swap = [(m, m ^ 1) for m in range(members)]

    def pair(step):
        order = [list(range(1, bits)), list(range(2, bits)) + [1]]
        return [(m, m ^ (1 << order[m % 2][step])) for m in range(members)]

    def along(mine):
        moves = []
        for m in range(members):
            step = -1 if (m % 2 == 0) == mine else 1
            for s in range(subs):
                moves.append((m * subs + s, m * subs + (s + step) % subs))
        return moves

    other = lax.ppermute(velocity, "member", swap)
    vp, gp, first, last = call(
        arrange_kernel,
        [(comps, nx, *layer)] * 2 + [(comps, 1, *layer)] * 2,
        [velocity, forcing],
        10 * velocity.size,
        name="arrange",
    )
    above = lax.ppermute(first, "sub", [(s, (s - 1) % subs) for s in range(subs)])
    below = lax.ppermute(last, "sub", [(s, (s + 1) % subs) for s in range(subs)])
    hold = []
    if FAKE:
        hold = call(gate_kernel, [(FAKE, 1, *layer)], [below, above], 1, name="gate")
        hold = [lax.ppermute(hold[0], "member", swap)]
    parts = list(call(
        functools.partial(sums_kernel, PIECES),
        [(comps + 1, far - near, *layer) for near, far in PIECES],
        [vp, other],
        6 * velocity.size,
        name="sums",
    ))
    got = [None] * len(parts)
    for step in range(bits - 1):
        for i, part in enumerate(parts):
            if step:
                tie = [parts[i - 1]] if i else []
                if i and step == 1:
                    tie += hold or [below, above]
                parts[i] = part = call(
                    add_kernel, [part.shape], [part, got[i]] + tie, part.size, name="add%d" % i
                )[0]
            got[i] = lax.ppermute(part, "member", pair(step))
    stats_mine, stats_theirs, src_mine, src_theirs, halo_mine, halo_theirs = [], [], [], [], [], []
    tie = parts[1:]
    for i, ((near, far), part, last_got) in enumerate(zip(PIECES, parts, got)):
        terms = [part] if last_got is None else [part, last_got]
        stats = call(
            functools.partial(stats_kernel, members, len(terms) == 2),
            [(comps - 1, far - near, *layer), (2, far - near, *layer)],
            terms + tie,
            10 * part.size,
            name="stats%d" % i,
        )
        swapped = [lax.ppermute(x, "member", swap) for x in stats]
        if SINGLE:
            swapped = [jnp.concatenate([lax.ppermute(x[:1], "member", swap), lax.ppermute(x[1:], "member", swap)]) for x in stats]
        stats_mine.append(stats[1])
        stats_theirs.append(swapped[1])
        mine, theirs = call(
            functools.partial(source_kernel, (near, far)),
            [(comps, far - near, *layer)] * 2,
            [vp, gp, below, above, *stats, *swapped],
            20 * part.size,
            name="source%d" % i,
        )
        mines, theirses = [mine], [theirs]
        src_mine.append(mine)
        src_theirs.append(theirs)
        for mine_part, theirs_part in zip(mines, theirses):
            halo_mine.append(lax.ppermute(mine_part, ("member", "sub"), along(True)))
            halo_theirs.append(lax.ppermute(theirs_part, ("member", "sub"), along(False)))
        tie = [mine]
    visc = jnp.concatenate([rest[1] for rest in stats_mine], 0)
    visc_got = lax.ppermute(visc, ("member", "sub"), along(True))
    own = call(
        functools.partial(own_kernel, PIECES, sizes, nx),
        [(2, 7, depth, *layer), (2, comps, depth, *layer), (depth, 2, comps, 2, *layer), (2, depth, *layer)],
        src_mine + src_theirs + stats_mine + stats_theirs,
        20 * 3 * velocity.size,
        scratch=[pltpu.VMEM((depth, 2, comps, depth, *layer), f32)],
        name="own",
    )
    coef_own, scaled_own, edges, visc_own = own
    if GATE:
        tie = [src_mine[-1]] if TIE else []
        visc_got = call(
            gate_kernel,
            [(PAD + depth, *layer)],
            [visc_got, halo_mine[0], halo_theirs[0]] + tie + ([edges] if OWN else []),
            1,
            name="gate",
        )[0]
    visc_other = lax.ppermute(visc_got, "member", swap)
    olds, scaled_old, parts = [], [], []
    for n, (piece, mine, theirs) in enumerate(zip(STAGES, halo_mine, halo_theirs)):
        first, final = n == 0, n == len(STAGES) - 1
        width = piece[1] - piece[0]
        ins = [coef_own]
        ins += [visc_own, visc_got, visc_other] if first else [coef_halo]
        ins += [scaled_own] + scaled_old + [edges, mine, theirs]
        scratch = [pltpu.VMEM((depth, 2, comps, width + 2, *layer), f32)]
        if first:
            scratch.append(pltpu.VMEM((2, depth + 2, *layer), f32))
        if final:
            ins += parts
            outs = [velocity.shape]
            scratch += [
                pltpu.VMEM((2, comps, width, *layer), f32),
                pltpu.VMEM((2, comps, width, ny, nz), f32),
                pltpu.SemaphoreType.DMA((2 * len(STAGES),)),
            ]
        else:
            outs = [
                (2, comps, width + 1, *layer),
                (depth, 2, comps, 2, *layer),
                (2, comps, width, ny, nz),
            ]
            if first:
                outs.append((2, 7, depth + 1, *layer))
        results = call(
            functools.partial(stage_kernel, PIECES, piece, first, final, sizes, nx, list(olds)),
            outs,
            ins,
            20 * width * velocity.size,
            scratch=scratch,
            any_out=final,
            name="stage%d" % n,
        )
        if final:
            return results[0]
        if first:
            coef_halo = results[3]
        olds.append(piece)
        scaled_old.append(results[0])
        edges = results[1]
        parts.append(results[2])


def solution(mesh):
    in_specs = (P("member", None, "sub", None, None), P("member", None, "sub", None, None))
    out_specs = P("member", None, "sub", None, None)
    return jax.shard_map(fast, mesh=mesh, in_specs=in_specs, out_specs=out_specs, check_vma=False)
```

time: 155 us -> 46.2 us (0.30)
  waiting for transfers between devices: 88.4 us -> 14.4 us
  other arithmetic: 13.8 us -> 0.01 us
  between operations: 13.8 us -> 0.14 us
  local copies, waits for them, and re-layouts: 13 us -> 2.28 us
  Pallas kernels: 0 us -> 7.45 us
  starting transfers between devices: 25.6 us -> 21.7 us
    psum x1 -> x0, waiting for transfers between devices: 54.4 us -> none  [per_device(): total, squares = lax.psum((flow, jnp.sum(flow * flow, 0)), 'member')]
    ppermute x20 -> x18, waiting for transfers between devices: 34 us -> 14.4 us  [the longest x2 3.61 us: fast(): lax.ppermute(theirs_part, ('member', 'sub'), along(False))]
    slice x50 -> x0, local copies, waits for them, and re-layouts: 10.3 us -> none  [the longest x14 4.09 us: sweep(): jnp.roll(center, 1, 3)]
    add x10 -> x0, other arithmetic: 8.54 us -> none  [the longest x7 7.2 us: sweep(): return center + step_size * (source - image) / diagonal]
    pallas_call x0 -> x13, Pallas kernels: none -> 7.45 us  [call(): pl.pallas_call(kernel, out_shape=shapes, in_specs=vmem(len(ins)), out_spe...]
    ppermute x20 -> x18, starting transfers between devices: 25.6 us -> 21.7 us  [the longest x4 6.36 us: fast(): got[i] = lax.ppermute(part, 'member', pair(step))]
    reduce_sum x2 -> x0, other arithmetic: 3.27 us -> none  [the longest x1 1.94 us: per_device(): total, squares = lax.psum((flow, jnp.sum(flow * flow, 0)), 'member')]
    broadcast_in_dim x1 -> x0, other arithmetic: 1.92 us -> none  [per_device(): return field[None]]
  transfers between devices with their start and end apart: 21 -> 18, of which waited for: 17 -> 10; matrix products, arithmetic and copies ran while one was open for 5% -> 0% of each run, Pallas kernels for 0% -> 10%
where the time goes in v2:
time: 46.2 us; the launch traced here: 46 us
  starting transfers between devices  21.7 us (47%)
  waiting for transfers between devices  14.4 us (31%)
  Pallas kernels  7.45 us (16%)
  local copies, waits for them, and re-layouts  2.28 us (5%)
    pallas_call x13, Pallas kernels, call(): pl.pallas_call(kernel, out_shape=shapes, in_specs=vmem(len(ins)), out_spe...  7.45 us
    ppermute x4, starting transfers between devices, fast(): got[i] = lax.ppermute(part, 'member', pair(step))  6.36 us
    ppermute x2, starting transfers between devices, fast(): halo_mine.append(lax.ppermute(mine_part, ('member', 'sub'), along(True)))  5.48 us
    ppermute x2, waiting for transfers between devices, fast(): lax.ppermute(theirs_part, ('member', 'sub'), along(False))  3.61 us
    ppermute x1, waiting for transfers between devices, fast(): visc_got = lax.ppermute(visc, ('member', 'sub'), along(True))  3.26 us
    ppermute x1, starting transfers between devices, fast(): visc_got = lax.ppermute(visc, ('member', 'sub'), along(True))  2.48 us
    unnamed x4, local copies, waits for them, and re-layouts  2.27 us
    ppermute x2, waiting for transfers between devices, fast(): halo_mine.append(lax.ppermute(mine_part, ('member', 'sub'), along(True)))  2.22 us
  transfers between devices with their start and end apart: 18, of which 10 were waited for; matrix products, arithmetic and copies ran while one was open for 0% of the time, Pallas kernels for 10%

profile of v2, /device:TPU:0, one launch (start us, length us, event | category | flops | bytes accessed | tf_op | source)
XLA Modules:
  0.0 46.0 jit_solution(9810774801788988763)
XLA Ops:
  0.0 0.5 collective-permute-start.2
  0.5 0.0 copy-start
  0.5 1.1 %copy-done = f32[1,3,16,32,128]{4,3,2,1,0:T(8,128)S(1)} copy-done((f32[1,3,16,32,128]{4,3,2,1,0:T(8,128)S(1)}, f32[1,3,16,32,128]{4,3,2,1,0:T(8,128)}, u32[]{:S(2)}) %copy-start) | copy-done | bytes 786456
  1.6 1.1 %copy-done.1 = f32[1,3,16,32,128]{4,3,2,1,0:T(8,128)S(1)} copy-done((f32[1,3,16,32,128]{4,3,2,1,0:T(8,128)S(1)}, f32[1,3,16,32,128]{4,3,2,1,0:T(8,128)}, u32[]{:S(2)}) %copy-start.1) | copy-done | bytes 786456
  2.7 0.2 arrange.1
  2.9 0.0 collective-permute-done.2.other
  2.9 0.1 sums.1
  3.0 2.6 %collective-permute-start.3 = (f32[4,4,4,8,128]{4,3,2,1,0:T(8,128)S(1)}, f32[4,4,4,8,128]{4,3,2,1,0:T(8,128)S(1)}, u32[]{:S(2)}, u32[]{:S(2)}) collective-permute-start(f32[4,4,4,8,128]{4,3,2,1,0:T(8,128)S(1)} %get-tuple-element.31.refs_0_), channel_id=1, source_target_pairs={{0,8},{4,20},{8,0},{12,28},{16,24},{20,4},{24,16},{28,12},{1,9},{5... | collective-permute-start | bytes 786440 | tf_op jit(solution)/shard_map/ppermute | solution.py:530
  5.6 0.1 collective-permute-start.5
  5.7 2.0 %collective-permute-start = (f32[3,1,4,8,128]{4,3,2,1,0:T(8,128)S(1)}, f32[3,1,4,8,128]{4,3,2,1,0:T(8,128)S(1)}, u32[]{:S(2)}, u32[]{:S(2)}) collective-permute-start(f32[3,1,4,8,128]{4,3,2,1,0:T(8,128)S(1)} %get-tuple-element.29), channel_id=1, source_target_pairs={{0,1},{1,2},{2,3},{3,0},{4,5},{5,6},{6,7},{7,4},{8,9},{9,10},{10,1... | collective-permute-start | bytes 147464 | tf_op jit(solution)/shard_map/ppermute | solution.py:508
  7.7 2.0 %collective-permute-start.1 = (f32[3,1,4,8,128]{4,3,2,1,0:T(8,128)S(1)}, f32[3,1,4,8,128]{4,3,2,1,0:T(8,128)S(1)}, u32[]{:S(2)}, u32[]{:S(2)}) collective-permute-start(f32[3,1,4,8,128]{4,3,2,1,0:T(8,128)S(1)} %get-tuple-element.30), channel_id=1, source_target_pairs={{0,3},{1,0},{2,1},{3,2},{4,7},{5,4},{6,5},{7,6},{8,11},{9,8},{10,9... | collective-permute-start | bytes 147464 | tf_op jit(solution)/shard_map/ppermute | solution.py:507
  9.8 0.2 collective-permute-done.3.refs_1_
  10.0 2.1 %collective-permute-start.4 = (f32[4,4,4,8,128]{4,3,2,1,0:T(8,128)S(1)}, f32[4,4,4,8,128]{4,3,2,1,0:T(8,128)S(1)}, u32[]{:S(2)}, u32[]{:S(2)}) collective-permute-start(f32[4,4,4,8,128]{4,3,2,1,0:T(8,128)S(1)} %add0.1.refs_2_.refs_0_), channel_id=1, source_target_pairs={{0,16},{4,12},{8,24},{12,4},{16,0},{20,28},{24,8},{28,20},{1,17},{... | collective-permute-start | bytes 786440 | tf_op jit(solution)/shard_map/ppermute | solution.py:530
  12.1 0.0 collective-permute-done.refs_0_.below
  12.1 0.2 collective-permute-done.1.refs_1_.above
  12.3 0.0 collective-permute-start.6
  12.4 1.4 %collective-permute-done.6.refs_3_ = f32[11,1,4,8,128]{4,3,2,1,0:T(8,128)S(1)} collective-permute-done((f32[11,1,4,8,128]{4,3,2,1,0:T(8,128)S(1)}, f32[11,1,4,8,128]{4,3,2,1,0:T(8,128)S(1)}, u32[]{:S(2)}, u32[]{:S(2)}) %collective-permute-start.6) | collective-permute-done | bytes 180256 | tf_op jit(solution)/shard_map/ppermute | solution.py:512
  13.8 0.0 collective-permute-done.5.refs_1_
  13.8 1.6 %collective-permute-start.9 = (f32[4,4,4,8,128]{4,3,2,1,0:T(8,128)S(1)}, f32[4,4,4,8,128]{4,3,2,1,0:T(8,128)S(1)}, u32[]{:S(2)}, u32[]{:S(2)}) collective-permute-start(f32[4,4,4,8,128]{4,3,2,1,0:T(8,128)S(1)} %add1.1.refs_2_.refs_0_), channel_id=1, source_target_pairs={{0,16},{4,12},{8,24},{12,4},{16,0},{20,28},{24,8},{28,20},{1,17},{... | collective-permute-start | bytes 786440 | tf_op jit(solution)/shard_map/ppermute | solution.py:530
  15.4 1.1 %collective-permute-done.4.refs_1_ = f32[4,4,4,8,128]{4,3,2,1,0:T(8,128)S(1)} collective-permute-done((f32[4,4,4,8,128]{4,3,2,1,0:T(8,128)S(1)}, f32[4,4,4,8,128]{4,3,2,1,0:T(8,128)S(1)}, u32[]{:S(2)}, u32[]{:S(2)}) %collective-permute-start.4) | collective-permute-done | bytes 262176 | tf_op jit(solution)/shard_map/ppermute | solution.py:530
  16.5 0.1 stats0.1
  16.5 0.1 collective-permute-start.7
  16.6 0.5 %collective-permute-start.8 = (f32[2,4,4,8,128]{4,3,2,1,0:T(8,128)S(1)}, f32[2,4,4,8,128]{4,3,2,1,0:T(8,128)S(1)}, u32[]{:S(2)}, u32[]{:S(2)}) collective-permute-start(f32[2,4,4,8,128]{4,3,2,1,0:T(8,128)S(1)} %get-tuple-element.34.mine_rest.refs_4_), channel_id=1, source_target_pairs={{0,4},{4,0},{8,12},{12,8},{16,20},{20,16},{24,28},{28,24},{1,5},{5... | collective-permute-start | bytes 393224 | tf_op jit(solution)/shard_map/ppermute | solution.py:542
  17.1 0.8 %collective-permute-done.7.theirs = f32[2,4,4,8,128]{4,3,2,1,0:T(8,128)S(1)} collective-permute-done((f32[2,4,4,8,128]{4,3,2,1,0:T(8,128)S(1)}, f32[2,4,4,8,128]{4,3,2,1,0:T(8,128)S(1)}, u32[]{:S(2)}, u32[]{:S(2)}) %collective-permute-start.7) | collective-permute-done | bytes 131104 | tf_op jit(solution)/shard_map/ppermute | solution.py:542
  17.9 0.2 collective-permute-done.8.theirs_rest.refs_6_
  18.1 0.3 source0.1
  18.4 4.2 %collective-permute-start.13 = (f32[3,4,4,8,128]{4,3,2,1,0:T(8,128)S(1)}, f32[3,4,4,8,128]{4,3,2,1,0:T(8,128)S(1)}, u32[]{:S(2)}, u32[]{:S(2)}) collective-permute-start(f32[3,4,4,8,128]{4,3,2,1,0:T(8,128)S(1)} %get-tuple-element.35.refs_2_.refs_0_), channel_id=1, source_target_pairs={{0,3},{1,0},{2,1},{3,2},{4,5},{5,6},{6,7},{7,4},{8,11},{9,8},{10,9... | collective-permute-start | bytes 589832 | tf_op jit(solution)/shard_map/ppermute | solution.py:558
  22.6 0.0 collective-permute-done.9.refs_1_
  22.6 0.1 stats1.1
  22.7 0.1 collective-permute-start.11
  22.7 0.1 collective-permute-start.14
  22.8 1.4 %collective-permute-start.10 = (f32[2,4,4,8,128]{4,3,2,1,0:T(8,128)S(1)}, f32[2,4,4,8,128]{4,3,2,1,0:T(8,128)S(1)}, u32[]{:S(2)}, u32[]{:S(2)}) collective-permute-start(f32[2,4,4,8,128]{4,3,2,1,0:T(8,128)S(1)} %get-tuple-element.36.mine), channel_id=1, source_target_pairs={{0,4},{4,0},{8,12},{12,8},{16,20},{20,16},{24,28},{28,24},{1,5},{5... | collective-permute-start | bytes 393224 | tf_op jit(solution)/shard_map/ppermute | solution.py:542
  24.2 2.5 %collective-permute-start.12 = (f32[8,4,8,128]{3,2,1,0:T(8,128)S(1)}, f32[8,4,8,128]{3,2,1,0:T(8,128)S(1)}, u32[]{:S(2)}, u32[]{:S(2)}) collective-permute-start(f32[8,4,8,128]{3,2,1,0:T(8,128)S(1)} %pad_maximum_fusion), channel_id=1, source_target_pairs={{0,3},{1,0},{2,1},{3,2},{4,5},{5,6},{6,7},{7,4},{8,11},{9,8},{10,9... | collective-permute-start | bytes 393224 | tf_op jit(solution)/shard_map/ppermute | solution.py:562
  26.7 0.0 collective-permute-done.10.theirs
  26.7 0.0 collective-permute-done.11.theirs_rest.refs_7_
  26.7 0.3 source1.1
  27.0 1.3 %collective-permute-start.16 = (f32[3,4,4,8,128]{4,3,2,1,0:T(8,128)S(1)}, f32[3,4,4,8,128]{4,3,2,1,0:T(8,128)S(1)}, u32[]{:S(2)}, u32[]{:S(2)}) collective-permute-start(f32[3,4,4,8,128]{4,3,2,1,0:T(8,128)S(1)} %get-tuple-element.38.refs_1_), channel_id=1, source_target_pairs={{0,3},{1,0},{2,1},{3,2},{4,5},{5,6},{6,7},{7,4},{8,11},{9,8},{10,9... | collective-permute-start | bytes 589832 | tf_op jit(solution)/shard_map/ppermute | solution.py:558
  28.3 0.8 %collective-permute-start.17 = (f32[3,4,4,8,128]{4,3,2,1,0:T(8,128)S(1)}, f32[3,4,4,8,128]{4,3,2,1,0:T(8,128)S(1)}, u32[]{:S(2)}, u32[]{:S(2)}) collective-permute-start(f32[3,4,4,8,128]{4,3,2,1,0:T(8,128)S(1)} %get-tuple-element.40.refs_3_), channel_id=1, source_target_pairs={{0,1},{1,2},{2,3},{3,0},{4,7},{5,4},{6,5},{7,6},{8,9},{9,10},{10,1... | collective-permute-start | bytes 589832 | tf_op jit(solution)/shard_map/ppermute | solution.py:559
  29.0 1.8 %own.1 = (f32[2,7,8,4,8,128]{5,4,3,2,1,0:T(8,128)S(1)}, f32[2,3,8,4,8,128]{5,4,3,2,1,0:T(8,128)S(1)}, f32[8,2,3,2,4,8,128]{6,5,4,3,2,1,0:T(8,128)S(1)}, f32[2,8,4,8,128]{4,3,2,1,0:T(8,128)S(1)}) custom-call(f32[3,4,4,8,128]{4,3,2,1,0:T(8,128)S(1)} %get-tuple-element.35.refs_2_.refs_0_, f32[3,4,4,8,128]{4,3,2,1,0:T(8,128)S(1)} %get-tuple-element.38.refs_1_, ...), custom_call_target="tpu_custom_call" | custom-call | flops 11796480 | bytes 5767168 | tf_op jit(solution)/shard_map/own/pallas_call | solution.py:461
  30.9 3.3 %collective-permute-done.12.refs_0_ = f32[8,4,8,128]{3,2,1,0:T(8,128)S(1)} collective-permute-done((f32[8,4,8,128]{3,2,1,0:T(8,128)S(1)}, f32[8,4,8,128]{3,2,1,0:T(8,128)S(1)}, u32[]{:S(2)}, u32[]{:S(2)}) %collective-permute-start.12) | collective-permute-done | bytes 131104 | tf_op jit(solution)/shard_map/ppermute | solution.py:562
  34.1 0.0 collective-permute-done.14.refs_2_.refs_7_
  34.1 0.0 collective-permute-done.13.refs_1_.refs_6_
  34.2 0.1 collective-permute-start.15
  34.2 1.4 %collective-permute-done.15.refs_3_ = f32[9,4,8,128]{3,2,1,0:T(8,128)S(1)} collective-permute-done((f32[9,4,8,128]{3,2,1,0:T(8,128)S(1)}, f32[9,4,8,128]{3,2,1,0:T(8,128)S(1)}, u32[]{:S(2)}, u32[]{:S(2)}) %collective-permute-start.15) | collective-permute-done | bytes 147488 | tf_op jit(solution)/shard_map/ppermute | solution.py:581
  35.6 2.0 %stage0.1 = (f32[2,3,5,4,8,128]{5,4,3,2,1,0:T(8,128)S(1)}, f32[8,2,3,2,4,8,128]{6,5,4,3,2,1,0:T(8,128)S(1)}, f32[2,3,4,32,128]{4,3,2,1,0:T(8,128)S(1)}, f32[2,7,9,4,8,128]{5,4,3,2,1,0:T(8,128)S(1)}) custom-call(f32[2,7,8,4,8,128]{5,4,3,2,1,0:T(8,128)S(1)} %get-tuple-element.41.refs_0_, f32[2,8,4,8,128]{4,3,2,1,0:T(8,128)S(1)} %get-tuple-element.42.refs_1_, ...), custom_call_target="tpu_custom_call" | custom-call | flops 15728640 | bytes 9666560 | tf_op jit(solution)/shard_map/stage0/pallas_call | solution.py:461
  37.6 2.2 %collective-permute-done.16.refs_5_ = f32[3,4,4,8,128]{4,3,2,1,0:T(8,128)S(1)} collective-permute-done((f32[3,4,4,8,128]{4,3,2,1,0:T(8,128)S(1)}, f32[3,4,4,8,128]{4,3,2,1,0:T(8,128)S(1)}, u32[]{:S(2)}, u32[]{:S(2)}) %collective-permute-start.16) | collective-permute-done | bytes 196640 | tf_op jit(solution)/shard_map/ppermute | solution.py:558
  39.8 3.6 %collective-permute-done.17.refs_6_ = f32[3,4,4,8,128]{4,3,2,1,0:T(8,128)S(1)} collective-permute-done((f32[3,4,4,8,128]{4,3,2,1,0:T(8,128)S(1)}, f32[3,4,4,8,128]{4,3,2,1,0:T(8,128)S(1)}, u32[]{:S(2)}, u32[]{:S(2)}) %collective-permute-start.17) | collective-permute-done | bytes 196640 | tf_op jit(solution)/shard_map/ppermute | solution.py:559
  43.5 2.6 %stage1.1 = f32[1,3,16,32,128]{4,3,2,1,0:T(8,128)} custom-call(f32[2,7,8,4,8,128]{5,4,3,2,1,0:T(8,128)S(1)} %get-tuple-element.41.refs_0_, f32[2,7,9,4,8,128]{5,4,3,2,1,0:T(8,128)S(1)} %get-tuple-element.45.refs_1_, f32[2,3,8,4,8,128]{5,4,3,2,1,0:T(8,128)S(1)} %get-tuple-element.44.refs_4_.refs_2_, f32[2,3,5,4,8,128]{5,4,3,2,1,0:T(8,128)S(1)} %get-tuple-element.46.refs_3_, ...), custom_call_target="tpu_custom_call" | custom-call | flops 15728640 | bytes 8323072 | tf_op jit(solution)/shard_map/stage1/pallas_call | solution.py:461
  (8 shorter events, 0.1 us)
Async XLA Ops:
  0.0 2.9 %collective-permute-start.2 = (f32[1,3,16,32,128]{4,3,2,1,0:T(8,128)}, f32[1,3,16,32,128]{4,3,2,1,0:T(8,128)S(1)}, u32[]{:S(2)}, u32[]{:S(2)}) collective-permute-start(f32[1,3,16,32,128]{4,3,2,1,0:T(8,128)} %vel.1), channel_id=1, source_target_pairs={{0,4},{4,0},{8,12},{12,8},{16,20},{20,16},{24,28},{28,24},{1,5},{5... | collective-permute-start | bytes 2359304 | tf_op jit(solution)/shard_map/ppermute | solution.py:499
  0.5 1.1 %copy-start = (f32[1,3,16,32,128]{4,3,2,1,0:T(8,128)S(1)}, f32[1,3,16,32,128]{4,3,2,1,0:T(8,128)}, u32[]{:S(2)}) copy-start(f32[1,3,16,32,128]{4,3,2,1,0:T(8,128)} %force.1) | copy-start | bytes 2359300
  1.6 1.1 %copy-start.1 = (f32[1,3,16,32,128]{4,3,2,1,0:T(8,128)S(1)}, f32[1,3,16,32,128]{4,3,2,1,0:T(8,128)}, u32[]{:S(2)}) copy-start(f32[1,3,16,32,128]{4,3,2,1,0:T(8,128)} %vel.1) | copy-start | bytes 2359300
  3.0 6.9 %collective-permute-start.3 = (f32[4,4,4,8,128]{4,3,2,1,0:T(8,128)S(1)}, f32[4,4,4,8,128]{4,3,2,1,0:T(8,128)S(1)}, u32[]{:S(2)}, u32[]{:S(2)}) collective-permute-start(f32[4,4,4,8,128]{4,3,2,1,0:T(8,128)S(1)} %get-tuple-element.31.refs_0_), channel_id=1, source_target_pairs={{0,8},{4,20},{8,0},{12,28},{16,24},{20,4},{24,16},{28,12},{1,9},{5... | collective-permute-start | bytes 786440 | tf_op jit(solution)/shard_map/ppermute | solution.py:530
  5.6 8.2 %collective-permute-start.5 = (f32[4,4,4,8,128]{4,3,2,1,0:T(8,128)S(1)}, f32[4,4,4,8,128]{4,3,2,1,0:T(8,128)S(1)}, u32[]{:S(2)}, u32[]{:S(2)}) collective-permute-start(f32[4,4,4,8,128]{4,3,2,1,0:T(8,128)S(1)} %get-tuple-element.32.refs_0_), channel_id=1, source_target_pairs={{0,8},{4,20},{8,0},{12,28},{16,24},{20,4},{24,16},{28,12},{1,9},{5... | collective-permute-start | bytes 786440 | tf_op jit(solution)/shard_map/ppermute | solution.py:530
  5.7 6.4 %collective-permute-start = (f32[3,1,4,8,128]{4,3,2,1,0:T(8,128)S(1)}, f32[3,1,4,8,128]{4,3,2,1,0:T(8,128)S(1)}, u32[]{:S(2)}, u32[]{:S(2)}) collective-permute-start(f32[3,1,4,8,128]{4,3,2,1,0:T(8,128)S(1)} %get-tuple-element.29), channel_id=1, source_target_pairs={{0,1},{1,2},{2,3},{3,0},{4,5},{5,6},{6,7},{7,4},{8,9},{9,10},{10,1... | collective-permute-start | bytes 147464 | tf_op jit(solution)/shard_map/ppermute | solution.py:508
  7.7 4.6 %collective-permute-start.1 = (f32[3,1,4,8,128]{4,3,2,1,0:T(8,128)S(1)}, f32[3,1,4,8,128]{4,3,2,1,0:T(8,128)S(1)}, u32[]{:S(2)}, u32[]{:S(2)}) collective-permute-start(f32[3,1,4,8,128]{4,3,2,1,0:T(8,128)S(1)} %get-tuple-element.30), channel_id=1, source_target_pairs={{0,3},{1,0},{2,1},{3,2},{4,7},{5,4},{6,5},{7,6},{8,11},{9,8},{10,9... | collective-permute-start | bytes 147464 | tf_op jit(solution)/shard_map/ppermute | solution.py:507
  10.0 6.5 %collective-permute-start.4 = (f32[4,4,4,8,128]{4,3,2,1,0:T(8,128)S(1)}, f32[4,4,4,8,128]{4,3,2,1,0:T(8,128)S(1)}, u32[]{:S(2)}, u32[]{:S(2)}) collective-permute-start(f32[4,4,4,8,128]{4,3,2,1,0:T(8,128)S(1)} %add0.1.refs_2_.refs_0_), channel_id=1, source_target_pairs={{0,16},{4,12},{8,24},{12,4},{16,0},{20,28},{24,8},{28,20},{1,17},{... | collective-permute-start | bytes 786440 | tf_op jit(solution)/shard_map/ppermute | solution.py:530
  12.3 1.4 %collective-permute-start.6 = (f32[11,1,4,8,128]{4,3,2,1,0:T(8,128)S(1)}, f32[11,1,4,8,128]{4,3,2,1,0:T(8,128)S(1)}, u32[]{:S(2)}, u32[]{:S(2)}) collective-permute-start(f32[11,1,4,8,128]{4,3,2,1,0:T(8,128)S(1)} %gate.2), channel_id=1, source_target_pairs={{0,4},{4,0},{8,12},{12,8},{16,20},{20,16},{24,28},{28,24},{1,5},{5... | collective-permute-start | bytes 540680 | tf_op jit(solution)/shard_map/ppermute | solution.py:512
  13.8 8.8 %collective-permute-start.9 = (f32[4,4,4,8,128]{4,3,2,1,0:T(8,128)S(1)}, f32[4,4,4,8,128]{4,3,2,1,0:T(8,128)S(1)}, u32[]{:S(2)}, u32[]{:S(2)}) collective-permute-start(f32[4,4,4,8,128]{4,3,2,1,0:T(8,128)S(1)} %add1.1.refs_2_.refs_0_), channel_id=1, source_target_pairs={{0,16},{4,12},{8,24},{12,4},{16,0},{20,28},{24,8},{28,20},{1,17},{... | collective-permute-start | bytes 786440 | tf_op jit(solution)/shard_map/ppermute | solution.py:530
  16.5 1.4 %collective-permute-start.7 = (f32[2,4,4,8,128]{4,3,2,1,0:T(8,128)S(1)}, f32[2,4,4,8,128]{4,3,2,1,0:T(8,128)S(1)}, u32[]{:S(2)}, u32[]{:S(2)}) collective-permute-start(f32[2,4,4,8,128]{4,3,2,1,0:T(8,128)S(1)} %get-tuple-element.33.mine), channel_id=1, source_target_pairs={{0,4},{4,0},{8,12},{12,8},{16,20},{20,16},{24,28},{28,24},{1,5},{5... | collective-permute-start | bytes 393224 | tf_op jit(solution)/shard_map/ppermute | solution.py:542
  16.6 1.5 %collective-permute-start.8 = (f32[2,4,4,8,128]{4,3,2,1,0:T(8,128)S(1)}, f32[2,4,4,8,128]{4,3,2,1,0:T(8,128)S(1)}, u32[]{:S(2)}, u32[]{:S(2)}) collective-permute-start(f32[2,4,4,8,128]{4,3,2,1,0:T(8,128)S(1)} %get-tuple-element.34.mine_rest.refs_4_), channel_id=1, source_target_pairs={{0,4},{4,0},{8,12},{12,8},{16,20},{20,16},{24,28},{28,24},{1,5},{5... | collective-permute-start | bytes 393224 | tf_op jit(solution)/shard_map/ppermute | solution.py:542
  18.4 15.7 %collective-permute-start.13 = (f32[3,4,4,8,128]{4,3,2,1,0:T(8,128)S(1)}, f32[3,4,4,8,128]{4,3,2,1,0:T(8,128)S(1)}, u32[]{:S(2)}, u32[]{:S(2)}) collective-permute-start(f32[3,4,4,8,128]{4,3,2,1,0:T(8,128)S(1)} %get-tuple-element.35.refs_2_.refs_0_), channel_id=1, source_target_pairs={{0,3},{1,0},{2,1},{3,2},{4,5},{5,6},{6,7},{7,4},{8,11},{9,8},{10,9... | collective-permute-start | bytes 589832 | tf_op jit(solution)/shard_map/ppermute | solution.py:558
  22.7 4.0 %collective-permute-start.11 = (f32[2,4,4,8,128]{4,3,2,1,0:T(8,128)S(1)}, f32[2,4,4,8,128]{4,3,2,1,0:T(8,128)S(1)}, u32[]{:S(2)}, u32[]{:S(2)}) collective-permute-start(f32[2,4,4,8,128]{4,3,2,1,0:T(8,128)S(1)} %get-tuple-element.37.mine_rest.refs_5_), channel_id=1, source_target_pairs={{0,4},{4,0},{8,12},{12,8},{16,20},{20,16},{24,28},{28,24},{1,5},{5... | collective-permute-start | bytes 393224 | tf_op jit(solution)/shard_map/ppermute | solution.py:542
  22.7 11.4 %collective-permute-start.14 = (f32[3,4,4,8,128]{4,3,2,1,0:T(8,128)S(1)}, f32[3,4,4,8,128]{4,3,2,1,0:T(8,128)S(1)}, u32[]{:S(2)}, u32[]{:S(2)}) collective-permute-start(f32[3,4,4,8,128]{4,3,2,1,0:T(8,128)S(1)} %get-tuple-element.39.refs_2_), channel_id=1, source_target_pairs={{0,1},{1,2},{2,3},{3,0},{4,7},{5,4},{6,5},{7,6},{8,9},{9,10},{10,1... | collective-permute-start | bytes 589832 | tf_op jit(solution)/shard_map/ppermute | solution.py:559
  22.8 3.9 %collective-permute-start.10 = (f32[2,4,4,8,128]{4,3,2,1,0:T(8,128)S(1)}, f32[2,4,4,8,128]{4,3,2,1,0:T(8,128)S(1)}, u32[]{:S(2)}, u32[]{:S(2)}) collective-permute-start(f32[2,4,4,8,128]{4,3,2,1,0:T(8,128)S(1)} %get-tuple-element.36.mine), channel_id=1, source_target_pairs={{0,4},{4,0},{8,12},{12,8},{16,20},{20,16},{24,28},{28,24},{1,5},{5... | collective-permute-start | bytes 393224 | tf_op jit(solution)/shard_map/ppermute | solution.py:542
  24.2 9.9 %collective-permute-start.12 = (f32[8,4,8,128]{3,2,1,0:T(8,128)S(1)}, f32[8,4,8,128]{3,2,1,0:T(8,128)S(1)}, u32[]{:S(2)}, u32[]{:S(2)}) collective-permute-start(f32[8,4,8,128]{3,2,1,0:T(8,128)S(1)} %pad_maximum_fusion), channel_id=1, source_target_pairs={{0,3},{1,0},{2,1},{3,2},{4,5},{5,6},{6,7},{7,4},{8,11},{9,8},{10,9... | collective-permute-start | bytes 393224 | tf_op jit(solution)/shard_map/ppermute | solution.py:562
  27.0 12.9 %collective-permute-start.16 = (f32[3,4,4,8,128]{4,3,2,1,0:T(8,128)S(1)}, f32[3,4,4,8,128]{4,3,2,1,0:T(8,128)S(1)}, u32[]{:S(2)}, u32[]{:S(2)}) collective-permute-start(f32[3,4,4,8,128]{4,3,2,1,0:T(8,128)S(1)} %get-tuple-element.38.refs_1_), channel_id=1, source_target_pairs={{0,3},{1,0},{2,1},{3,2},{4,5},{5,6},{6,7},{7,4},{8,11},{9,8},{10,9... | collective-permute-start | bytes 589832 | tf_op jit(solution)/shard_map/ppermute | solution.py:558
  28.3 15.2 %collective-permute-start.17 = (f32[3,4,4,8,128]{4,3,2,1,0:T(8,128)S(1)}, f32[3,4,4,8,128]{4,3,2,1,0:T(8,128)S(1)}, u32[]{:S(2)}, u32[]{:S(2)}) collective-permute-start(f32[3,4,4,8,128]{4,3,2,1,0:T(8,128)S(1)} %get-tuple-element.40.refs_3_), channel_id=1, source_target_pairs={{0,1},{1,2},{2,3},{3,0},{4,7},{5,4},{6,5},{7,6},{8,9},{9,10},{10,1... | collective-permute-start | bytes 589832 | tf_op jit(solution)/shard_map/ppermute | solution.py:559
  34.2 1.4 %collective-permute-start.15 = (f32[9,4,8,128]{3,2,1,0:T(8,128)S(1)}, f32[9,4,8,128]{3,2,1,0:T(8,128)S(1)}, u32[]{:S(2)}, u32[]{:S(2)}) collective-permute-start(f32[9,4,8,128]{3,2,1,0:T(8,128)S(1)} %gate.3.refs_2_), channel_id=1, source_target_pairs={{0,4},{4,0},{8,12},{12,8},{16,20},{20,16},{24,28},{28,24},{1,5},{5... | collective-permute-start | bytes 442376 | tf_op jit(solution)/shard_map/ppermute | solution.py:581

commit v3 on v2

--- a/solution.py
+++ b/solution.py
@@ -20,13 +20,8 @@
 ROWS = 8
 PIECES = ((0, 4), (4, 8))
 STAGES = ((0, 4), (4, 8))
-OWN = True
-GATE = True
-PAD = 1
-TIE = False
-SINGLE = False
-FAKE = 11
-WEIGHT = {}
+PAD = 5
+FAKE = 9
 VMEM_LIMIT = 40 * 1024 * 1024
 
 
@@ -112,9 +107,23 @@
     refs[-1][...] = refs[0][...] + refs[1][...]
 
 
+def quarter():
+    return lax.rem(lax.axis_index("member") // 2, 2)
+
+
 def gate_kernel(*refs):
     count = refs[0].shape[0]
     refs[-1][:count] = refs[0][...]
+
+
+def share_kernel(*refs):
+    count = refs[0].shape[0]
+    refs[-2][...] = refs[0][...]
+    refs[-1][:count] = refs[0][...]
+
+
+def pick_kernel(first, second, out):
+    out[...] = jnp.where(quarter() == 0, first[1], second[1])
 
 
 def stats_kernel(members, add_two, *refs):
@@ -319,7 +328,8 @@
     width = far - near
     (coef_own,) = take()
     if first:
-        visc_own, visc_got, visc_other = take(3)
+        (visc_own,) = take()
+        visc_halo = take(4)
     else:
         (coef_halo,) = take()
     scaled_own = take()[0]
@@ -364,11 +374,13 @@
                     field[k, s, c, width + e] = edges_in[k, s, c, e]
 
     if first:
-        for which, got in ((side, visc_got), (1 - side, visc_other)):
-            for lo, hi in pieces:
-                for e in range(hi - lo):
-                    i = jnp.where(which == 0, depth - 1 - lo - e, depth - hi + e)
-                    visc[1 - which, i] = got[lo + e]
+        length = pieces[0][1] - pieces[0][0]
+        for hop, got in enumerate(visc_halo):
+            which = side if hop % 2 == 0 else 1 - side
+            lo = length * (quarter() if hop < 2 else 1 - quarter())
+            for e in range(length):
+                i = jnp.where(which == 0, depth - 1 - lo - e, depth - lo - length + e)
+                visc[1 - which, i] = got[e]
         for s in range(2):
             for d in range(2):
                 visc[s, depth + d] = visc_own[s, d]
@@ -456,8 +468,7 @@
 
 def call(kernel, outs, ins, flops, scratch=(), any_out=False, name=None):
     shapes = [jax.ShapeDtypeStruct(shape, jnp.float32) for shape in outs]
-    size = int(3.7e6 * WEIGHT[name]) if name in WEIGHT else 4 * sum(math.prod(shape) for shape in outs) + 4 * sum(x.size for x in ins)
-    flops = 0 if name in WEIGHT else flops
+    size = 4 * sum(math.prod(shape) for shape in outs) + 4 * sum(x.size for x in ins)
     result = pl.pallas_call(
         kernel,
         out_shape=shapes,
@@ -540,8 +551,6 @@
             name="stats%d" % i,
         )
         swapped = [lax.ppermute(x, "member", swap) for x in stats]
-        if SINGLE:
-            swapped = [jnp.concatenate([lax.ppermute(x[:1], "member", swap), lax.ppermute(x[1:], "member", swap)]) for x in stats]
         stats_mine.append(stats[1])
         stats_theirs.append(swapped[1])
         mine, theirs = call(
@@ -558,8 +567,9 @@
             halo_mine.append(lax.ppermute(mine_part, ("member", "sub"), along(True)))
             halo_theirs.append(lax.ppermute(theirs_part, ("member", "sub"), along(False)))
         tie = [mine]
-    visc = jnp.concatenate([rest[1] for rest in stats_mine], 0)
-    visc_got = lax.ppermute(visc, ("member", "sub"), along(True))
+    visc = call(pick_kernel, [stats_mine[0].shape[1:]], stats_mine, 1, name="pick")[0]
+    visc_mine = lax.ppermute(visc, ("member", "sub"), along(True))
+
     own = call(
         functools.partial(own_kernel, PIECES, sizes, nx),
         [(2, 7, depth, *layer), (2, comps, depth, *layer), (depth, 2, comps, 2, *layer), (2, depth, *layer)],
@@ -569,22 +579,23 @@
         name="own",
     )
     coef_own, scaled_own, edges, visc_own = own
-    if GATE:
-        tie = [src_mine[-1]] if TIE else []
-        visc_got = call(
-            gate_kernel,
-            [(PAD + depth, *layer)],
-            [visc_got, halo_mine[0], halo_theirs[0]] + tie + ([edges] if OWN else []),
-            1,
-            name="gate",
-        )[0]
-    visc_other = lax.ppermute(visc_got, "member", swap)
+    visc_mine, padded = call(
+        share_kernel,
+        [visc.shape, (PAD + visc.shape[0], *layer)],
+        [visc_mine, halo_mine[0], halo_theirs[0], edges],
+        1,
+        name="share",
+    )
+    visc_halo = [visc_mine] + [
+        lax.ppermute(value, "member", [(m, m ^ hop) for m in range(members)])
+        for hop, value in ((1, padded), (2, visc_mine), (3, visc_mine))
+    ]
     olds, scaled_old, parts = [], [], []
     for n, (piece, mine, theirs) in enumerate(zip(STAGES, halo_mine, halo_theirs)):
         first, final = n == 0, n == len(STAGES) - 1
         width = piece[1] - piece[0]
         ins = [coef_own]
-        ins += [visc_own, visc_got, visc_other] if first else [coef_halo]
+        ins += [visc_own, *visc_halo] if first else [coef_halo]
         ins += [scaled_own] + scaled_old + [edges, mine, theirs]
         scratch = [pltpu.VMEM((depth, 2, comps, width + 2, *layer), f32)]
         if first:

time: 46.2 us -> 44.9 us (0.972)
  waiting for transfers between devices: 14.4 us -> 9.84 us
  starting transfers between devices: 21.7 us -> 25 us
    ppermute x2 -> x4, starting transfers between devices: 2.55 us -> 6.73 us  [the longest x3 3.59 us: fast(): lax.ppermute(value, 'member', [(m, m ^ hop) for m in range(members)])]
    ppermute x2, waiting for transfers between devices: 3.61 us -> 0.89 us  [fast(): lax.ppermute(theirs_part, ('member', 'sub'), along(False))]
    ppermute x2, waiting for transfers between devices: 2.22 us -> 0.01 us  [fast(): halo_mine.append(lax.ppermute(mine_part, ('member', 'sub'), along(True)))]
    ppermute x2, starting transfers between devices: 0.81 us -> 2.99 us  [fast(): lax.ppermute(theirs_part, ('member', 'sub'), along(False))]
    ppermute x2, starting transfers between devices: 5.48 us -> 3.31 us  [fast(): halo_mine.append(lax.ppermute(mine_part, ('member', 'sub'), along(True)))]
    ppermute x4, starting transfers between devices: 2.02 us -> 1.14 us  [fast(): swapped = [lax.ppermute(x, 'member', swap) for x in stats]]
    ppermute x2 -> x4, waiting for transfers between devices: 4.62 us -> 4.98 us  [the longest x3 4.09 us: fast(): lax.ppermute(value, 'member', [(m, m ^ hop) for m in range(members)])]
    pallas_call x13 -> x14, Pallas kernels: 7.45 us -> 7.47 us  [call(): pl.pallas_call(kernel, out_shape=shapes, in_specs=vmem(len(ins)), out_spe...]
  transfers between devices with their start and end apart: 18 -> 20, of which waited for: 10 -> 10; matrix products, arithmetic and copies ran while one was open for 0% -> 0% of each run, Pallas kernels for 10% -> 11%
where the time goes in v3:
time: 44.9 us; the launch traced here: 44.7 us
  starting transfers between devices  25 us (56%)
  waiting for transfers between devices  9.84 us (22%)
  Pallas kernels  7.47 us (17%)
  local copies, waits for them, and re-layouts  2.27 us (5%)
    pallas_call x14, Pallas kernels, call(): pl.pallas_call(kernel, out_shape=shapes, in_specs=vmem(len(ins)), out_spe...  7.47 us
    ppermute x4, starting transfers between devices, fast(): got[i] = lax.ppermute(part, 'member', pair(step))  6.37 us
    ppermute x3, waiting for transfers between devices, fast(): lax.ppermute(value, 'member', [(m, m ^ hop) for m in range(members)])  4.09 us
    ppermute x3, starting transfers between devices, fast(): lax.ppermute(value, 'member', [(m, m ^ hop) for m in range(members)])  3.59 us
    ppermute x2, starting transfers between devices, fast(): halo_mine.append(lax.ppermute(mine_part, ('member', 'sub'), along(True)))  3.31 us
    ppermute x1, starting transfers between devices, fast(): visc_mine = lax.ppermute(visc, ('member', 'sub'), along(True))  3.14 us
    ppermute x2, starting transfers between devices, fast(): lax.ppermute(theirs_part, ('member', 'sub'), along(False))  2.99 us
    unnamed x4, local copies, waits for them, and re-layouts  2.27 us
  transfers between devices with their start and end apart: 20, of which 10 were waited for; matrix products, arithmetic and copies ran while one was open for 0% of the time, Pallas kernels for 11%

profile of v3, /device:TPU:0, one launch (start us, length us, event | category | flops | bytes accessed | tf_op | source)
XLA Modules:
  0.0 44.7 jit_solution(6939831393376252198)
XLA Ops:
  0.0 0.5 %collective-permute-start.2 = (f32[1,3,16,32,128]{4,3,2,1,0:T(8,128)}, f32[1,3,16,32,128]{4,3,2,1,0:T(8,128)S(1)}, u32[]{:S(2)}, u32[]{:S(2)}) collective-permute-start(f32[1,3,16,32,128]{4,3,2,1,0:T(8,128)} %vel.1), channel_id=1, source_target_pairs={{0,4},{4,0},{8,12},{12,8},{16,20},{20,16},{24,28},{28,24},{1,5},{5... | collective-permute-start | bytes 2359304 | tf_op jit(solution)/shard_map/ppermute | solution.py:510
  0.5 1.1 %copy-done = f32[1,3,16,32,128]{4,3,2,1,0:T(8,128)S(1)} copy-done((f32[1,3,16,32,128]{4,3,2,1,0:T(8,128)S(1)}, f32[1,3,16,32,128]{4,3,2,1,0:T(8,128)}, u32[]{:S(2)}) %copy-start) | copy-done | bytes 786456
  1.6 1.1 %copy-done.1 = f32[1,3,16,32,128]{4,3,2,1,0:T(8,128)S(1)} copy-done((f32[1,3,16,32,128]{4,3,2,1,0:T(8,128)S(1)}, f32[1,3,16,32,128]{4,3,2,1,0:T(8,128)}, u32[]{:S(2)}) %copy-start.1) | copy-done | bytes 786456
  2.7 0.2 arrange.1
  2.9 0.0 collective-permute-done.2.other
  2.9 0.1 sums.1
  3.0 2.6 %collective-permute-start.3 = (f32[4,4,4,8,128]{4,3,2,1,0:T(8,128)S(1)}, f32[4,4,4,8,128]{4,3,2,1,0:T(8,128)S(1)}, u32[]{:S(2)}, u32[]{:S(2)}) collective-permute-start(f32[4,4,4,8,128]{4,3,2,1,0:T(8,128)S(1)} %get-tuple-element.33.refs_0_), channel_id=1, source_target_pairs={{0,8},{4,20},{8,0},{12,28},{16,24},{20,4},{24,16},{28,12},{1,9},{5... | collective-permute-start | bytes 786440 | tf_op jit(solution)/shard_map/ppermute | solution.py:541
  5.6 0.1 collective-permute-start.5
  5.7 2.0 %collective-permute-start = (f32[3,1,4,8,128]{4,3,2,1,0:T(8,128)S(1)}, f32[3,1,4,8,128]{4,3,2,1,0:T(8,128)S(1)}, u32[]{:S(2)}, u32[]{:S(2)}) collective-permute-start(f32[3,1,4,8,128]{4,3,2,1,0:T(8,128)S(1)} %get-tuple-element.31), channel_id=1, source_target_pairs={{0,1},{1,2},{2,3},{3,0},{4,5},{5,6},{6,7},{7,4},{8,9},{9,10},{10,1... | collective-permute-start | bytes 147464 | tf_op jit(solution)/shard_map/ppermute | solution.py:519
  7.7 2.0 %collective-permute-start.1 = (f32[3,1,4,8,128]{4,3,2,1,0:T(8,128)S(1)}, f32[3,1,4,8,128]{4,3,2,1,0:T(8,128)S(1)}, u32[]{:S(2)}, u32[]{:S(2)}) collective-permute-start(f32[3,1,4,8,128]{4,3,2,1,0:T(8,128)S(1)} %get-tuple-element.32), channel_id=1, source_target_pairs={{0,3},{1,0},{2,1},{3,2},{4,7},{5,4},{6,5},{7,6},{8,11},{9,8},{10,9... | collective-permute-start | bytes 147464 | tf_op jit(solution)/shard_map/ppermute | solution.py:518
  9.8 0.2 collective-permute-done.3.refs_1_
  10.0 2.1 %collective-permute-start.4 = (f32[4,4,4,8,128]{4,3,2,1,0:T(8,128)S(1)}, f32[4,4,4,8,128]{4,3,2,1,0:T(8,128)S(1)}, u32[]{:S(2)}, u32[]{:S(2)}) collective-permute-start(f32[4,4,4,8,128]{4,3,2,1,0:T(8,128)S(1)} %add0.1.refs_2_.refs_0_), channel_id=1, source_target_pairs={{0,16},{4,12},{8,24},{12,4},{16,0},{20,28},{24,8},{28,20},{1,17},{... | collective-permute-start | bytes 786440 | tf_op jit(solution)/shard_map/ppermute | solution.py:541
  12.1 0.0 collective-permute-done.refs_0_.below
  12.1 0.2 collective-permute-done.1.refs_1_.above
  12.3 0.0 collective-permute-start.6
  12.4 1.4 %collective-permute-done.6.refs_3_ = f32[9,1,4,8,128]{4,3,2,1,0:T(8,128)S(1)} collective-permute-done((f32[9,1,4,8,128]{4,3,2,1,0:T(8,128)S(1)}, f32[9,1,4,8,128]{4,3,2,1,0:T(8,128)S(1)}, u32[]{:S(2)}, u32[]{:S(2)}) %collective-permute-start.6) | collective-permute-done | bytes 147488 | tf_op jit(solution)/shard_map/ppermute | solution.py:523
  13.8 1.6 %collective-permute-start.9 = (f32[4,4,4,8,128]{4,3,2,1,0:T(8,128)S(1)}, f32[4,4,4,8,128]{4,3,2,1,0:T(8,128)S(1)}, u32[]{:S(2)}, u32[]{:S(2)}) collective-permute-start(f32[4,4,4,8,128]{4,3,2,1,0:T(8,128)S(1)} %add1.1.refs_2_.refs_0_), channel_id=1, source_target_pairs={{0,16},{4,12},{8,24},{12,4},{16,0},{20,28},{24,8},{28,20},{1,17},{... | collective-permute-start | bytes 786440 | tf_op jit(solution)/shard_map/ppermute | solution.py:541
  15.3 1.1 %collective-permute-done.4.refs_1_ = f32[4,4,4,8,128]{4,3,2,1,0:T(8,128)S(1)} collective-permute-done((f32[4,4,4,8,128]{4,3,2,1,0:T(8,128)S(1)}, f32[4,4,4,8,128]{4,3,2,1,0:T(8,128)S(1)}, u32[]{:S(2)}, u32[]{:S(2)}) %collective-permute-start.4) | collective-permute-done | bytes 262176 | tf_op jit(solution)/shard_map/ppermute | solution.py:541
  16.5 0.1 stats0.1
  16.5 0.1 collective-permute-start.7
  16.6 0.5 %collective-permute-start.8 = (f32[2,4,4,8,128]{4,3,2,1,0:T(8,128)S(1)}, f32[2,4,4,8,128]{4,3,2,1,0:T(8,128)S(1)}, u32[]{:S(2)}, u32[]{:S(2)}) collective-permute-start(f32[2,4,4,8,128]{4,3,2,1,0:T(8,128)S(1)} %get-tuple-element.36.mine_rest.refs_4_.first), channel_id=1, source_target_pairs={{0,4},{4,0},{8,12},{12,8},{16,20},{20,16},{24,28},{28,24},{1,5},{5... | collective-permute-start | bytes 393224 | tf_op jit(solution)/shard_map/ppermute | solution.py:553
  17.1 0.8 %collective-permute-done.7.theirs = f32[2,4,4,8,128]{4,3,2,1,0:T(8,128)S(1)} collective-permute-done((f32[2,4,4,8,128]{4,3,2,1,0:T(8,128)S(1)}, f32[2,4,4,8,128]{4,3,2,1,0:T(8,128)S(1)}, u32[]{:S(2)}, u32[]{:S(2)}) %collective-permute-start.7) | collective-permute-done | bytes 131104 | tf_op jit(solution)/shard_map/ppermute | solution.py:553
  17.9 0.2 collective-permute-done.8.theirs_rest.refs_6_
  18.1 0.3 source0.1
  18.4 2.2 %collective-permute-start.14 = (f32[3,4,4,8,128]{4,3,2,1,0:T(8,128)S(1)}, f32[3,4,4,8,128]{4,3,2,1,0:T(8,128)S(1)}, u32[]{:S(2)}, u32[]{:S(2)}) collective-permute-start(f32[3,4,4,8,128]{4,3,2,1,0:T(8,128)S(1)} %get-tuple-element.41.refs_2_), channel_id=1, source_target_pairs={{0,1},{1,2},{2,3},{3,0},{4,7},{5,4},{6,5},{7,6},{8,9},{9,10},{10,1... | collective-permute-start | bytes 589832 | tf_op jit(solution)/shard_map/ppermute | solution.py:568
  20.6 2.1 %collective-permute-start.13 = (f32[3,4,4,8,128]{4,3,2,1,0:T(8,128)S(1)}, f32[3,4,4,8,128]{4,3,2,1,0:T(8,128)S(1)}, u32[]{:S(2)}, u32[]{:S(2)}) collective-permute-start(f32[3,4,4,8,128]{4,3,2,1,0:T(8,128)S(1)} %get-tuple-element.37.refs_2_.refs_0_), channel_id=1, source_target_pairs={{0,3},{1,0},{2,1},{3,2},{4,5},{5,6},{6,7},{7,4},{8,11},{9,8},{10,9... | collective-permute-start | bytes 589832 | tf_op jit(solution)/shard_map/ppermute | solution.py:567
  22.6 0.1 stats1.1
  22.7 0.1 collective-permute-start.10
  22.8 0.5 %collective-permute-start.11 = (f32[2,4,4,8,128]{4,3,2,1,0:T(8,128)S(1)}, f32[2,4,4,8,128]{4,3,2,1,0:T(8,128)S(1)}, u32[]{:S(2)}, u32[]{:S(2)}) collective-permute-start(f32[2,4,4,8,128]{4,3,2,1,0:T(8,128)S(1)} %get-tuple-element.39.mine_rest.refs_5_.second), channel_id=1, source_target_pairs={{0,4},{4,0},{8,12},{12,8},{16,20},{20,16},{24,28},{28,24},{1,5},{5... | collective-permute-start | bytes 393224 | tf_op jit(solution)/shard_map/ppermute | solution.py:553
  23.3 3.1 %collective-permute-start.12 = (f32[4,4,8,128]{3,2,1,0:T(8,128)S(1)}, f32[4,4,8,128]{3,2,1,0:T(8,128)S(1)}, u32[]{:S(2)}, u32[]{:S(2)}) collective-permute-start(f32[4,4,8,128]{3,2,1,0:T(8,128)S(1)} %pick.1), channel_id=1, source_target_pairs={{0,3},{1,0},{2,1},{3,2},{4,5},{5,6},{6,7},{7,4},{8,11},{9,8},{10,9... | collective-permute-start | bytes 196616 | tf_op jit(solution)/shard_map/ppermute | solution.py:571
  26.4 0.0 collective-permute-done.10.theirs
  26.4 0.0 collective-permute-done.11.theirs_rest.refs_7_
  26.4 0.3 source1.1
  26.7 1.2 %collective-permute-start.18 = (f32[3,4,4,8,128]{4,3,2,1,0:T(8,128)S(1)}, f32[3,4,4,8,128]{4,3,2,1,0:T(8,128)S(1)}, u32[]{:S(2)}, u32[]{:S(2)}) collective-permute-start(f32[3,4,4,8,128]{4,3,2,1,0:T(8,128)S(1)} %get-tuple-element.40.refs_1_), channel_id=1, source_target_pairs={{0,3},{1,0},{2,1},{3,2},{4,5},{5,6},{6,7},{7,4},{8,11},{9,8},{10,9... | collective-permute-start | bytes 589832 | tf_op jit(solution)/shard_map/ppermute | solution.py:567
  28.0 0.8 %collective-permute-start.19 = (f32[3,4,4,8,128]{4,3,2,1,0:T(8,128)S(1)}, f32[3,4,4,8,128]{4,3,2,1,0:T(8,128)S(1)}, u32[]{:S(2)}, u32[]{:S(2)}) collective-permute-start(f32[3,4,4,8,128]{4,3,2,1,0:T(8,128)S(1)} %get-tuple-element.42.refs_3_), channel_id=1, source_target_pairs={{0,1},{1,2},{2,3},{3,0},{4,7},{5,4},{6,5},{7,6},{8,9},{9,10},{10,1... | collective-permute-start | bytes 589832 | tf_op jit(solution)/shard_map/ppermute | solution.py:568
  28.8 1.8 %own.1 = (f32[2,7,8,4,8,128]{5,4,3,2,1,0:T(8,128)S(1)}, f32[2,3,8,4,8,128]{5,4,3,2,1,0:T(8,128)S(1)}, f32[8,2,3,2,4,8,128]{6,5,4,3,2,1,0:T(8,128)S(1)}, f32[2,8,4,8,128]{4,3,2,1,0:T(8,128)S(1)}) custom-call(f32[3,4,4,8,128]{4,3,2,1,0:T(8,128)S(1)} %get-tuple-element.37.refs_2_.refs_0_, f32[3,4,4,8,128]{4,3,2,1,0:T(8,128)S(1)} %get-tuple-element.40.refs_1_, ...), custom_call_target="tpu_custom_call" | custom-call | flops 11796480 | bytes 5767168 | tf_op jit(solution)/shard_map/own/pallas_call | solution.py:472
  30.6 0.9 %collective-permute-done.12.refs_0_ = f32[4,4,8,128]{3,2,1,0:T(8,128)S(1)} collective-permute-done((f32[4,4,8,128]{3,2,1,0:T(8,128)S(1)}, f32[4,4,8,128]{3,2,1,0:T(8,128)S(1)}, u32[]{:S(2)}, u32[]{:S(2)}) %collective-permute-start.12) | collective-permute-done | bytes 65568 | tf_op jit(solution)/shard_map/ppermute | solution.py:571
  31.5 0.0 collective-permute-done.14.refs_2_.refs_9_
  31.5 0.0 collective-permute-done.13.refs_1_.refs_8_
  31.6 1.9 %collective-permute-start.15 = (f32[9,4,8,128]{3,2,1,0:T(8,128)S(1)}, f32[9,4,8,128]{3,2,1,0:T(8,128)S(1)}, u32[]{:S(2)}, u32[]{:S(2)}) collective-permute-start(f32[9,4,8,128]{3,2,1,0:T(8,128)S(1)} %get-tuple-element.47), channel_id=1, source_target_pairs={{0,4},{4,0},{8,12},{12,8},{16,20},{20,16},{24,28},{28,24},{1,5},{5... | collective-permute-start | bytes 442376 | tf_op jit(solution)/shard_map/ppermute | solution.py:590
  33.4 1.0 %collective-permute-start.17 = (f32[4,4,8,128]{3,2,1,0:T(8,128)S(1)}, f32[4,4,8,128]{3,2,1,0:T(8,128)S(1)}, u32[]{:S(2)}, u32[]{:S(2)}) collective-permute-start(f32[4,4,8,128]{3,2,1,0:T(8,128)S(1)} %get-tuple-element.46.refs_2_), channel_id=1, source_target_pairs={{0,12},{4,8},{8,4},{12,0},{16,28},{20,24},{24,20},{28,16},{1,13},{... | collective-permute-start | bytes 196616 | tf_op jit(solution)/shard_map/ppermute | solution.py:590
  34.5 0.7 %collective-permute-start.16 = (f32[4,4,8,128]{3,2,1,0:T(8,128)S(1)}, f32[4,4,8,128]{3,2,1,0:T(8,128)S(1)}, u32[]{:S(2)}, u32[]{:S(2)}) collective-permute-start(f32[4,4,8,128]{3,2,1,0:T(8,128)S(1)} %get-tuple-element.46.refs_2_), channel_id=1, source_target_pairs={{0,8},{4,12},{8,0},{12,4},{16,24},{20,28},{24,16},{28,20},{1,9},{5... | collective-permute-start | bytes 196616 | tf_op jit(solution)/shard_map/ppermute | solution.py:590
  35.2 2.4 %collective-permute-done.17.refs_5_ = f32[4,4,8,128]{3,2,1,0:T(8,128)S(1)} collective-permute-done((f32[4,4,8,128]{3,2,1,0:T(8,128)S(1)}, f32[4,4,8,128]{3,2,1,0:T(8,128)S(1)}, u32[]{:S(2)}, u32[]{:S(2)}) %collective-permute-start.17) | collective-permute-done | bytes 65568 | tf_op jit(solution)/shard_map/ppermute | solution.py:590
  37.6 1.7 %collective-permute-done.16.refs_4_ = f32[4,4,8,128]{3,2,1,0:T(8,128)S(1)} collective-permute-done((f32[4,4,8,128]{3,2,1,0:T(8,128)S(1)}, f32[4,4,8,128]{3,2,1,0:T(8,128)S(1)}, u32[]{:S(2)}, u32[]{:S(2)}) %collective-permute-start.16) | collective-permute-done | bytes 65568 | tf_op jit(solution)/shard_map/ppermute | solution.py:590
  39.2 2.0 %stage0.1 = (f32[2,3,5,4,8,128]{5,4,3,2,1,0:T(8,128)S(1)}, f32[8,2,3,2,4,8,128]{6,5,4,3,2,1,0:T(8,128)S(1)}, f32[2,3,4,32,128]{4,3,2,1,0:T(8,128)S(1)}, f32[2,7,9,4,8,128]{5,4,3,2,1,0:T(8,128)S(1)}) custom-call(f32[2,7,8,4,8,128]{5,4,3,2,1,0:T(8,128)S(1)} %get-tuple-element.43.refs_0_, f32[2,8,4,8,128]{4,3,2,1,0:T(8,128)S(1)} %get-tuple-element.44.refs_1_, ...), custom_call_target="tpu_custom_call" | custom-call | flops 15728640 | bytes 9715712 | tf_op jit(solution)/shard_map/stage0/pallas_call | solution.py:472
  41.3 0.0 collective-permute-done.18.refs_5_
  41.3 0.9 %collective-permute-done.19.refs_6_ = f32[3,4,4,8,128]{4,3,2,1,0:T(8,128)S(1)} collective-permute-done((f32[3,4,4,8,128]{4,3,2,1,0:T(8,128)S(1)}, f32[3,4,4,8,128]{4,3,2,1,0:T(8,128)S(1)}, u32[]{:S(2)}, u32[]{:S(2)}) %collective-permute-start.19) | collective-permute-done | bytes 196640 | tf_op jit(solution)/shard_map/ppermute | solution.py:568
  42.2 2.6 %stage1.1 = f32[1,3,16,32,128]{4,3,2,1,0:T(8,128)} custom-call(f32[2,7,8,4,8,128]{5,4,3,2,1,0:T(8,128)S(1)} %get-tuple-element.43.refs_0_, f32[2,7,9,4,8,128]{5,4,3,2,1,0:T(8,128)S(1)} %get-tuple-element.49.refs_1_, f32[2,3,8,4,8,128]{5,4,3,2,1,0:T(8,128)S(1)} %get-tuple-element.48.refs_6_.refs_2_, f32[2,3,5,4,8,128]{5,4,3,2,1,0:T(8,128)S(1)} %get-tuple-element.50.refs_3_, ...), custom_call_target="tpu_custom_call" | custom-call | flops 15728640 | bytes 8323072 | tf_op jit(solution)/shard_map/stage1/pallas_call | solution.py:472
  (10 shorter events, 0.1 us)
Async XLA Ops:
  0.0 2.9 %collective-permute-start.2 = (f32[1,3,16,32,128]{4,3,2,1,0:T(8,128)}, f32[1,3,16,32,128]{4,3,2,1,0:T(8,128)S(1)}, u32[]{:S(2)}, u32[]{:S(2)}) collective-permute-start(f32[1,3,16,32,128]{4,3,2,1,0:T(8,128)} %vel.1), channel_id=1, source_target_pairs={{0,4},{4,0},{8,12},{12,8},{16,20},{20,16},{24,28},{28,24},{1,5},{5... | collective-permute-start | bytes 2359304 | tf_op jit(solution)/shard_map/ppermute | solution.py:510
  0.5 1.1 %copy-start = (f32[1,3,16,32,128]{4,3,2,1,0:T(8,128)S(1)}, f32[1,3,16,32,128]{4,3,2,1,0:T(8,128)}, u32[]{:S(2)}) copy-start(f32[1,3,16,32,128]{4,3,2,1,0:T(8,128)} %force.1) | copy-start | bytes 2359300
  1.6 1.1 %copy-start.1 = (f32[1,3,16,32,128]{4,3,2,1,0:T(8,128)S(1)}, f32[1,3,16,32,128]{4,3,2,1,0:T(8,128)}, u32[]{:S(2)}) copy-start(f32[1,3,16,32,128]{4,3,2,1,0:T(8,128)} %vel.1) | copy-start | bytes 2359300
  3.0 6.9 %collective-permute-start.3 = (f32[4,4,4,8,128]{4,3,2,1,0:T(8,128)S(1)}, f32[4,4,4,8,128]{4,3,2,1,0:T(8,128)S(1)}, u32[]{:S(2)}, u32[]{:S(2)}) collective-permute-start(f32[4,4,4,8,128]{4,3,2,1,0:T(8,128)S(1)} %get-tuple-element.33.refs_0_), channel_id=1, source_target_pairs={{0,8},{4,20},{8,0},{12,28},{16,24},{20,4},{24,16},{28,12},{1,9},{5... | collective-permute-start | bytes 786440 | tf_op jit(solution)/shard_map/ppermute | solution.py:541
  5.6 8.1 %collective-permute-start.5 = (f32[4,4,4,8,128]{4,3,2,1,0:T(8,128)S(1)}, f32[4,4,4,8,128]{4,3,2,1,0:T(8,128)S(1)}, u32[]{:S(2)}, u32[]{:S(2)}) collective-permute-start(f32[4,4,4,8,128]{4,3,2,1,0:T(8,128)S(1)} %get-tuple-element.34.refs_0_), channel_id=1, source_target_pairs={{0,8},{4,20},{8,0},{12,28},{16,24},{20,4},{24,16},{28,12},{1,9},{5... | collective-permute-start | bytes 786440 | tf_op jit(solution)/shard_map/ppermute | solution.py:541
  5.7 6.4 %collective-permute-start = (f32[3,1,4,8,128]{4,3,2,1,0:T(8,128)S(1)}, f32[3,1,4,8,128]{4,3,2,1,0:T(8,128)S(1)}, u32[]{:S(2)}, u32[]{:S(2)}) collective-permute-start(f32[3,1,4,8,128]{4,3,2,1,0:T(8,128)S(1)} %get-tuple-element.31), channel_id=1, source_target_pairs={{0,1},{1,2},{2,3},{3,0},{4,5},{5,6},{6,7},{7,4},{8,9},{9,10},{10,1... | collective-permute-start | bytes 147464 | tf_op jit(solution)/shard_map/ppermute | solution.py:519
  7.7 4.6 %collective-permute-start.1 = (f32[3,1,4,8,128]{4,3,2,1,0:T(8,128)S(1)}, f32[3,1,4,8,128]{4,3,2,1,0:T(8,128)S(1)}, u32[]{:S(2)}, u32[]{:S(2)}) collective-permute-start(f32[3,1,4,8,128]{4,3,2,1,0:T(8,128)S(1)} %get-tuple-element.32), channel_id=1, source_target_pairs={{0,3},{1,0},{2,1},{3,2},{4,7},{5,4},{6,5},{7,6},{8,11},{9,8},{10,9... | collective-permute-start | bytes 147464 | tf_op jit(solution)/shard_map/ppermute | solution.py:518
  10.0 6.5 %collective-permute-start.4 = (f32[4,4,4,8,128]{4,3,2,1,0:T(8,128)S(1)}, f32[4,4,4,8,128]{4,3,2,1,0:T(8,128)S(1)}, u32[]{:S(2)}, u32[]{:S(2)}) collective-permute-start(f32[4,4,4,8,128]{4,3,2,1,0:T(8,128)S(1)} %add0.1.refs_2_.refs_0_), channel_id=1, source_target_pairs={{0,16},{4,12},{8,24},{12,4},{16,0},{20,28},{24,8},{28,20},{1,17},{... | collective-permute-start | bytes 786440 | tf_op jit(solution)/shard_map/ppermute | solution.py:541
  12.3 1.4 %collective-permute-start.6 = (f32[9,1,4,8,128]{4,3,2,1,0:T(8,128)S(1)}, f32[9,1,4,8,128]{4,3,2,1,0:T(8,128)S(1)}, u32[]{:S(2)}, u32[]{:S(2)}) collective-permute-start(f32[9,1,4,8,128]{4,3,2,1,0:T(8,128)S(1)} %gate.1), channel_id=1, source_target_pairs={{0,4},{4,0},{8,12},{12,8},{16,20},{20,16},{24,28},{28,24},{1,5},{5... | collective-permute-start | bytes 442376 | tf_op jit(solution)/shard_map/ppermute | solution.py:523
  13.8 8.9 %collective-permute-start.9 = (f32[4,4,4,8,128]{4,3,2,1,0:T(8,128)S(1)}, f32[4,4,4,8,128]{4,3,2,1,0:T(8,128)S(1)}, u32[]{:S(2)}, u32[]{:S(2)}) collective-permute-start(f32[4,4,4,8,128]{4,3,2,1,0:T(8,128)S(1)} %add1.1.refs_2_.refs_0_), channel_id=1, source_target_pairs={{0,16},{4,12},{8,24},{12,4},{16,0},{20,28},{24,8},{28,20},{1,17},{... | collective-permute-start | bytes 786440 | tf_op jit(solution)/shard_map/ppermute | solution.py:541
  16.5 1.4 %collective-permute-start.7 = (f32[2,4,4,8,128]{4,3,2,1,0:T(8,128)S(1)}, f32[2,4,4,8,128]{4,3,2,1,0:T(8,128)S(1)}, u32[]{:S(2)}, u32[]{:S(2)}) collective-permute-start(f32[2,4,4,8,128]{4,3,2,1,0:T(8,128)S(1)} %get-tuple-element.35.mine), channel_id=1, source_target_pairs={{0,4},{4,0},{8,12},{12,8},{16,20},{20,16},{24,28},{28,24},{1,5},{5... | collective-permute-start | bytes 393224 | tf_op jit(solution)/shard_map/ppermute | solution.py:553
  16.6 1.5 %collective-permute-start.8 = (f32[2,4,4,8,128]{4,3,2,1,0:T(8,128)S(1)}, f32[2,4,4,8,128]{4,3,2,1,0:T(8,128)S(1)}, u32[]{:S(2)}, u32[]{:S(2)}) collective-permute-start(f32[2,4,4,8,128]{4,3,2,1,0:T(8,128)S(1)} %get-tuple-element.36.mine_rest.refs_4_.first), channel_id=1, source_target_pairs={{0,4},{4,0},{8,12},{12,8},{16,20},{20,16},{24,28},{28,24},{1,5},{5... | collective-permute-start | bytes 393224 | tf_op jit(solution)/shard_map/ppermute | solution.py:553
  18.4 13.1 %collective-permute-start.14 = (f32[3,4,4,8,128]{4,3,2,1,0:T(8,128)S(1)}, f32[3,4,4,8,128]{4,3,2,1,0:T(8,128)S(1)}, u32[]{:S(2)}, u32[]{:S(2)}) collective-permute-start(f32[3,4,4,8,128]{4,3,2,1,0:T(8,128)S(1)} %get-tuple-element.41.refs_2_), channel_id=1, source_target_pairs={{0,1},{1,2},{2,3},{3,0},{4,7},{5,4},{6,5},{7,6},{8,9},{9,10},{10,1... | collective-permute-start | bytes 589832 | tf_op jit(solution)/shard_map/ppermute | solution.py:568
  20.6 11.0 %collective-permute-start.13 = (f32[3,4,4,8,128]{4,3,2,1,0:T(8,128)S(1)}, f32[3,4,4,8,128]{4,3,2,1,0:T(8,128)S(1)}, u32[]{:S(2)}, u32[]{:S(2)}) collective-permute-start(f32[3,4,4,8,128]{4,3,2,1,0:T(8,128)S(1)} %get-tuple-element.37.refs_2_.refs_0_), channel_id=1, source_target_pairs={{0,3},{1,0},{2,1},{3,2},{4,5},{5,6},{6,7},{7,4},{8,11},{9,8},{10,9... | collective-permute-start | bytes 589832 | tf_op jit(solution)/shard_map/ppermute | solution.py:567
  22.7 3.7 %collective-permute-start.10 = (f32[2,4,4,8,128]{4,3,2,1,0:T(8,128)S(1)}, f32[2,4,4,8,128]{4,3,2,1,0:T(8,128)S(1)}, u32[]{:S(2)}, u32[]{:S(2)}) collective-permute-start(f32[2,4,4,8,128]{4,3,2,1,0:T(8,128)S(1)} %get-tuple-element.38.mine), channel_id=1, source_target_pairs={{0,4},{4,0},{8,12},{12,8},{16,20},{20,16},{24,28},{28,24},{1,5},{5... | collective-permute-start | bytes 393224 | tf_op jit(solution)/shard_map/ppermute | solution.py:553
  22.8 3.7 %collective-permute-start.11 = (f32[2,4,4,8,128]{4,3,2,1,0:T(8,128)S(1)}, f32[2,4,4,8,128]{4,3,2,1,0:T(8,128)S(1)}, u32[]{:S(2)}, u32[]{:S(2)}) collective-permute-start(f32[2,4,4,8,128]{4,3,2,1,0:T(8,128)S(1)} %get-tuple-element.39.mine_rest.refs_5_.second), channel_id=1, source_target_pairs={{0,4},{4,0},{8,12},{12,8},{16,20},{20,16},{24,28},{28,24},{1,5},{5... | collective-permute-start | bytes 393224 | tf_op jit(solution)/shard_map/ppermute | solution.py:553
  23.3 8.2 %collective-permute-start.12 = (f32[4,4,8,128]{3,2,1,0:T(8,128)S(1)}, f32[4,4,8,128]{3,2,1,0:T(8,128)S(1)}, u32[]{:S(2)}, u32[]{:S(2)}) collective-permute-start(f32[4,4,8,128]{3,2,1,0:T(8,128)S(1)} %pick.1), channel_id=1, source_target_pairs={{0,3},{1,0},{2,1},{3,2},{4,5},{5,6},{6,7},{7,4},{8,11},{9,8},{10,9... | collective-permute-start | bytes 196616 | tf_op jit(solution)/shard_map/ppermute | solution.py:571
  26.7 14.5 %collective-permute-start.18 = (f32[3,4,4,8,128]{4,3,2,1,0:T(8,128)S(1)}, f32[3,4,4,8,128]{4,3,2,1,0:T(8,128)S(1)}, u32[]{:S(2)}, u32[]{:S(2)}) collective-permute-start(f32[3,4,4,8,128]{4,3,2,1,0:T(8,128)S(1)} %get-tuple-element.40.refs_1_), channel_id=1, source_target_pairs={{0,3},{1,0},{2,1},{3,2},{4,5},{5,6},{6,7},{7,4},{8,11},{9,8},{10,9... | collective-permute-start | bytes 589832 | tf_op jit(solution)/shard_map/ppermute | solution.py:567
  28.0 14.2 %collective-permute-start.19 = (f32[3,4,4,8,128]{4,3,2,1,0:T(8,128)S(1)}, f32[3,4,4,8,128]{4,3,2,1,0:T(8,128)S(1)}, u32[]{:S(2)}, u32[]{:S(2)}) collective-permute-start(f32[3,4,4,8,128]{4,3,2,1,0:T(8,128)S(1)} %get-tuple-element.42.refs_3_), channel_id=1, source_target_pairs={{0,1},{1,2},{2,3},{3,0},{4,7},{5,4},{6,5},{7,6},{8,9},{9,10},{10,1... | collective-permute-start | bytes 589832 | tf_op jit(solution)/shard_map/ppermute | solution.py:568
  31.6 7.7 %collective-permute-start.15 = (f32[9,4,8,128]{3,2,1,0:T(8,128)S(1)}, f32[9,4,8,128]{3,2,1,0:T(8,128)S(1)}, u32[]{:S(2)}, u32[]{:S(2)}) collective-permute-start(f32[9,4,8,128]{3,2,1,0:T(8,128)S(1)} %get-tuple-element.47), channel_id=1, source_target_pairs={{0,4},{4,0},{8,12},{12,8},{16,20},{20,16},{24,28},{28,24},{1,5},{5... | collective-permute-start | bytes 442376 | tf_op jit(solution)/shard_map/ppermute | solution.py:590
  33.4 4.1 %collective-permute-start.17 = (f32[4,4,8,128]{3,2,1,0:T(8,128)S(1)}, f32[4,4,8,128]{3,2,1,0:T(8,128)S(1)}, u32[]{:S(2)}, u32[]{:S(2)}) collective-permute-start(f32[4,4,8,128]{3,2,1,0:T(8,128)S(1)} %get-tuple-element.46.refs_2_), channel_id=1, source_target_pairs={{0,12},{4,8},{8,4},{12,0},{16,28},{20,24},{24,20},{28,16},{1,13},{... | collective-permute-start | bytes 196616 | tf_op jit(solution)/shard_map/ppermute | solution.py:590
  34.5 4.8 %collective-permute-start.16 = (f32[4,4,8,128]{3,2,1,0:T(8,128)S(1)}, f32[4,4,8,128]{3,2,1,0:T(8,128)S(1)}, u32[]{:S(2)}, u32[]{:S(2)}) collective-permute-start(f32[4,4,8,128]{3,2,1,0:T(8,128)S(1)} %get-tuple-element.46.refs_2_), channel_id=1, source_target_pairs={{0,8},{4,12},{8,0},{12,4},{16,24},{20,28},{24,16},{28,20},{1,9},{5... | collective-permute-start | bytes 196616 | tf_op jit(solution)/shard_map/ppermute | solution.py:590

commit v4 on v3

--- a/solution.py
+++ b/solution.py
@@ -66,19 +66,28 @@
     lax.fori_loop(0, count, step, 0, unroll=unroll)
 
 
-def arrange_kernel(vel, force, vp, gp, first, last):
+def arrange_kernel(vel, vp, first, last):
     comps, nx, planes = vp.shape[:3]
 
     def body(x):
         for c in range(comps):
             for j in range(planes):
-                value = vel[0, c, x, rows_of(j, planes), :]
-                vp[c, x, j] = value
-                gp[c, x, j] = value + TIME_STEP * force[0, c, x, rows_of(j, planes), :]
+                vp[c, x, j] = vel[0, c, x, rows_of(j, planes), :]
 
     for_layers(nx, body, 2)
     first[...] = vp[:, :1]
     last[...] = vp[:, nx - 1 :]
+
+
+def push_kernel(vp, force, gp):
+    comps, nx, planes = vp.shape[:3]
+
+    def body(x):
+        for c in range(comps):
+            for j in range(planes):
+                gp[c, x, j] = vp[c, x, j] + TIME_STEP * force[0, c, x, rows_of(j, planes), :]
+
+    for_layers(nx, body, 2)
 
 
 def sums_kernel(pieces, vp, other, *refs):
@@ -508,13 +517,14 @@
         return moves
 
     other = lax.ppermute(velocity, "member", swap)
-    vp, gp, first, last = call(
+    vp, first, last = call(
         arrange_kernel,
-        [(comps, nx, *layer)] * 2 + [(comps, 1, *layer)] * 2,
-        [velocity, forcing],
-        10 * velocity.size,
+        [(comps, nx, *layer)] + [(comps, 1, *layer)] * 2,
+        [velocity],
+        velocity.size,
         name="arrange",
     )
+    gp = call(push_kernel, [vp.shape], [vp, forcing], 2 * velocity.size, name="push")[0]
     above = lax.ppermute(first, "sub", [(s, (s - 1) % subs) for s in range(subs)])
     below = lax.ppermute(last, "sub", [(s, (s + 1) % subs) for s in range(subs)])
     hold = []
@@ -534,7 +544,7 @@
             if step:
                 tie = [parts[i - 1]] if i else []
                 if i and step == 1:
-                    tie += hold or [below, above]
+                    tie += (hold or [below, above]) + [gp]
                 parts[i] = part = call(
                     add_kernel, [part.shape], [part, got[i]] + tie, part.size, name="add%d" % i
                 )[0]

time: 44.9 us -> 44.9 us (level)
  local copies, waits for them, and re-layouts: 2.27 us -> 1.14 us
  starting transfers between devices: 25 us -> 25.7 us
    unnamed x4, local copies, waits for them, and re-layouts: 2.27 us -> 1.14 us
    ppermute x1, waiting for transfers between devices: 0.01 us -> 0.9 us  [fast(): other = lax.ppermute(velocity, 'member', swap)]
    ppermute x4, starting transfers between devices: 6.37 us -> 7.05 us  [fast(): got[i] = lax.ppermute(part, 'member', pair(step))]
    pallas_call x14 -> x15, Pallas kernels: 7.47 us -> 7.5 us  [call(): pl.pallas_call(kernel, out_shape=shapes, in_specs=vmem(len(ins)), out_spe...]
  transfers between devices with their start and end apart: 20 -> 20, of which waited for: 10 -> 11; matrix products, arithmetic and copies ran while one was open for 0% -> 0% of each run, Pallas kernels for 11% -> 11%
where the time goes in v4:
time: 44.9 us; the launch traced here: 44.7 us
  starting transfers between devices  25.7 us (57%)
  waiting for transfers between devices  10.2 us (23%)
  Pallas kernels  7.5 us (17%)
  local copies, waits for them, and re-layouts  1.14 us (3%)
    pallas_call x15, Pallas kernels, call(): pl.pallas_call(kernel, out_shape=shapes, in_specs=vmem(len(ins)), out_spe...  7.5 us
    ppermute x4, starting transfers between devices, fast(): got[i] = lax.ppermute(part, 'member', pair(step))  7.05 us
    ppermute x3, waiting for transfers between devices, fast(): lax.ppermute(value, 'member', [(m, m ^ hop) for m in range(members)])  4.09 us
    ppermute x3, starting transfers between devices, fast(): lax.ppermute(value, 'member', [(m, m ^ hop) for m in range(members)])  3.59 us
    ppermute x2, starting transfers between devices, fast(): halo_mine.append(lax.ppermute(mine_part, ('member', 'sub'), along(True)))  3.31 us
    ppermute x1, starting transfers between devices, fast(): visc_mine = lax.ppermute(visc, ('member', 'sub'), along(True))  3.14 us
    ppermute x2, starting transfers between devices, fast(): lax.ppermute(theirs_part, ('member', 'sub'), along(False))  2.99 us
    ppermute x1, starting transfers between devices, fast(): lax.ppermute(last, 'sub', [(s, (s + 1) % subs) for s in range(subs)])  2.03 us
  transfers between devices with their start and end apart: 20, of which 11 were waited for; matrix products, arithmetic and copies ran while one was open for 0% of the time, Pallas kernels for 11%

profile of v4, /device:TPU:0, one launch (start us, length us, event | category | flops | bytes accessed | tf_op | source)
XLA Modules:
  0.0 44.7 jit_solution(14782639974209448178)
XLA Ops:
  0.0 0.5 %collective-permute-start.2 = (f32[1,3,16,32,128]{4,3,2,1,0:T(8,128)}, f32[1,3,16,32,128]{4,3,2,1,0:T(8,128)S(1)}, u32[]{:S(2)}, u32[]{:S(2)}) collective-permute-start(f32[1,3,16,32,128]{4,3,2,1,0:T(8,128)} %vel.1), channel_id=1, source_target_pairs={{0,4},{4,0},{8,12},{12,8},{16,20},{20,16},{24,28},{28,24},{1,5},{5... | collective-permute-start | bytes 2359304 | tf_op jit(solution)/shard_map/ppermute | solution.py:519
  0.5 1.1 %copy-done = f32[1,3,16,32,128]{4,3,2,1,0:T(8,128)S(1)} copy-done((f32[1,3,16,32,128]{4,3,2,1,0:T(8,128)S(1)}, f32[1,3,16,32,128]{4,3,2,1,0:T(8,128)}, u32[]{:S(2)}) %copy-start) | copy-done | bytes 786456
  1.6 0.1 arrange.1
  1.7 0.9 %collective-permute-done.2.other = f32[1,3,16,32,128]{4,3,2,1,0:T(8,128)S(1)} collective-permute-done((f32[1,3,16,32,128]{4,3,2,1,0:T(8,128)}, f32[1,3,16,32,128]{4,3,2,1,0:T(8,128)S(1)}, u32[]{:S(2)}, u32[]{:S(2)}) %collective-permute-start.2) | collective-permute-done | bytes 786464 | tf_op jit(solution)/shard_map/ppermute | solution.py:519
  2.6 0.1 sums.1
  2.7 2.9 %collective-permute-start.3 = (f32[4,4,4,8,128]{4,3,2,1,0:T(8,128)S(1)}, f32[4,4,4,8,128]{4,3,2,1,0:T(8,128)S(1)}, u32[]{:S(2)}, u32[]{:S(2)}) collective-permute-start(f32[4,4,4,8,128]{4,3,2,1,0:T(8,128)S(1)} %get-tuple-element.31.refs_0_), channel_id=1, source_target_pairs={{0,8},{4,20},{8,0},{12,28},{16,24},{20,4},{24,16},{28,12},{1,9},{5... | collective-permute-start | bytes 786440 | tf_op jit(solution)/shard_map/ppermute | solution.py:551
  5.6 0.1 collective-permute-start.5
  5.7 2.0 %collective-permute-start = (f32[3,1,4,8,128]{4,3,2,1,0:T(8,128)S(1)}, f32[3,1,4,8,128]{4,3,2,1,0:T(8,128)S(1)}, u32[]{:S(2)}, u32[]{:S(2)}) collective-permute-start(f32[3,1,4,8,128]{4,3,2,1,0:T(8,128)S(1)} %get-tuple-element.29), channel_id=1, source_target_pairs={{0,1},{1,2},{2,3},{3,0},{4,5},{5,6},{6,7},{7,4},{8,9},{9,10},{10,1... | collective-permute-start | bytes 147464 | tf_op jit(solution)/shard_map/ppermute | solution.py:529
  7.7 2.0 %collective-permute-start.1 = (f32[3,1,4,8,128]{4,3,2,1,0:T(8,128)S(1)}, f32[3,1,4,8,128]{4,3,2,1,0:T(8,128)S(1)}, u32[]{:S(2)}, u32[]{:S(2)}) collective-permute-start(f32[3,1,4,8,128]{4,3,2,1,0:T(8,128)S(1)} %get-tuple-element.30), channel_id=1, source_target_pairs={{0,3},{1,0},{2,1},{3,2},{4,7},{5,4},{6,5},{7,6},{8,11},{9,8},{10,9... | collective-permute-start | bytes 147464 | tf_op jit(solution)/shard_map/ppermute | solution.py:528
  9.8 0.2 collective-permute-done.3.refs_1_
  10.0 2.1 %collective-permute-start.4 = (f32[4,4,4,8,128]{4,3,2,1,0:T(8,128)S(1)}, f32[4,4,4,8,128]{4,3,2,1,0:T(8,128)S(1)}, u32[]{:S(2)}, u32[]{:S(2)}) collective-permute-start(f32[4,4,4,8,128]{4,3,2,1,0:T(8,128)S(1)} %add0.1.refs_2_.refs_0_), channel_id=1, source_target_pairs={{0,16},{4,12},{8,24},{12,4},{16,0},{20,28},{24,8},{28,20},{1,17},{... | collective-permute-start | bytes 786440 | tf_op jit(solution)/shard_map/ppermute | solution.py:551
  12.1 0.0 collective-permute-done.refs_0_.below
  12.1 0.2 collective-permute-done.1.refs_1_.above
  12.3 0.0 collective-permute-start.6
  12.4 0.1 push.1.refs_4_.gp
  12.5 1.2 %collective-permute-done.6.refs_3_ = f32[9,1,4,8,128]{4,3,2,1,0:T(8,128)S(1)} collective-permute-done((f32[9,1,4,8,128]{4,3,2,1,0:T(8,128)S(1)}, f32[9,1,4,8,128]{4,3,2,1,0:T(8,128)S(1)}, u32[]{:S(2)}, u32[]{:S(2)}) %collective-permute-start.6) | collective-permute-done | bytes 147488 | tf_op jit(solution)/shard_map/ppermute | solution.py:533
  13.8 1.9 %collective-permute-start.9 = (f32[4,4,4,8,128]{4,3,2,1,0:T(8,128)S(1)}, f32[4,4,4,8,128]{4,3,2,1,0:T(8,128)S(1)}, u32[]{:S(2)}, u32[]{:S(2)}) collective-permute-start(f32[4,4,4,8,128]{4,3,2,1,0:T(8,128)S(1)} %add1.1.refs_2_.refs_0_), channel_id=1, source_target_pairs={{0,16},{4,12},{8,24},{12,4},{16,0},{20,28},{24,8},{28,20},{1,17},{... | collective-permute-start | bytes 786440 | tf_op jit(solution)/shard_map/ppermute | solution.py:551
  15.7 0.8 %collective-permute-done.4.refs_1_ = f32[4,4,4,8,128]{4,3,2,1,0:T(8,128)S(1)} collective-permute-done((f32[4,4,4,8,128]{4,3,2,1,0:T(8,128)S(1)}, f32[4,4,4,8,128]{4,3,2,1,0:T(8,128)S(1)}, u32[]{:S(2)}, u32[]{:S(2)}) %collective-permute-start.4) | collective-permute-done | bytes 262176 | tf_op jit(solution)/shard_map/ppermute | solution.py:551
  16.5 0.1 stats0.1
  16.5 0.1 collective-permute-start.7
  16.6 0.5 %collective-permute-start.8 = (f32[2,4,4,8,128]{4,3,2,1,0:T(8,128)S(1)}, f32[2,4,4,8,128]{4,3,2,1,0:T(8,128)S(1)}, u32[]{:S(2)}, u32[]{:S(2)}) collective-permute-start(f32[2,4,4,8,128]{4,3,2,1,0:T(8,128)S(1)} %get-tuple-element.34.mine_rest.refs_4_.first), channel_id=1, source_target_pairs={{0,4},{4,0},{8,12},{12,8},{16,20},{20,16},{24,28},{28,24},{1,5},{5... | collective-permute-start | bytes 393224 | tf_op jit(solution)/shard_map/ppermute | solution.py:563
  17.1 0.8 %collective-permute-done.7.theirs = f32[2,4,4,8,128]{4,3,2,1,0:T(8,128)S(1)} collective-permute-done((f32[2,4,4,8,128]{4,3,2,1,0:T(8,128)S(1)}, f32[2,4,4,8,128]{4,3,2,1,0:T(8,128)S(1)}, u32[]{:S(2)}, u32[]{:S(2)}) %collective-permute-start.7) | collective-permute-done | bytes 131104 | tf_op jit(solution)/shard_map/ppermute | solution.py:563
  17.9 0.2 collective-permute-done.8.theirs_rest.refs_6_
  18.1 0.3 source0.1
  18.4 2.2 %collective-permute-start.14 = (f32[3,4,4,8,128]{4,3,2,1,0:T(8,128)S(1)}, f32[3,4,4,8,128]{4,3,2,1,0:T(8,128)S(1)}, u32[]{:S(2)}, u32[]{:S(2)}) collective-permute-start(f32[3,4,4,8,128]{4,3,2,1,0:T(8,128)S(1)} %get-tuple-element.39.refs_2_), channel_id=1, source_target_pairs={{0,1},{1,2},{2,3},{3,0},{4,7},{5,4},{6,5},{7,6},{8,9},{9,10},{10,1... | collective-permute-start | bytes 589832 | tf_op jit(solution)/shard_map/ppermute | solution.py:578
  20.6 2.1 %collective-permute-start.13 = (f32[3,4,4,8,128]{4,3,2,1,0:T(8,128)S(1)}, f32[3,4,4,8,128]{4,3,2,1,0:T(8,128)S(1)}, u32[]{:S(2)}, u32[]{:S(2)}) collective-permute-start(f32[3,4,4,8,128]{4,3,2,1,0:T(8,128)S(1)} %get-tuple-element.35.refs_2_.refs_0_), channel_id=1, source_target_pairs={{0,3},{1,0},{2,1},{3,2},{4,5},{5,6},{6,7},{7,4},{8,11},{9,8},{10,9... | collective-permute-start | bytes 589832 | tf_op jit(solution)/shard_map/ppermute | solution.py:577
  22.6 0.1 stats1.1
  22.7 0.1 collective-permute-start.10
  22.8 0.5 %collective-permute-start.11 = (f32[2,4,4,8,128]{4,3,2,1,0:T(8,128)S(1)}, f32[2,4,4,8,128]{4,3,2,1,0:T(8,128)S(1)}, u32[]{:S(2)}, u32[]{:S(2)}) collective-permute-start(f32[2,4,4,8,128]{4,3,2,1,0:T(8,128)S(1)} %get-tuple-element.37.mine_rest.refs_5_.second), channel_id=1, source_target_pairs={{0,4},{4,0},{8,12},{12,8},{16,20},{20,16},{24,28},{28,24},{1,5},{5... | collective-permute-start | bytes 393224 | tf_op jit(solution)/shard_map/ppermute | solution.py:563
  23.3 3.1 %collective-permute-start.12 = (f32[4,4,8,128]{3,2,1,0:T(8,128)S(1)}, f32[4,4,8,128]{3,2,1,0:T(8,128)S(1)}, u32[]{:S(2)}, u32[]{:S(2)}) collective-permute-start(f32[4,4,8,128]{3,2,1,0:T(8,128)S(1)} %pick.1), channel_id=1, source_target_pairs={{0,3},{1,0},{2,1},{3,2},{4,5},{5,6},{6,7},{7,4},{8,11},{9,8},{10,9... | collective-permute-start | bytes 196616 | tf_op jit(solution)/shard_map/ppermute | solution.py:581
  26.4 0.0 collective-permute-done.10.theirs
  26.4 0.0 collective-permute-done.11.theirs_rest.refs_7_
  26.4 0.3 source1.1
  26.7 1.2 %collective-permute-start.18 = (f32[3,4,4,8,128]{4,3,2,1,0:T(8,128)S(1)}, f32[3,4,4,8,128]{4,3,2,1,0:T(8,128)S(1)}, u32[]{:S(2)}, u32[]{:S(2)}) collective-permute-start(f32[3,4,4,8,128]{4,3,2,1,0:T(8,128)S(1)} %get-tuple-element.38.refs_1_), channel_id=1, source_target_pairs={{0,3},{1,0},{2,1},{3,2},{4,5},{5,6},{6,7},{7,4},{8,11},{9,8},{10,9... | collective-permute-start | bytes 589832 | tf_op jit(solution)/shard_map/ppermute | solution.py:577
  28.0 0.8 %collective-permute-start.19 = (f32[3,4,4,8,128]{4,3,2,1,0:T(8,128)S(1)}, f32[3,4,4,8,128]{4,3,2,1,0:T(8,128)S(1)}, u32[]{:S(2)}, u32[]{:S(2)}) collective-permute-start(f32[3,4,4,8,128]{4,3,2,1,0:T(8,128)S(1)} %get-tuple-element.40.refs_3_), channel_id=1, source_target_pairs={{0,1},{1,2},{2,3},{3,0},{4,7},{5,4},{6,5},{7,6},{8,9},{9,10},{10,1... | collective-permute-start | bytes 589832 | tf_op jit(solution)/shard_map/ppermute | solution.py:578
  28.8 1.8 %own.1 = (f32[2,7,8,4,8,128]{5,4,3,2,1,0:T(8,128)S(1)}, f32[2,3,8,4,8,128]{5,4,3,2,1,0:T(8,128)S(1)}, f32[8,2,3,2,4,8,128]{6,5,4,3,2,1,0:T(8,128)S(1)}, f32[2,8,4,8,128]{4,3,2,1,0:T(8,128)S(1)}) custom-call(f32[3,4,4,8,128]{4,3,2,1,0:T(8,128)S(1)} %get-tuple-element.35.refs_2_.refs_0_, f32[3,4,4,8,128]{4,3,2,1,0:T(8,128)S(1)} %get-tuple-element.38.refs_1_, ...), custom_call_target="tpu_custom_call" | custom-call | flops 11796480 | bytes 5767168 | tf_op jit(solution)/shard_map/own/pallas_call | solution.py:481
  30.6 0.9 %collective-permute-done.12.refs_0_ = f32[4,4,8,128]{3,2,1,0:T(8,128)S(1)} collective-permute-done((f32[4,4,8,128]{3,2,1,0:T(8,128)S(1)}, f32[4,4,8,128]{3,2,1,0:T(8,128)S(1)}, u32[]{:S(2)}, u32[]{:S(2)}) %collective-permute-start.12) | collective-permute-done | bytes 65568 | tf_op jit(solution)/shard_map/ppermute | solution.py:581
  31.5 0.0 collective-permute-done.14.refs_2_.refs_9_
  31.5 0.0 collective-permute-done.13.refs_1_.refs_8_
  31.6 1.9 %collective-permute-start.15 = (f32[9,4,8,128]{3,2,1,0:T(8,128)S(1)}, f32[9,4,8,128]{3,2,1,0:T(8,128)S(1)}, u32[]{:S(2)}, u32[]{:S(2)}) collective-permute-start(f32[9,4,8,128]{3,2,1,0:T(8,128)S(1)} %get-tuple-element.45), channel_id=1, source_target_pairs={{0,4},{4,0},{8,12},{12,8},{16,20},{20,16},{24,28},{28,24},{1,5},{5... | collective-permute-start | bytes 442376 | tf_op jit(solution)/shard_map/ppermute | solution.py:600
  33.4 1.0 %collective-permute-start.17 = (f32[4,4,8,128]{3,2,1,0:T(8,128)S(1)}, f32[4,4,8,128]{3,2,1,0:T(8,128)S(1)}, u32[]{:S(2)}, u32[]{:S(2)}) collective-permute-start(f32[4,4,8,128]{3,2,1,0:T(8,128)S(1)} %get-tuple-element.44.refs_2_), channel_id=1, source_target_pairs={{0,12},{4,8},{8,4},{12,0},{16,28},{20,24},{24,20},{28,16},{1,13},{... | collective-permute-start | bytes 196616 | tf_op jit(solution)/shard_map/ppermute | solution.py:600
  34.5 0.7 %collective-permute-start.16 = (f32[4,4,8,128]{3,2,1,0:T(8,128)S(1)}, f32[4,4,8,128]{3,2,1,0:T(8,128)S(1)}, u32[]{:S(2)}, u32[]{:S(2)}) collective-permute-start(f32[4,4,8,128]{3,2,1,0:T(8,128)S(1)} %get-tuple-element.44.refs_2_), channel_id=1, source_target_pairs={{0,8},{4,12},{8,0},{12,4},{16,24},{20,28},{24,16},{28,20},{1,9},{5... | collective-permute-start | bytes 196616 | tf_op jit(solution)/shard_map/ppermute | solution.py:600
  35.2 2.4 %collective-permute-done.17.refs_5_ = f32[4,4,8,128]{3,2,1,0:T(8,128)S(1)} collective-permute-done((f32[4,4,8,128]{3,2,1,0:T(8,128)S(1)}, f32[4,4,8,128]{3,2,1,0:T(8,128)S(1)}, u32[]{:S(2)}, u32[]{:S(2)}) %collective-permute-start.17) | collective-permute-done | bytes 65568 | tf_op jit(solution)/shard_map/ppermute | solution.py:600
  37.6 1.7 %collective-permute-done.16.refs_4_ = f32[4,4,8,128]{3,2,1,0:T(8,128)S(1)} collective-permute-done((f32[4,4,8,128]{3,2,1,0:T(8,128)S(1)}, f32[4,4,8,128]{3,2,1,0:T(8,128)S(1)}, u32[]{:S(2)}, u32[]{:S(2)}) %collective-permute-start.16) | collective-permute-done | bytes 65568 | tf_op jit(solution)/shard_map/ppermute | solution.py:600
  39.2 2.0 %stage0.1 = (f32[2,3,5,4,8,128]{5,4,3,2,1,0:T(8,128)S(1)}, f32[8,2,3,2,4,8,128]{6,5,4,3,2,1,0:T(8,128)S(1)}, f32[2,3,4,32,128]{4,3,2,1,0:T(8,128)S(1)}, f32[2,7,9,4,8,128]{5,4,3,2,1,0:T(8,128)S(1)}) custom-call(f32[2,7,8,4,8,128]{5,4,3,2,1,0:T(8,128)S(1)} %get-tuple-element.41.refs_0_, f32[2,8,4,8,128]{4,3,2,1,0:T(8,128)S(1)} %get-tuple-element.42.refs_1_, ...), custom_call_target="tpu_custom_call" | custom-call | flops 15728640 | bytes 9715712 | tf_op jit(solution)/shard_map/stage0/pallas_call | solution.py:481
  41.3 0.0 collective-permute-done.18.refs_5_
  41.3 0.9 %collective-permute-done.19.refs_6_ = f32[3,4,4,8,128]{4,3,2,1,0:T(8,128)S(1)} collective-permute-done((f32[3,4,4,8,128]{4,3,2,1,0:T(8,128)S(1)}, f32[3,4,4,8,128]{4,3,2,1,0:T(8,128)S(1)}, u32[]{:S(2)}, u32[]{:S(2)}) %collective-permute-start.19) | collective-permute-done | bytes 196640 | tf_op jit(solution)/shard_map/ppermute | solution.py:578
  42.2 2.6 %stage1.1 = f32[1,3,16,32,128]{4,3,2,1,0:T(8,128)} custom-call(f32[2,7,8,4,8,128]{5,4,3,2,1,0:T(8,128)S(1)} %get-tuple-element.41.refs_0_, f32[2,7,9,4,8,128]{5,4,3,2,1,0:T(8,128)S(1)} %get-tuple-element.47.refs_1_, f32[2,3,8,4,8,128]{5,4,3,2,1,0:T(8,128)S(1)} %get-tuple-element.46.refs_6_.refs_2_, f32[2,3,5,4,8,128]{5,4,3,2,1,0:T(8,128)S(1)} %get-tuple-element.48.refs_3_, ...), custom_call_target="tpu_custom_call" | custom-call | flops 15728640 | bytes 8323072 | tf_op jit(solution)/shard_map/stage1/pallas_call | solution.py:481
  (11 shorter events, 0.1 us)
Async XLA Ops:
  0.0 2.6 %collective-permute-start.2 = (f32[1,3,16,32,128]{4,3,2,1,0:T(8,128)}, f32[1,3,16,32,128]{4,3,2,1,0:T(8,128)S(1)}, u32[]{:S(2)}, u32[]{:S(2)}) collective-permute-start(f32[1,3,16,32,128]{4,3,2,1,0:T(8,128)} %vel.1), channel_id=1, source_target_pairs={{0,4},{4,0},{8,12},{12,8},{16,20},{20,16},{24,28},{28,24},{1,5},{5... | collective-permute-start | bytes 2359304 | tf_op jit(solution)/shard_map/ppermute | solution.py:519
  0.5 1.1 %copy-start = (f32[1,3,16,32,128]{4,3,2,1,0:T(8,128)S(1)}, f32[1,3,16,32,128]{4,3,2,1,0:T(8,128)}, u32[]{:S(2)}) copy-start(f32[1,3,16,32,128]{4,3,2,1,0:T(8,128)} %vel.1) | copy-start | bytes 2359300
  1.6 10.8 %copy-start.1 = (f32[1,3,16,32,128]{4,3,2,1,0:T(8,128)S(1)}, f32[1,3,16,32,128]{4,3,2,1,0:T(8,128)}, u32[]{:S(2)}) copy-start(f32[1,3,16,32,128]{4,3,2,1,0:T(8,128)} %force.1) | copy-start | bytes 2359300
  2.7 7.3 %collective-permute-start.3 = (f32[4,4,4,8,128]{4,3,2,1,0:T(8,128)S(1)}, f32[4,4,4,8,128]{4,3,2,1,0:T(8,128)S(1)}, u32[]{:S(2)}, u32[]{:S(2)}) collective-permute-start(f32[4,4,4,8,128]{4,3,2,1,0:T(8,128)S(1)} %get-tuple-element.31.refs_0_), channel_id=1, source_target_pairs={{0,8},{4,20},{8,0},{12,28},{16,24},{20,4},{24,16},{28,12},{1,9},{5... | collective-permute-start | bytes 786440 | tf_op jit(solution)/shard_map/ppermute | solution.py:551
  5.6 8.1 %collective-permute-start.5 = (f32[4,4,4,8,128]{4,3,2,1,0:T(8,128)S(1)}, f32[4,4,4,8,128]{4,3,2,1,0:T(8,128)S(1)}, u32[]{:S(2)}, u32[]{:S(2)}) collective-permute-start(f32[4,4,4,8,128]{4,3,2,1,0:T(8,128)S(1)} %get-tuple-element.32.refs_0_), channel_id=1, source_target_pairs={{0,8},{4,20},{8,0},{12,28},{16,24},{20,4},{24,16},{28,12},{1,9},{5... | collective-permute-start | bytes 786440 | tf_op jit(solution)/shard_map/ppermute | solution.py:551
  5.7 6.4 %collective-permute-start = (f32[3,1,4,8,128]{4,3,2,1,0:T(8,128)S(1)}, f32[3,1,4,8,128]{4,3,2,1,0:T(8,128)S(1)}, u32[]{:S(2)}, u32[]{:S(2)}) collective-permute-start(f32[3,1,4,8,128]{4,3,2,1,0:T(8,128)S(1)} %get-tuple-element.29), channel_id=1, source_target_pairs={{0,1},{1,2},{2,3},{3,0},{4,5},{5,6},{6,7},{7,4},{8,9},{9,10},{10,1... | collective-permute-start | bytes 147464 | tf_op jit(solution)/shard_map/ppermute | solution.py:529
  7.7 4.6 %collective-permute-start.1 = (f32[3,1,4,8,128]{4,3,2,1,0:T(8,128)S(1)}, f32[3,1,4,8,128]{4,3,2,1,0:T(8,128)S(1)}, u32[]{:S(2)}, u32[]{:S(2)}) collective-permute-start(f32[3,1,4,8,128]{4,3,2,1,0:T(8,128)S(1)} %get-tuple-element.30), channel_id=1, source_target_pairs={{0,3},{1,0},{2,1},{3,2},{4,7},{5,4},{6,5},{7,6},{8,11},{9,8},{10,9... | collective-permute-start | bytes 147464 | tf_op jit(solution)/shard_map/ppermute | solution.py:528
  10.0 6.5 %collective-permute-start.4 = (f32[4,4,4,8,128]{4,3,2,1,0:T(8,128)S(1)}, f32[4,4,4,8,128]{4,3,2,1,0:T(8,128)S(1)}, u32[]{:S(2)}, u32[]{:S(2)}) collective-permute-start(f32[4,4,4,8,128]{4,3,2,1,0:T(8,128)S(1)} %add0.1.refs_2_.refs_0_), channel_id=1, source_target_pairs={{0,16},{4,12},{8,24},{12,4},{16,0},{20,28},{24,8},{28,20},{1,17},{... | collective-permute-start | bytes 786440 | tf_op jit(solution)/shard_map/ppermute | solution.py:551
  12.3 1.4 %collective-permute-start.6 = (f32[9,1,4,8,128]{4,3,2,1,0:T(8,128)S(1)}, f32[9,1,4,8,128]{4,3,2,1,0:T(8,128)S(1)}, u32[]{:S(2)}, u32[]{:S(2)}) collective-permute-start(f32[9,1,4,8,128]{4,3,2,1,0:T(8,128)S(1)} %gate.1), channel_id=1, source_target_pairs={{0,4},{4,0},{8,12},{12,8},{16,20},{20,16},{24,28},{28,24},{1,5},{5... | collective-permute-start | bytes 442376 | tf_op jit(solution)/shard_map/ppermute | solution.py:533
  13.8 8.9 %collective-permute-start.9 = (f32[4,4,4,8,128]{4,3,2,1,0:T(8,128)S(1)}, f32[4,4,4,8,128]{4,3,2,1,0:T(8,128)S(1)}, u32[]{:S(2)}, u32[]{:S(2)}) collective-permute-start(f32[4,4,4,8,128]{4,3,2,1,0:T(8,128)S(1)} %add1.1.refs_2_.refs_0_), channel_id=1, source_target_pairs={{0,16},{4,12},{8,24},{12,4},{16,0},{20,28},{24,8},{28,20},{1,17},{... | collective-permute-start | bytes 786440 | tf_op jit(solution)/shard_map/ppermute | solution.py:551
  16.5 1.4 %collective-permute-start.7 = (f32[2,4,4,8,128]{4,3,2,1,0:T(8,128)S(1)}, f32[2,4,4,8,128]{4,3,2,1,0:T(8,128)S(1)}, u32[]{:S(2)}, u32[]{:S(2)}) collective-permute-start(f32[2,4,4,8,128]{4,3,2,1,0:T(8,128)S(1)} %get-tuple-element.33.mine), channel_id=1, source_target_pairs={{0,4},{4,0},{8,12},{12,8},{16,20},{20,16},{24,28},{28,24},{1,5},{5... | collective-permute-start | bytes 393224 | tf_op jit(solution)/shard_map/ppermute | solution.py:563
  16.6 1.5 %collective-permute-start.8 = (f32[2,4,4,8,128]{4,3,2,1,0:T(8,128)S(1)}, f32[2,4,4,8,128]{4,3,2,1,0:T(8,128)S(1)}, u32[]{:S(2)}, u32[]{:S(2)}) collective-permute-start(f32[2,4,4,8,128]{4,3,2,1,0:T(8,128)S(1)} %get-tuple-element.34.mine_rest.refs_4_.first), channel_id=1, source_target_pairs={{0,4},{4,0},{8,12},{12,8},{16,20},{20,16},{24,28},{28,24},{1,5},{5... | collective-permute-start | bytes 393224 | tf_op jit(solution)/shard_map/ppermute | solution.py:563
  18.4 13.1 %collective-permute-start.14 = (f32[3,4,4,8,128]{4,3,2,1,0:T(8,128)S(1)}, f32[3,4,4,8,128]{4,3,2,1,0:T(8,128)S(1)}, u32[]{:S(2)}, u32[]{:S(2)}) collective-permute-start(f32[3,4,4,8,128]{4,3,2,1,0:T(8,128)S(1)} %get-tuple-element.39.refs_2_), channel_id=1, source_target_pairs={{0,1},{1,2},{2,3},{3,0},{4,7},{5,4},{6,5},{7,6},{8,9},{9,10},{10,1... | collective-permute-start | bytes 589832 | tf_op jit(solution)/shard_map/ppermute | solution.py:578
  20.6 11.0 %collective-permute-start.13 = (f32[3,4,4,8,128]{4,3,2,1,0:T(8,128)S(1)}, f32[3,4,4,8,128]{4,3,2,1,0:T(8,128)S(1)}, u32[]{:S(2)}, u32[]{:S(2)}) collective-permute-start(f32[3,4,4,8,128]{4,3,2,1,0:T(8,128)S(1)} %get-tuple-element.35.refs_2_.refs_0_), channel_id=1, source_target_pairs={{0,3},{1,0},{2,1},{3,2},{4,5},{5,6},{6,7},{7,4},{8,11},{9,8},{10,9... | collective-permute-start | bytes 589832 | tf_op jit(solution)/shard_map/ppermute | solution.py:577
  22.7 3.7 %collective-permute-start.10 = (f32[2,4,4,8,128]{4,3,2,1,0:T(8,128)S(1)}, f32[2,4,4,8,128]{4,3,2,1,0:T(8,128)S(1)}, u32[]{:S(2)}, u32[]{:S(2)}) collective-permute-start(f32[2,4,4,8,128]{4,3,2,1,0:T(8,128)S(1)} %get-tuple-element.36.mine), channel_id=1, source_target_pairs={{0,4},{4,0},{8,12},{12,8},{16,20},{20,16},{24,28},{28,24},{1,5},{5... | collective-permute-start | bytes 393224 | tf_op jit(solution)/shard_map/ppermute | solution.py:563
  22.8 3.7 %collective-permute-start.11 = (f32[2,4,4,8,128]{4,3,2,1,0:T(8,128)S(1)}, f32[2,4,4,8,128]{4,3,2,1,0:T(8,128)S(1)}, u32[]{:S(2)}, u32[]{:S(2)}) collective-permute-start(f32[2,4,4,8,128]{4,3,2,1,0:T(8,128)S(1)} %get-tuple-element.37.mine_rest.refs_5_.second), channel_id=1, source_target_pairs={{0,4},{4,0},{8,12},{12,8},{16,20},{20,16},{24,28},{28,24},{1,5},{5... | collective-permute-start | bytes 393224 | tf_op jit(solution)/shard_map/ppermute | solution.py:563
  23.3 8.2 %collective-permute-start.12 = (f32[4,4,8,128]{3,2,1,0:T(8,128)S(1)}, f32[4,4,8,128]{3,2,1,0:T(8,128)S(1)}, u32[]{:S(2)}, u32[]{:S(2)}) collective-permute-start(f32[4,4,8,128]{3,2,1,0:T(8,128)S(1)} %pick.1), channel_id=1, source_target_pairs={{0,3},{1,0},{2,1},{3,2},{4,5},{5,6},{6,7},{7,4},{8,11},{9,8},{10,9... | collective-permute-start | bytes 196616 | tf_op jit(solution)/shard_map/ppermute | solution.py:581
  26.7 14.5 %collective-permute-start.18 = (f32[3,4,4,8,128]{4,3,2,1,0:T(8,128)S(1)}, f32[3,4,4,8,128]{4,3,2,1,0:T(8,128)S(1)}, u32[]{:S(2)}, u32[]{:S(2)}) collective-permute-start(f32[3,4,4,8,128]{4,3,2,1,0:T(8,128)S(1)} %get-tuple-element.38.refs_1_), channel_id=1, source_target_pairs={{0,3},{1,0},{2,1},{3,2},{4,5},{5,6},{6,7},{7,4},{8,11},{9,8},{10,9... | collective-permute-start | bytes 589832 | tf_op jit(solution)/shard_map/ppermute | solution.py:577
  28.0 14.2 %collective-permute-start.19 = (f32[3,4,4,8,128]{4,3,2,1,0:T(8,128)S(1)}, f32[3,4,4,8,128]{4,3,2,1,0:T(8,128)S(1)}, u32[]{:S(2)}, u32[]{:S(2)}) collective-permute-start(f32[3,4,4,8,128]{4,3,2,1,0:T(8,128)S(1)} %get-tuple-element.40.refs_3_), channel_id=1, source_target_pairs={{0,1},{1,2},{2,3},{3,0},{4,7},{5,4},{6,5},{7,6},{8,9},{9,10},{10,1... | collective-permute-start | bytes 589832 | tf_op jit(solution)/shard_map/ppermute | solution.py:578
  31.6 7.7 %collective-permute-start.15 = (f32[9,4,8,128]{3,2,1,0:T(8,128)S(1)}, f32[9,4,8,128]{3,2,1,0:T(8,128)S(1)}, u32[]{:S(2)}, u32[]{:S(2)}) collective-permute-start(f32[9,4,8,128]{3,2,1,0:T(8,128)S(1)} %get-tuple-element.45), channel_id=1, source_target_pairs={{0,4},{4,0},{8,12},{12,8},{16,20},{20,16},{24,28},{28,24},{1,5},{5... | collective-permute-start | bytes 442376 | tf_op jit(solution)/shard_map/ppermute | solution.py:600
  33.4 4.1 %collective-permute-start.17 = (f32[4,4,8,128]{3,2,1,0:T(8,128)S(1)}, f32[4,4,8,128]{3,2,1,0:T(8,128)S(1)}, u32[]{:S(2)}, u32[]{:S(2)}) collective-permute-start(f32[4,4,8,128]{3,2,1,0:T(8,128)S(1)} %get-tuple-element.44.refs_2_), channel_id=1, source_target_pairs={{0,12},{4,8},{8,4},{12,0},{16,28},{20,24},{24,20},{28,16},{1,13},{... | collective-permute-start | bytes 196616 | tf_op jit(solution)/shard_map/ppermute | solution.py:600
  34.5 4.8 %collective-permute-start.16 = (f32[4,4,8,128]{3,2,1,0:T(8,128)S(1)}, f32[4,4,8,128]{3,2,1,0:T(8,128)S(1)}, u32[]{:S(2)}, u32[]{:S(2)}) collective-permute-start(f32[4,4,8,128]{3,2,1,0:T(8,128)S(1)} %get-tuple-element.44.refs_2_), channel_id=1, source_target_pairs={{0,8},{4,12},{8,0},{12,4},{16,24},{20,28},{24,16},{28,20},{1,9},{5... | collective-permute-start | bytes 196616 | tf_op jit(solution)/shard_map/ppermute | solution.py:600
